TPU v7x, 32 devices: a whole 2x2x4 slice. The times are simulated.
32 devices in a mesh: seq: 16 (over z, y, core), rep: 2 (over x).
Axes of the slice: x: 2, y: 2, z: 4, core: 2. Of those that a mesh axis runs over, the one named last changes fastest.
Arguments:
- tokens: bfloat16 [4096, 2048], P(('seq', 'rep')), may hold values from -6 to 6
- cotangent: bfloat16 [4096, 2048], P(('seq', 'rep')), may hold values from -6 to 6
- domain_tags: int32 [4096], P(('seq', 'rep')), may hold values from 0 to 3, as said below
- doc_ids: int32 [4096], replicated, may hold values from 0 to 7, never falling along the last dimension, each value on 1 to 1024 neighbouring positions
- counts: int32 [4], replicated, may hold values from 1 to 1, as said below
- w_in: bfloat16 [2048, 2048], P('seq'), may hold values from -0.125 to 0.125
- w_forget: bfloat16 [2048, 2048], P('seq'), may hold values from -0.125 to 0.125
- w_gate_out: bfloat16 [2048, 2048], P('seq'), may hold values from -0.125 to 0.125
- w_out: bfloat16 [2048, 2048], P('seq'), may hold values from -0.25 to 0.25
- ffn_gate: bfloat16 [2048, 5632], P('seq'), may hold values from -0.125 to 0.125
- ffn_up: bfloat16 [2048, 5632], P('seq'), may hold values from -0.125 to 0.125
- ffn_down: bfloat16 [5632, 2048], P('seq'), may hold values from -0.15625 to 0.15625
- norm_gain: float32 [2048], replicated, may hold values from 0.25 to 1.75
- out_gain: float32 [2048], replicated, may hold values from 0.25 to 1.75
- ffn_gain: float32 [2048], replicated, may hold values from 0.25 to 1.75
- bound_logits: float32 [24, 2048], P(None, ('seq', 'rep')), may hold values from -6 to 6
Outputs:
- output_rows: bfloat16 [4096, 2048], P(('seq', 'rep'))
- grad_tokens: float32 [4096, 2048], P(('seq', 'rep'))
- grad_w_in: float32 [2048, 2048], P(('seq', 'rep'))
- grad_w_forget: float32 [2048, 2048], P(('seq', 'rep'))
- grad_w_gate_out: float32 [2048, 2048], P(('seq', 'rep'))
- grad_w_out: float32 [2048, 2048], P(('seq', 'rep'))
- grad_ffn_gate: float32 [2048, 5632], P(('seq', 'rep'))
- grad_ffn_up: float32 [2048, 5632], P(('seq', 'rep'))
- grad_ffn_down: float32 [5632, 2048], P(None, ('seq', 'rep'))
- grad_norm_gain: float32 [2048], P(('seq', 'rep'))
- grad_out_gain: float32 [2048], P(('seq', 'rep'))
- grad_ffn_gain: float32 [2048], P(('seq', 'rep'))
- grad_bound_logits: float32 [24, 2048], P(None, ('seq', 'rep'))
Inputs may be any that keep to these rules, and one draw needn't show every extreme that they name: `domain_tags`: all 1024 tokens of a sequence share one domain, and every domain has at least one sequence. counts is the number of sequences whose tokens carry each domain.
All inputs are finite; a program needn't handle non-finite values.
Results may differ from a plain program's by a relative error of at most 0.011.
Values may be sent and summed in bfloat16 or wider, within the bound.
A program may use at most 704 MiB of HBM per device.

v0:
```python
import jax
import jax.numpy as jnp
from jax import lax
from jax.sharding import PartitionSpec as P

LAYER_AT = 12
SEQ_LEN = 1024


EPS = 1e-06
GAIN_PAD = 125


def chain_link(earlier, later):
    return (earlier[0] * later[0], later[0] * earlier[1] + later[1])


def silu_grad(values):
    sig = jax.nn.sigmoid(values)
    return sig * (1.0 + values * (1.0 - sig))


def body(
    tokens,
    cotangent,
    domain_tags,
    doc_ids,
    counts,
    w_in,
    w_forget,
    w_gate_out,
    w_out,
    ffn_gate,
    ffn_up,
    ffn_down,
    norm_gain,
    out_gain,
    ffn_gain,
    bound_logits,
):
    f32 = jnp.float32
    bf16 = jnp.bfloat16
    groups = lax.axis_size("seq")
    copies = lax.axis_size("rep")
    width = tokens.shape[1]
    chan_count = width // (groups * copies)
    unit_count = ffn_gate.shape[1]
    full_in, full_forget, full_gate_out, full_out, full_fgate, full_fup, full_fdown = (
        lax.all_gather(w_in, "seq", axis=0, tiled=True),
        lax.all_gather(w_forget, "seq", axis=0, tiled=True),
        lax.all_gather(w_gate_out, "seq", axis=0, tiled=True),
        lax.all_gather(w_out, "seq", axis=0, tiled=True),
        lax.all_gather(ffn_gate, "seq", axis=0, tiled=True),
        lax.all_gather(ffn_up, "seq", axis=0, tiled=True),
        lax.all_gather(ffn_down, "seq", axis=0, tiled=True),
    )
    token_f = tokens.astype(f32)
    scale_one = lax.rsqrt(jnp.mean(token_f * token_f, axis=-1, keepdims=True) + EPS)
    normed_one = token_f * scale_one
    act_one = (normed_one * norm_gain).astype(bf16)
    in_proj = jnp.einsum("td,de->et", act_one, full_in, preferred_element_type=f32).astype(bf16)
    forget_proj = jnp.einsum("td,de->et", act_one, full_forget, preferred_element_type=f32).astype(
        bf16
    )
    gate_proj = jnp.dot(act_one, full_gate_out, preferred_element_type=f32)
    in_chan, forget_chan = (
        lax.all_to_all(in_proj, ("seq", "rep"), split_axis=0, concat_axis=1, tiled=True),
        lax.all_to_all(forget_proj, ("seq", "rep"), split_axis=0, concat_axis=1, tiled=True),
    )
    all_rows = doc_ids.shape[0]
    places = jnp.arange(all_rows, dtype=jnp.int32)
    previous = jnp.concatenate([doc_ids[:1], doc_ids[:-1]])
    keep_mask = jnp.where((places % SEQ_LEN != 0) & (doc_ids == previous), 1.0, 0.0).astype(f32)[
        None, :
    ]
    layer_count = bound_logits.shape[0]
    layer_probs = jax.nn.softmax(bound_logits, axis=0)
    layer_index = jnp.arange(layer_count, dtype=jnp.int32)
    layer_pick = ((layer_index >= 1) & (layer_index <= LAYER_AT)).astype(f32)[:, None]
    lower_bound = jnp.sum(layer_probs * layer_pick, axis=0)[:, None]
    in_f = in_chan.astype(f32)
    sig_forget = jax.nn.sigmoid(forget_chan.astype(f32))
    forget = lower_bound + (1.0 - lower_bound) * sig_forget
    act_in = jax.nn.silu(in_f)
    drive_in = act_in * (1.0 - forget)
    decay_step = forget * keep_mask
    _, states = lax.associative_scan(chain_link, (decay_step, drive_in), axis=1)
    state_rows = lax.all_to_all(
        states.astype(bf16), ("seq", "rep"), split_axis=1, concat_axis=0, tiled=True
    )
    state_f = state_rows.astype(f32)
    state_scale = lax.rsqrt(jnp.mean(state_f * state_f, axis=0, keepdims=True) + EPS)
    state_norm = (state_f * state_scale).T
    state_scale_rows = state_scale.T
    gate_act = jax.nn.silu(gate_proj)
    mixed_out = (state_norm * out_gain * gate_act).astype(bf16)
    residual = token_f + jnp.dot(mixed_out, full_out, preferred_element_type=f32)
    scale_two = lax.rsqrt(jnp.mean(residual * residual, axis=-1, keepdims=True) + EPS)
    normed_two = residual * scale_two
    act_two = (normed_two * ffn_gain).astype(bf16)
    gate_ffn = jnp.dot(act_two, full_fgate, preferred_element_type=f32)
    up_ffn = jnp.dot(act_two, full_fup, preferred_element_type=f32)
    gate_silu = jax.nn.silu(gate_ffn)
    hidden = (gate_silu * up_ffn).astype(bf16)
    down_term = jnp.dot(hidden, full_fdown, preferred_element_type=f32)
    result = residual + down_term
    output_rows = result.astype(bf16)
    domain_count = counts.shape[0]
    domain_hits = domain_tags[:, None] == jnp.arange(domain_count, dtype=jnp.int32)[None, :]
    per_token = jnp.sum(jnp.where(domain_hits, counts[None, :], 0), axis=1).astype(f32)
    seq_total = all_rows // SEQ_LEN
    weighting = seq_total / (domain_count * per_token)
    grad_z = cotangent.astype(f32) * weighting[:, None]
    grad_m = grad_z.astype(bf16)
    grad_hidden = jnp.einsum("td,fd->tf", grad_m, full_fdown, preferred_element_type=f32)
    grad_gate_ffn = (grad_hidden * up_ffn * silu_grad(gate_ffn)).astype(bf16)
    grad_up_ffn = (grad_hidden * gate_silu).astype(bf16)
    back_term = jnp.einsum(
        "tf,df->td", grad_gate_ffn, full_fgate, preferred_element_type=f32
    ) + jnp.einsum("tf,df->td", grad_up_ffn, full_fup, preferred_element_type=f32)
    act_cols = act_two
    ffn_block = lax.psum_scatter(
        jnp.concatenate(
            [
                jnp.einsum("tc,tf->cf", act_cols, grad_gate_ffn, preferred_element_type=f32),
                jnp.einsum("tc,tf->cf", act_cols, grad_up_ffn, preferred_element_type=f32),
                jnp.einsum("tc,tf->cf", grad_m, hidden, preferred_element_type=f32),
            ],
            axis=1,
        ),
        ("seq", "rep"),
        scatter_dimension=0,
        tiled=True,
    )
    summed_fgate = ffn_block[:, :unit_count]
    summed_fup = ffn_block[:, unit_count : 2 * unit_count]
    summed_fdown = ffn_block[:, 2 * unit_count :].T
    grad_ffn_gain = jnp.sum(back_term * normed_two, axis=0)
    scaled_two = back_term * ffn_gain
    grad_resid = grad_z + scale_two * (
        scaled_two - normed_two * jnp.mean(scaled_two * normed_two, axis=-1, keepdims=True)
    )
    grad_branch = grad_resid.astype(bf16)
    grad_mixed = jnp.einsum("te,de->td", grad_branch, full_out, preferred_element_type=f32)
    grad_out_gain = jnp.sum(grad_mixed * state_norm * gate_act, axis=0)
    grad_gate_proj = (grad_mixed * state_norm * out_gain * silu_grad(gate_proj)).astype(bf16)
    scaled_out = grad_mixed * out_gain * gate_act
    grad_state = state_scale_rows * (
        scaled_out - state_norm * jnp.mean(scaled_out * state_norm, axis=-1, keepdims=True)
    )
    grad_state_chan = lax.all_to_all(
        grad_state.T.astype(bf16), ("seq", "rep"), split_axis=0, concat_axis=1, tiled=True
    )
    decay_next = jnp.concatenate([decay_step[:, 1:], jnp.zeros((chan_count, 1), f32)], axis=1)
    _, carried = lax.associative_scan(
        chain_link, (decay_next, grad_state_chan.astype(f32)), reverse=True, axis=1
    )
    prev_states = jnp.concatenate([jnp.zeros((chan_count, 1), f32), states[:, :-1]], axis=1)
    grad_in_chan = (carried * (1.0 - forget) * silu_grad(in_f)).astype(bf16)
    grad_forget = carried * prev_states * keep_mask - carried * act_in
    grad_fproj_chan = (grad_forget * (1.0 - lower_bound) * sig_forget * (1.0 - sig_forget)).astype(
        bf16
    )
    grad_lower = jnp.sum(grad_forget * (1.0 - sig_forget), axis=1)
    grad_probs = layer_pick * grad_lower[None, :]
    grad_bounds = layer_probs * (
        grad_probs - jnp.sum(layer_probs * grad_probs, axis=0, keepdims=True)
    )
    grad_in_rows, grad_fproj_rows = (
        lax.all_to_all(grad_in_chan, ("seq", "rep"), split_axis=1, concat_axis=0, tiled=True),
        lax.all_to_all(grad_fproj_chan, ("seq", "rep"), split_axis=1, concat_axis=0, tiled=True),
    )
    grad_act_one = (
        jnp.einsum("et,de->td", grad_in_rows, full_in, preferred_element_type=f32)
        + jnp.einsum("et,de->td", grad_fproj_rows, full_forget, preferred_element_type=f32)
        + jnp.einsum("te,de->td", grad_gate_proj, full_gate_out, preferred_element_type=f32)
    )
    grad_norm_gain = jnp.sum(grad_act_one * normed_one, axis=0)
    scaled_one = grad_act_one * norm_gain
    grad_tokens = grad_resid + scale_one * (
        scaled_one - normed_one * jnp.mean(scaled_one * normed_one, axis=-1, keepdims=True)
    )
    gain_block = jnp.concatenate(
        [
            jnp.stack([grad_norm_gain, grad_out_gain, grad_ffn_gain], axis=1),
            jnp.zeros((width, GAIN_PAD), f32),
        ],
        axis=1,
    )
    act_cols = act_one
    mixer_block = lax.psum_scatter(
        jnp.concatenate(
            [
                jnp.einsum("tc,et->ce", act_cols, grad_in_rows, preferred_element_type=f32),
                jnp.einsum("tc,et->ce", act_cols, grad_fproj_rows, preferred_element_type=f32),
                jnp.einsum("tc,te->ce", act_cols, grad_gate_proj, preferred_element_type=f32),
                jnp.einsum("tc,te->ce", mixed_out, grad_branch, preferred_element_type=f32),
                gain_block,
            ],
            axis=1,
        ),
        ("seq", "rep"),
        scatter_dimension=0,
        tiled=True,
    )
    summed_win = mixer_block[:, :width]
    summed_wforget = mixer_block[:, width : 2 * width]
    summed_wgate = mixer_block[:, 2 * width : 3 * width]
    summed_wout = mixer_block[:, 3 * width : 4 * width]
    summed_norm = mixer_block[:, 4 * width]
    summed_outg = mixer_block[:, 4 * width + 1]
    summed_ffng = mixer_block[:, 4 * width + 2]
    return (
        output_rows,
        grad_tokens,
        summed_win,
        summed_wforget,
        summed_wgate,
        summed_wout,
        summed_fgate,
        summed_fup,
        summed_fdown,
        summed_norm,
        summed_outg,
        summed_ffng,
        grad_bounds,
    )


def solution(mesh):
    placed = (
        P(("seq", "rep"), None),
        P(("seq", "rep"), None),
        P(("seq", "rep")),
        P(),
        P(),
        P("seq", None),
        P("seq", None),
        P("seq", None),
        P("seq", None),
        P("seq", None),
        P("seq", None),
        P("seq", None),
        P(),
        P(),
        P(),
        P(None, ("seq", "rep")),
    )
    return jax.shard_map(
        body,
        mesh=mesh,
        in_specs=placed,
        out_specs=(
            P(("seq", "rep"), None),
            P(("seq", "rep"), None),
            P(("seq", "rep"), None),
            P(("seq", "rep"), None),
            P(("seq", "rep"), None),
            P(("seq", "rep"), None),
            P(("seq", "rep"), None),
            P(("seq", "rep"), None),
            P(None, ("seq", "rep")),
            P(("seq", "rep")),
            P(("seq", "rep")),
            P(("seq", "rep")),
            P(None, ("seq", "rep")),
        ),
        check_vma=False,
    )
```

profile of v0, /device:TPU:0, one launch (start us, length us, event | category | flops | bytes accessed | tf_op | source)
XLA Modules:
  0.0 4270.1 jit_solution(9863755754077432784)
XLA Ops:
  13.2 74.6 %all-gather.10.cloned.1.call-done = bf16[2048,2048]{1,0:T(8,128)(2,1)} async-done(((bf16[128,2048]{1,0:T(8,128)(2,1)}), bf16[2048,2048]{1,0:T(8,128)(2,1)}) %all-gather.10.cloned.1.call-update) | async-done | bytes 8388624 | tf_op jit(solution)/shard_map/all_gather | solution.py:50
  96.6 77.7 %all-gather.8.cloned.1.call-done = bf16[2048,2048]{1,0:T(8,128)(2,1)} async-done(((bf16[128,2048]{1,0:T(8,128)(2,1)}), bf16[2048,2048]{1,0:T(8,128)(2,1)}) %all-gather.8.cloned.1.call-update) | async-done | bytes 8388624 | tf_op jit(solution)/shard_map/all_gather | solution.py:49
  185.5 26.3 all-to-all-done
  213.5 18.2 slice.627
  231.6 18.1 slice.623
  249.8 18.1 slice.622
  268.5 18.5 slice.711
  287.1 18.1 slice.625
  305.2 18.2 slice.624
  520.7 23.0 all-to-all-done.2
  595.4 109.9 %all-gather.20.cloned.1.call-done = bf16[5632,2048]{1,0:T(8,128)(2,1)} async-done(((bf16[352,2048]{1,0:T(8,128)(2,1)}), bf16[5632,2048]{1,0:T(8,128)(2,1)}) %all-gather.20.cloned.1.call-update) | async-done | bytes 23068688 | tf_op jit(solution)/shard_map/all_gather | solution.py:55
  720.4 19.3 fusion.49
  757.8 18.3 fusion.119
  776.1 88.6 %pad_maximum_fusion = f32[2048,16896]{1,0:T(8,128)} fusion(f32[2048,5632]{1,0:T(8,128)} %fusion.49, f32[2048,5632]{1,0:T(8,128)} %fusion.120, f32[2048,5632]{1,0:T(8,128)} %fusion.119), kind=kLoop, calls=%fused_computation | loop fusion | flops 69206016 | bytes 276824064 | tf_op jit(solution)/shard_map/concatenate | solution.py:123
  925.6 18.2 slice.716
  943.8 18.1 slice.714
  1003.8 18.2 slice.720
  1022.0 18.1 slice.718
  1226.3 19.9 pad.194
  1246.2 21.8 pad.195
  1377.3 154.3 %concatenate.106 = f32[2048,8320]{0,1:T(8,128)} concatenate(f32[2048,2048]{0,1:T(8,128)} %fusion.83, f32[2048,2048]{0,1:T(8,128)} %fusion.85, f32[2048,2048]{0,1:T(8,128)} %fusion.81, f32[2048,2048]{0,1:T(8,128)} %fusion.45, f32[2048,1]{0,1:T(1,128)S(1)} %bitcast.213, f32[2048,1]{0,1:T(1,128)S(1)} %bitcast.214, f32[2048,1]{0,1:T(1,128)S(1)} %bitcast.212, ...), dimensions={1} | concatenate | bytes 136314880 | tf_op jit(solution)/shard_map/concatenate | solution.py:192
  1531.7 66.8 %copy.99 = f32[2048,8320]{1,0:T(8,128)} copy(f32[2048,8320]{0,1:T(8,128)} %concatenate.106) | data formatting | bytes 136314880
  1615.0 1214.8 %all-reduce.53.cloned.1.call-done = f32[2048,16896]{1,0:T(8,128)} async-done(((f32[2048,16896]{1,0:T(8,128)}), f32[2048,16896]{1,0:T(8,128)}) %all-reduce.53.cloned.1.call-update) | async-done | bytes 138412048
  2835.0 1422.6 %reduce-scatter.4.cloned.1.call-done = f32[64,8320]{1,0:T(8,128)} async-done(((f32[2048,8320]{1,0:T(8,128)}), f32[64,8320]{1,0:T(8,128)}) %reduce-scatter.4.cloned.1.call-update) | async-done | bytes 2129936
  (475 shorter events, 733.7 us)
Async XLA Ops:
  7.2 80.6 %all-gather.10.cloned.1.call-start = ((), (), s32[]{:S(2)}) async-start(), calls=%async_computation.8 | async-start | bytes 8912896 | tf_op jit(solution)/shard_map/all_gather | solution.py:50
  7.9 166.4 %all-gather.8.cloned.1.call-start = ((), (), s32[]{:S(2)}) async-start(), calls=%async_computation.7 | async-start | bytes 8912896 | tf_op jit(solution)/shard_map/all_gather | solution.py:49
  8.7 539.0 %all-gather.12.cloned.1.call-start = ((), (), s32[]{:S(2)}) async-start(), calls=%async_computation.9 | async-start | bytes 8912896 | tf_op jit(solution)/shard_map/all_gather | solution.py:51
  9.4 544.6 %all-gather.14.cloned.1.call-start = ((), (), s32[]{:S(2)}) async-start(), calls=%async_computation.10 | async-start | bytes 8912896 | tf_op jit(solution)/shard_map/all_gather | solution.py:52
  10.0 550.4 %all-gather.18.cloned.1.call-start = ((), (), s32[]{:S(2)}) async-start(), calls=%async_computation.12 | async-start | bytes 24510464 | tf_op jit(solution)/shard_map/all_gather | solution.py:54
  10.6 572.5 %all-gather.16.cloned.1.call-start = ((), (), s32[]{:S(2)}) async-start(), calls=%async_computation.11 | async-start | bytes 24510464 | tf_op jit(solution)/shard_map/all_gather | solution.py:53
  11.1 694.1 %all-gather.20.cloned.1.call-start = ((), (), s32[]{:S(2)}) async-start(), calls=%async_computation.13 | async-start | bytes 24510464 | tf_op jit(solution)/shard_map/all_gather | solution.py:55
  13.1 534.6 %copy-start.32 = (f32[128]{0:T(128)}, f32[128]{0:T(128)S(1)}, u32[]{:S(2)}) copy-start(f32[128]{0:T(128)S(1)} %add_rsqrt_fusion.2) | copy-start | bytes 1540
  13.1 161.2 %copy-start = (bf16[128,2048]{1,0:T(8,128)(2,1)S(1)}, bf16[128,2048]{1,0:T(8,128)(2,1)}, u32[]{:S(2)}) copy-start(bf16[128,2048]{1,0:T(8,128)(2,1)} %param.16) | copy-start | bytes 1572868
  93.7 86.3 %all-to-all-start.1 = ((bf16[32,64,128]{2,1,0:T(8,128)(2,1)}), bf16[32,64,128]{2,1,0:T(8,128)(2,1)S(1)}, u32[]{:S(2)}, u32[]{:S(2)}) async-start(bf16[32,64,128]{2,1,0:T(8,128)(2,1)} %bitcast.4), calls=%async_computation.1 | async-start | bytes 1048576 | tf_op jit(solution)/shard_map/all_to_all | solution.py:68
  180.0 200.6 %copy-start.9 = (bf16[32,64,128]{2,1,0:T(8,128)(2,1)}, bf16[32,64,128]{2,1,0:T(8,128)(2,1)S(1)}, u32[]{:S(2)}) copy-start(bf16[32,64,128]{2,1,0:T(8,128)(2,1)S(1)} %all-to-all-done.1) | copy-start | bytes 1572868
  180.0 31.7 all-to-all-start
  184.1 197.7 %copy-start.35 = (f32[64]{0:T(128)}, f32[64]{0:T(128)S(1)}, u32[]{:S(2)}) copy-start(f32[64]{0:T(128)S(1)} %reduce_max.9) | copy-start | bytes 772
  184.7 197.1 %copy-start.42 = (f32[64]{0:T(128)}, f32[64]{0:T(128)S(1)}, u32[]{:S(2)}) copy-start(f32[64]{0:T(128)S(1)} %fusion.80) | copy-start | bytes 772
  184.8 197.1 %copy-start.48 = (f32[64]{0:T(128)}, f32[64]{0:T(128)S(1)}, u32[]{:S(2)}) copy-start(f32[64]{0:T(128)S(1)} %multiply_reduce_fusion.6) | copy-start | bytes 772
  184.8 197.1 %copy-start.44 = (f32[64]{0:T(128)}, f32[64]{0:T(128)S(1)}, u32[]{:S(2)}) copy-start(f32[64]{0:T(128)S(1)} %broadcast_subtract_fusion) | copy-start | bytes 772
  213.4 199.4 %copy-start.5 = (f32[64,4096]{1,0:T(8,128)}, f32[64,4096]{1,0:T(8,128)S(1)}, u32[]{:S(2)}) copy-start(f32[64,4096]{1,0:T(8,128)S(1)} %get-tuple-element.88) | copy-start | bytes 3145732
  517.6 26.1 all-to-all-start.2
  520.5 2309.3 %all-reduce.53.cloned.1.call-start = ((), (), s32[]{:S(2)}) async-start(), calls=%async_computation.15 | async-start | bytes 276824064
  520.7 199.7 %copy-start.40 = (f32[128]{0:T(128)}, f32[128]{0:T(128)S(1)}, u32[]{:S(2)}) copy-start(f32[128]{0:T(128)S(1)} %multiply_divide_fusion) | copy-start | bytes 1540
  902.9 82.9 %all-to-all-start.3 = ((bf16[32,64,128]{2,1,0:T(8,128)(2,1)}), bf16[32,64,128]{2,1,0:T(8,128)(2,1)S(1)}, u32[]{:S(2)}, u32[]{:S(2)}) async-start(bf16[32,64,128]{2,1,0:T(8,128)(2,1)} %bitcast.11), calls=%async_computation.3 | async-start | bytes 1048576 | tf_op jit(solution)/shard_map/all_to_all | solution.py:151
  1291.5 29.2 all-to-all-start.4
  1320.7 24.7 all-to-all-start.5
  1323.3 2934.2 %reduce-scatter.4.cloned.1.call-start = ((), (), s32[]{:S(2)}) async-start(), calls=%async_computation.14 | async-start | bytes 70287360
  (47 other events, 1725.3 us)
Sparse Core Ops, SparseCore 0:
  10.2 77.5 all-gather.9
  90.0 84.3 all-gather.7
  176.5 84.3 all-gather.11
  262.8 73.1 all-gather.13
  337.5 116.9 all-gather.17
  455.9 127.1 all-gather.15
  584.7 120.5 all-gather.19
  864.9 1964.8 all-reduce.52
  2832.2 1425.3 reduce-scatter.3
where the time goes:
time: 4290 us; the launch traced here: 4270 us
  waiting for transfers between devices  2980 us (69%)
  local copies, waits for them, and re-layouts  899 us (21%)
  matrix products  223 us (5%)
  other arithmetic  126 us (3%)
    unnamed x11, waiting for transfers between devices  2640 us
    slice x73, local copies, waits for them, and re-layouts, body(): lax.associative_scan(chain_link, (decay_next, grad_state_chan.astype(f32)...  254 us
    slice x69, local copies, waits for them, and re-layouts, body(): _, states = lax.associative_scan(chain_link, (decay_step, drive_in), axis=1)  223 us
    concatenate x1, local copies, waits for them, and re-layouts, body(): jnp.concatenate([jnp.einsum('tc,et->ce', act_cols, grad_in_rows, preferre...  154 us
    all_gather x1, waiting for transfers between devices, body(): lax.all_gather(ffn_down, 'seq', axis=0, tiled=True)  110 us
    concatenate x1, other arithmetic, body(): jnp.concatenate([jnp.einsum('tc,tf->cf', act_cols, grad_gate_ffn, preferr...  88.6 us
  transfers between devices with their start and end apart: 15, of which 10 were waited for; matrix products, arithmetic and copies ran while one was open for 25% of the time, Pallas kernels for 0%

commit v1 on v0

v1 whole, which is shorter than its diff:
```python
import functools

import jax
import jax.numpy as jnp
from jax import lax
from jax.experimental import pallas as pl
from jax.experimental.pallas import tpu as pltpu
from jax.sharding import Mesh
from jax.sharding import PartitionSpec as P

LAYER_AT = 12
SEQ_LEN = 1024
EPS = 1e-06
ROWS = 16
PLANE = ("p", "c", "x")
ALL = ("g", "p", "c", "x")
f32 = jnp.float32
bf16 = jnp.bfloat16


def split_hi_lo(v):
    hi = v.astype(bf16)
    return hi, (v - hi.astype(f32)).astype(bf16)


def gates(proj, chan, lower):
    ip = proj[:, :chan].astype(bf16).astype(f32)
    sf = jax.nn.sigmoid(proj[:, chan : 2 * chan].astype(bf16).astype(f32))
    forget = lower + (1.0 - lower) * sf
    sig_in = jax.nn.sigmoid(ip)
    return ip, sig_in, sf, forget


def forward_scan(chan, proj_ref, keep_ref, lower_ref, gain_ref, h_ref, o_ref, ss_ref):
    lower = lower_ref[...]
    gain = gain_ref[...]
    row = lax.broadcasted_iota(jnp.int32, (ROWS, chan), 0)

    def step(i, carry):
        rows = pl.ds(pl.multiple_of(i * ROWS, ROWS), ROWS)
        proj = proj_ref[rows, :]
        ip, sig_in, _, forget = gates(proj, chan, lower)
        u = ip * sig_in * (1.0 - forget)
        e = forget * keep_ref[rows, :]
        shift = 1
        while shift < ROWS:
            u = u + e * jnp.where(row >= shift, pltpu.roll(u, shift, 0), 0.0)
            e = e * jnp.where(row >= shift, pltpu.roll(e, shift, 0), 1.0)
            shift *= 2
        h = u + e * carry
        h_ref[rows, :] = h
        hb = h.astype(bf16).astype(f32)
        gate = proj[:, 2 * chan :]
        o_ref[rows, :] = (hb * gain * (gate * jax.nn.sigmoid(gate))).astype(bf16)
        ss_ref[rows, :] = jnp.sum(hb * hb, axis=1, keepdims=True)
        return h[ROWS - 1 : ROWS, :]

    lax.fori_loop(0, proj_ref.shape[0] // ROWS, step, jnp.zeros((1, chan), f32))


def backward_scan(
    chan, proj_ref, h_ref, do_ref, info_ref, keep_ref, lower_ref, gain_ref, grad_ref, o_ref, sums_ref
):
    lower = lower_ref[...]
    gain = gain_ref[...]
    row = lax.broadcasted_iota(jnp.int32, (ROWS, chan), 0)
    blocks = proj_ref.shape[0] // ROWS

    def step(j, carried):
        later, sum_lower, sum_gain = carried
        i = blocks - 1 - j
        rows = pl.ds(pl.multiple_of(i * ROWS, ROWS), ROWS)
        proj = proj_ref[rows, :]
        ip, sig_in, sf, forget = gates(proj, chan, lower)
        keep = keep_ref[rows, :]
        act_in = ip * sig_in
        h = h_ref[rows, :]
        before = h_ref[pl.ds(pl.multiple_of(jnp.maximum(i * ROWS - 8, 0), 8), 8), :][7:8, :]
        h_prev = jnp.where(row >= 1, pltpu.roll(h, 1, 0), before)
        scale = info_ref[rows, 0:1]
        mean = info_ref[rows, 1:2]
        hn = h.astype(bf16).astype(f32) * scale
        gate = proj[:, 2 * chan :]
        sig_gate = jax.nn.sigmoid(gate)
        gate_act = gate * sig_gate
        do = do_ref[rows, :]
        o_ref[rows, :] = (hn * gain * gate_act).astype(bf16)
        sum_gain = sum_gain + jnp.sum(do * hn * gate_act, axis=0, keepdims=True)
        dgp = do * hn * gain * (sig_gate * (1.0 + gate * (1.0 - sig_gate)))
        dhb = scale * (do * gain * gate_act - hn * mean)
        d = dhb.astype(bf16).astype(f32)
        e = forget * keep
        c = jnp.where(row < ROWS - 1, pltpu.roll(e, ROWS - 1, 0), 1.0)
        shift = 1
        while shift < ROWS:
            inside = row < ROWS - shift
            d = d + c * jnp.where(inside, pltpu.roll(d, ROWS - shift, 0), 0.0)
            c = c * jnp.where(inside, pltpu.roll(c, ROWS - shift, 0), 1.0)
            shift *= 2
        dh = d + c * later
        dip = dh * (1.0 - forget) * (sig_in * (1.0 + ip * (1.0 - sig_in)))
        df = dh * (h_prev * keep - act_in)
        tail = df * (1.0 - sf)
        dfp = tail * (1.0 - lower) * sf
        grad_ref[rows, :] = jnp.concatenate([dip, dfp, dgp], axis=1).astype(bf16)
        sum_lower = sum_lower + jnp.sum(tail, axis=0, keepdims=True)
        return (e * dh)[0:1, :], sum_lower, sum_gain

    zero = jnp.zeros((1, chan), f32)
    _, sum_lower, sum_gain = lax.fori_loop(0, blocks, step, (zero, zero, zero))
    sums_ref[...] = jnp.concatenate([sum_lower, sum_gain], axis=0)


def kernel_call(kernel, outs, *args):
    vmem = pl.BlockSpec(memory_space=pltpu.VMEM)
    return pl.pallas_call(
        kernel,
        out_shape=outs,
        in_specs=[vmem] * len(args),
        out_specs=[vmem] * len(outs),
        compiler_params=pltpu.CompilerParams(vmem_limit_bytes=48 * 2**20),
    )(*args)


def gather_plane(v):
    return lax.all_gather(v, PLANE, axis=0, tiled=True)


def scatter_plane(part, n):
    got = lax.all_to_all(
        part.reshape(n, part.shape[0] // n, part.shape[1]), PLANE, split_axis=0, concat_axis=0, tiled=True
    )
    return jnp.sum(got.astype(f32), axis=0)


def dot(a, b):
    return jnp.dot(a, b, preferred_element_type=f32)


def dot_nt(a, b):
    return lax.dot_general(a, b, (((1,), (1,)), ((), ())), preferred_element_type=f32)


def dot_tn(a, b):
    return lax.dot_general(a, b, (((0,), (0,)), ((), ())), preferred_element_type=f32)


def body(
    tokens,
    cotangent,
    domain_tags,
    doc_ids,
    counts,
    w_in,
    w_forget,
    w_gate_out,
    w_out,
    ffn_gate,
    ffn_up,
    ffn_down,
    norm_gain,
    out_gain,
    ffn_gain,
    bound_logits,
):
    groups = lax.axis_size("g")
    members = lax.axis_size("p") * lax.axis_size("c")
    copies = lax.axis_size("x")
    ranks = members * copies
    rows, width = tokens.shape
    plane_rows = rows * ranks
    units = ffn_gate.shape[1]
    g, x = lax.axis_index("g"), lax.axis_index("x")
    rank = (lax.axis_index("p") * lax.axis_size("c") + lax.axis_index("c")) * copies + x
    ce = width // (groups * ranks)
    fe = units // (groups * ranks)
    chan, unit = ce * groups, fe * groups

    def columns(w, size):
        w = w.reshape(w.shape[0], groups, members, copies, size)
        w = lax.dynamic_index_in_dim(w, x, axis=3, keepdims=False)
        return jnp.moveaxis(w, 2, 0).reshape(members, w.shape[0], groups * size)

    def half_rows(w):
        half = w.shape[0] // copies
        return lax.dynamic_slice_in_dim(w, x * half, half, axis=0)

    def own_columns(v, size):
        v = v.reshape(groups, ranks, size)
        return lax.dynamic_index_in_dim(v, rank, axis=1, keepdims=False).reshape(1, groups * size)

    def gather_rows(v):
        return lax.all_gather(v, "g", axis=0, tiled=True)

    mix = jnp.concatenate([columns(w_in, ce), columns(w_forget, ce), columns(w_gate_out, ce)], axis=2)
    mix = lax.all_to_all(mix, ("p", "c"), split_axis=0, concat_axis=0, tiled=True)
    mix_w = gather_rows(mix.reshape(-1, 3 * chan))
    out_w = gather_rows(half_rows(w_out))
    ffn = jnp.concatenate([columns(ffn_gate, fe), columns(ffn_up, fe)], axis=2)
    ffn = lax.all_to_all(ffn, ("p", "c"), split_axis=0, concat_axis=0, tiled=True)
    ffn_w = gather_rows(ffn.reshape(-1, 2 * unit))
    down_w = gather_rows(half_rows(ffn_down))

    layer_count = bound_logits.shape[0]
    layer_probs = jax.nn.softmax(bound_logits, axis=0)
    layer_index = jnp.arange(layer_count, dtype=jnp.int32)
    layer_pick = ((layer_index >= 1) & (layer_index <= LAYER_AT)).astype(f32)[:, None]
    lower = jnp.sum(layer_probs * layer_pick, axis=0)
    lower = lax.all_gather(lower, "g", axis=0, tiled=True).reshape(1, chan)
    gain = own_columns(out_gain, ce)

    places = jnp.arange(doc_ids.shape[0], dtype=jnp.int32)
    previous = jnp.concatenate([doc_ids[:1], doc_ids[:-1]])
    keep = ((places % SEQ_LEN != 0) & (doc_ids == previous)).astype(f32)[:, None]
    keep = lax.dynamic_slice_in_dim(keep, g * plane_rows, plane_rows, axis=0)

    token_f = tokens.astype(f32)
    scale_one = lax.rsqrt(jnp.mean(token_f * token_f, axis=-1, keepdims=True) + EPS)
    normed_one = token_f * scale_one
    act_one_own = (normed_one * norm_gain).astype(bf16)

    domain_count = counts.shape[0]
    domain_hits = domain_tags[:, None] == jnp.arange(domain_count, dtype=jnp.int32)[None, :]
    per_token = jnp.sum(jnp.where(domain_hits, counts[None, :], 0), axis=1).astype(f32)
    seq_total = doc_ids.shape[0] // SEQ_LEN
    grad_z = cotangent.astype(f32) * (seq_total / (domain_count * per_token))[:, None]

    both = gather_plane(jnp.concatenate([act_one_own, grad_z.astype(bf16)], axis=1))
    act_one, grad_m = both[:, :width], both[:, width:]

    proj = dot(act_one, mix_w)
    states, mixed_raw, squares = kernel_call(
        functools.partial(forward_scan, chan),
        [
            jax.ShapeDtypeStruct((plane_rows, chan), f32),
            jax.ShapeDtypeStruct((plane_rows, chan), bf16),
            jax.ShapeDtypeStruct((plane_rows, 1), f32),
        ],
        proj,
        keep,
        lower,
        gain,
    )
    pad = jnp.zeros((plane_rows, 126), bf16)
    part = jnp.concatenate(
        [dot(mixed_raw, out_w).astype(bf16), *split_hi_lo(squares), pad], axis=1
    )
    total = scatter_plane(part, ranks)
    state_scale = lax.rsqrt((total[:, width : width + 1] + total[:, width + 1 : width + 2]) / width + EPS)
    branch = total[:, :width] * state_scale
    residual = token_f + branch
    scale_two = lax.rsqrt(jnp.mean(residual * residual, axis=-1, keepdims=True) + EPS)
    normed_two = residual * scale_two
    act_two = gather_plane((normed_two * ffn_gain).astype(bf16))

    pre = dot(act_two, ffn_w)
    gate_ffn, up_ffn = pre[:, :unit], pre[:, unit:]
    sig = jax.nn.sigmoid(gate_ffn)
    gate_silu = gate_ffn * sig
    hidden = (gate_silu * up_ffn).astype(bf16)
    down_part = dot(hidden, down_w).astype(bf16)
    grad_hidden = dot_nt(grad_m, down_w)
    grad_gate = (grad_hidden * up_ffn * (sig * (1.0 + gate_ffn * (1.0 - sig)))).astype(bf16)
    grad_up = (grad_hidden * gate_silu).astype(bf16)
    grad_pre = jnp.concatenate([grad_gate, grad_up], axis=1)
    back_part = dot_nt(grad_pre, ffn_w).astype(bf16)

    def scatter_rows(v):
        return lax.psum_scatter(v.astype(bf16), "g", scatter_dimension=0, tiled=True)

    ffn_sum = scatter_rows(jnp.concatenate([dot_tn(act_two, grad_pre), dot_tn(grad_m, hidden)], axis=1))

    back_term = scatter_plane(back_part, ranks)
    gain_two = jnp.sum(back_term * normed_two, axis=0)
    scaled_two = back_term * ffn_gain
    grad_resid = grad_z + scale_two * (
        scaled_two - normed_two * jnp.mean(scaled_two * normed_two, axis=-1, keepdims=True)
    )
    grad_branch_own = grad_resid.astype(bf16)
    mean_out = jnp.sum(grad_branch_own.astype(f32) * branch, axis=-1, keepdims=True) / width
    sent = jnp.concatenate(
        [
            grad_branch_own,
            *split_hi_lo(state_scale),
            *split_hi_lo(mean_out),
            jnp.zeros((rows, 124), bf16),
        ],
        axis=1,
    )
    got = gather_plane(sent)
    grad_branch = got[:, :width]
    info = got[:, width:].astype(f32)
    info = jnp.concatenate([info[:, 0:1] + info[:, 1:2], info[:, 2:3] + info[:, 3:4]], axis=1)
    grad_mixed = dot_nt(grad_branch, out_w)
    grad_proj, mixed_out, sums = kernel_call(
        functools.partial(backward_scan, chan),
        [
            jax.ShapeDtypeStruct((plane_rows, 3 * chan), bf16),
            jax.ShapeDtypeStruct((plane_rows, chan), bf16),
            jax.ShapeDtypeStruct((2, chan), f32),
        ],
        proj,
        states,
        grad_mixed,
        info,
        keep,
        lower,
        gain,
    )
    in_part = dot_nt(grad_proj, mix_w).astype(bf16)
    mix_sum = scatter_rows(dot_tn(act_one, grad_proj))
    summed_wout = scatter_rows(dot_tn(mixed_out, grad_branch)).astype(f32)
    down_term = scatter_plane(down_part, ranks)
    output_rows = (residual + down_term).astype(bf16)

    grad_act = scatter_plane(in_part, ranks)
    gain_one = jnp.sum(grad_act * normed_one, axis=0)
    scaled_one = grad_act * norm_gain
    grad_tokens = grad_resid + scale_one * (
        scaled_one - normed_one * jnp.mean(scaled_one * normed_one, axis=-1, keepdims=True)
    )

    def spread_rows(v):
        v = lax.all_to_all(
            v.reshape(ranks, -1, v.shape[1]), PLANE, split_axis=0, concat_axis=0, tiled=True
        )
        return v

    def whole_columns(v, size):
        v = v.reshape(ranks, v.shape[1], groups, size)
        return v.transpose(1, 2, 0, 3).reshape(v.shape[1], -1).astype(f32)

    ffn_rows = spread_rows(ffn_sum)
    summed_fgate = whole_columns(ffn_rows[:, :, :unit], fe)
    summed_fup = whole_columns(ffn_rows[:, :, unit : 2 * unit], fe)
    summed_fdown = whole_columns(ffn_rows[:, :, 2 * unit :], fe).T
    mix_rows = spread_rows(mix_sum)
    summed_win = whole_columns(mix_rows[:, :, :chan], ce)
    summed_wforget = whole_columns(mix_rows[:, :, chan : 2 * chan], ce)
    summed_wgate = whole_columns(mix_rows[:, :, 2 * chan :], ce)

    sums = sums.reshape(2, groups, ce).transpose(1, 0, 2)
    sums = lax.psum_scatter(sums, "g", scatter_dimension=0, tiled=True)[0]
    grad_lower, summed_outg = sums[0], sums[1]
    grad_probs = layer_pick * grad_lower[None, :]
    grad_bounds = layer_probs * (
        grad_probs - jnp.sum(layer_probs * grad_probs, axis=0, keepdims=True)
    )
    gains = jnp.stack([gain_one.reshape(-1, ce), gain_two.reshape(-1, ce)], axis=1)
    gains = lax.psum_scatter(gains, ALL, scatter_dimension=0, tiled=True)[0]
    return (
        output_rows,
        grad_tokens,
        summed_win,
        summed_wforget,
        summed_wgate,
        summed_wout,
        summed_fgate,
        summed_fup,
        summed_fdown,
        gains[0],
        summed_outg,
        gains[1],
        grad_bounds,
    )


def solution(mesh):
    seqs, copies = mesh.shape["seq"], mesh.shape["rep"]
    mesh = Mesh(mesh.devices.reshape(seqs // 4, 2, 2, copies), ALL)
    by_rows = P(ALL, None)
    by_seq = P(("g", "p", "c"), None)
    placed = (
        (by_rows, by_rows, P(ALL), P(), P()) + (by_seq,) * 7 + (P(), P(), P(), P(None, ALL))
    )
    return jax.shard_map(
        body,
        mesh=mesh,
        in_specs=placed,
        out_specs=(by_rows,) * 8 + (P(None, ALL),) + (P(ALL),) * 3 + (P(None, ALL),),
        check_vma=False,
    )
```

time: 4290 us -> 947 us (0.22)
  waiting for transfers between devices: 2980 us -> 454 us
  local copies, waits for them, and re-layouts: 899 us -> 83.8 us
  blocking collectives: 0 us -> 225 us
  matrix products: 223 us -> 86.6 us
  other arithmetic: 126 us -> 34.3 us
    unnamed x11 -> x10, waiting for transfers between devices: 2640 us -> 0.16 us
    slice x145 -> x6, local copies, waits for them, and re-layouts: 482 us -> 6.19 us  [the longest x2 2.82 us: body(): info[:, 1:2]]
    pad x44 -> x0, local copies, waits for them, and re-layouts: 151 us -> none  [the longest x22 78.7 us: body(): lax.associative_scan(chain_link, (decay_next, grad_state_chan.astype(f32)...]
    concatenate x2 -> x3, local copies, waits for them, and re-layouts: 154 us -> 10.1 us  [the longest x1 8.04 us: body(): jnp.concatenate([dot(mixed_raw, out_w).astype(bf16), *split_hi_lo(squares...]
    all_to_all x0 -> x4, blocking collectives: none -> 144 us  [the longest x2 107 us: scatter_plane(): lax.all_to_all(part.reshape(n, part.shape[0] // n, part.shape[1]), PLANE,...]
    dot_general x21 -> x12, matrix products: 223 us -> 86.6 us  [the longest x4 29.9 us: dot(): return jnp.dot(a, b, preferred_element_type=f32)]
    reduce_scatter x0 -> x3, waiting for transfers between devices: none -> 136 us  [scatter_rows(): lax.psum_scatter(v.astype(bf16), 'g', scatter_dimension=0, tiled=True)]
    concatenate x23 -> x5, other arithmetic: 92.3 us -> 5.33 us  [the longest x1 4.12 us: body(): jnp.concatenate([dot_tn(act_two, grad_pre), dot_tn(grad_m, hidden)], axis=1)]
  transfers between devices with their start and end apart: 15 -> 14, of which waited for: 10 -> 10; matrix products, arithmetic and copies ran while one was open for 25% -> 12% of each run, Pallas kernels for 0% -> 1%
where the time goes in v1:
time: 947 us; the launch traced here: 939 us
  waiting for transfers between devices  454 us (48%)
  blocking collectives  225 us (24%)
  matrix products  86.6 us (9%)
  local copies, waits for them, and re-layouts  83.8 us (9%)
  other arithmetic  34.3 us (4%)
  Pallas kernels  20 us (2%)
  starting transfers between devices  18.4 us (2%)
  between operations  16.2 us (2%)
    reduce_scatter x3, waiting for transfers between devices, scatter_rows(): lax.psum_scatter(v.astype(bf16), 'g', scatter_dimension=0, tiled=True)  136 us
    all_gather x3, waiting for transfers between devices, gather_plane(): return lax.all_gather(v, PLANE, axis=0, tiled=True)  128 us
    all_to_all x2, blocking collectives, scatter_plane(): lax.all_to_all(part.reshape(n, part.shape[0] // n, part.shape[1]), PLANE,...  107 us
    all_gather x4, waiting for transfers between devices, gather_rows(): return lax.all_gather(v, 'g', axis=0, tiled=True)  105 us
    all_to_all x2, waiting for transfers between devices, scatter_plane(): lax.all_to_all(part.reshape(n, part.shape[0] // n, part.shape[1]), PLANE,...  84.5 us
    unnamed x3, blocking collectives  81.3 us
    dot_general x4, matrix products, dot(): return jnp.dot(a, b, preferred_element_type=f32)  29.9 us
    dot_general x4, matrix products, dot_tn(): lax.dot_general(a, b, (((0,), (0,)), ((), ())), preferred_element_type=f32)  28.7 us
  transfers between devices with their start and end apart: 14, of which 10 were waited for; matrix products, arithmetic and copies ran while one was open for 12% of the time, Pallas kernels for 1%

profile of v1, /device:TPU:0, one launch (start us, length us, event | category | flops | bytes accessed | tf_op | source)
XLA Modules:
  0.0 938.9 jit_solution(2497155260889107253)
XLA Ops:
  10.6 15.8 %all_to_all.40 = bf16[4,128,768]{1,2,0:T(8,128)(2,1)S(1)} all-to-all(bf16[4,128,768]{1,2,0:T(8,128)(2,1)S(1)} %pad_maximum_fusion.6), channel_id=1, replica_groups=mesh['g'=4,'p'=2,'c'=2,'x'=2] {'p','c'}, dimensions={0} | all-to-all | bytes 1572864 | tf_op jit(solution)/shard_map/all_to_all | solution.py:196
  37.1 21.2 %all_to_all.41 = bf16[4,128,1408]{1,2,0:T(8,128)(2,1)S(1)} all-to-all(bf16[4,128,1408]{1,2,0:T(8,128)(2,1)S(1)} %pad_maximum_fusion.4), channel_id=1, replica_groups=mesh['g'=4,'p'=2,'c'=2,'x'=2] {'p','c'}, dimensions={0} | all-to-all | bytes 2883584 | tf_op jit(solution)/shard_map/all_to_all | solution.py:200
  63.3 12.4 %all-reduce = f32[256]{0:T(256)S(1)} all-reduce(f32[256]{0:T(256)S(1)} %dynamic-update-slice), channel_id=1, replica_groups=mesh['g'=4,'p'=2,'c'=2,'x'=2] {'g'}, use_global_device_ids=true, to_apply=%add | all-reduce | flops 256 | bytes 2048
  75.7 16.1 %all-gather.10.cloned.1.call-done = bf16[2048,768]{1,0:T(8,128)(2,1)} async-done(((bf16[512,768]{1,0:T(8,128)(2,1)}), bf16[2048,768]{1,0:T(8,128)(2,1)}) %all-gather.10.cloned.1.call-update) | async-done | bytes 3145744 | tf_op jit(solution)/shard_map/all_gather | solution.py:193
  91.8 55.5 %all-gather.8.cloned.1.call-done = bf16[1024,4096]{1,0:T(8,128)(2,1)} async-done(((bf16[128,4096]{1,0:T(8,128)(2,1)}), bf16[1024,4096]{1,0:T(8,128)(2,1)}) %all-gather.8.cloned.1.call-update) | async-done | bytes 8388624 | tf_op jit(solution)/shard_map/all_gather | solution.py:126
  153.5 10.8 %shard_map.255 = (f32[1024,256]{1,0:T(8,128)S(1)}, bf16[1024,256]{1,0:T(8,128)(2,1)S(1)}, f32[1024,1]{1,0:T(8,128)S(1)}) custom-call(f32[1024,768]{1,0:T(8,128)S(1)} %fusion.10.proj_ref, f32[1024,1]{1,0:T(8,128)S(1)} %copy.188.keep_ref, f32[1,256]{1,0:T(1,128)S(1)} %bitcast.103, f32[1,256]{1,0:T(1,128)S(1)} %reshape.221.gain_ref), custom_call_target="tpu_custom_call" | custom-call | tf_op jit(solution)/shard_map/pallas_call | solution.py:116
  166.7 10.8 %all-gather.12.cloned.1.call-done = bf16[256,2048]{1,0:T(8,128)(2,1)} async-done(((bf16[64,2048]{1,0:T(8,128)(2,1)}), bf16[256,2048]{1,0:T(8,128)(2,1)}) %all-gather.12.cloned.1.call-update) | async-done | bytes 1048592 | tf_op jit(solution)/shard_map/all_gather | solution.py:193
  182.1 8.0 concatenate.31
  190.1 55.1 %all_to_all.42 = bf16[8,128,2176]{2,1,0:T(8,128)(2,1)S(1)} all-to-all(bf16[8,128,2176]{2,1,0:T(8,128)(2,1)} %bitcast.105), channel_id=1, replica_groups=mesh['g'=4,'p'=2,'c'=2,'x'=2] {'p','c','x'}, dimensions={0} | all-to-all | bytes 8912896 | tf_op jit(solution)/shard_map/all_to_all | solution.py:130
  256.9 28.9 %all-gather.16.cloned.1.call-done = bf16[2048,1408]{1,0:T(8,128)(2,1)} async-done(((bf16[512,1408]{1,0:T(8,128)(2,1)}), bf16[2048,1408]{1,0:T(8,128)(2,1)}) %all-gather.16.cloned.1.call-update) | async-done | bytes 5767184 | tf_op jit(solution)/shard_map/all_gather | solution.py:193
  285.8 37.4 %all-gather.14.cloned.1.call-done = bf16[1024,2048]{1,0:T(8,128)(2,1)} async-done(((bf16[128,2048]{1,0:T(8,128)(2,1)}), bf16[1024,2048]{1,0:T(8,128)(2,1)}) %all-gather.14.cloned.1.call-update) | async-done | bytes 4194320 | tf_op jit(solution)/shard_map/all_gather | solution.py:126
  323.2 11.7 %fusion.49 = f32[1024,1408]{1,0:T(8,128)} fusion(bf16[1024,2048]{1,0:T(8,128)(2,1)} %all-gather.14.cloned.1.call-done, bf16[2048,1408]{1,0:T(8,128)(2,1)} %all-gather.16.cloned.1.call-done), kind=kOutput, calls=%fused_computation.120 | convolution fusion | flops 5905580032 | bytes 15728640 | tf_op jit(solution)/shard_map/dot_general | solution.py:137
  334.8 49.5 %all-gather.18.cloned.1.call-done = bf16[704,2048]{1,0:T(8,128)(2,1)} async-done(((bf16[176,2048]{1,0:T(8,128)(2,1)}), bf16[704,2048]{1,0:T(8,128)(2,1)}) %all-gather.18.cloned.1.call-update) | async-done | bytes 2883600 | tf_op jit(solution)/shard_map/all_gather | solution.py:193
  384.4 10.3 %multiply_convert_fusion.1 = (bf16[1024,704]{1,0:T(8,128)(2,1)S(1)}, bf16[1024,704]{1,0:T(8,128)(2,1)S(1)}, bf16[1024,704]{1,0:T(8,128)(2,1)}) fusion(f32[1024,1408]{1,0:T(8,128)} %fusion.49, bf16[704,2048]{1,0:T(8,128)(2,1)} %all-gather.18.cloned.1.call-done, bf16[1024,4096]{1,0:T(8,128)(2,1)} %all-gather.8.cloned.1.call-done), kind=kOutput, calls=%fused_computation.25 | convolution fusion | flops 2963603456 | bytes 17694720 | tf_op jit(solution)/shard_map/dot_general | solution.py:141
  394.7 8.3 convolution_convert_fusion.1
  415.2 41.0 %all-to-all-done.4 = bf16[8,128,2048]{2,1,0:T(8,128)(2,1)} async-done(((bf16[8,128,2048]{2,1,0:T(8,128)(2,1)}), bf16[8,128,2048]{2,1,0:T(8,128)(2,1)}, u32[]{:S(2)}, u32[]{:S(2)}) %all-to-all-start.4) | async-done | bytes 4194336 | tf_op jit(solution)/shard_map/all_to_all | solution.py:130
  466.1 43.5 %all-to-all-done.3 = bf16[8,128,2048]{2,1,0:T(8,128)(2,1)} async-done(((bf16[8,128,2048]{2,1,0:T(8,128)(2,1)}), bf16[8,128,2048]{2,1,0:T(8,128)(2,1)}, u32[]{:S(2)}, u32[]{:S(2)}) %all-to-all-start.3) | async-done | bytes 4194336 | tf_op jit(solution)/shard_map/all_to_all | solution.py:130
  516.8 35.2 %all-gather.20.cloned.1.call-done = bf16[1024,2176]{1,0:T(8,128)(2,1)} async-done(((bf16[128,2176]{1,0:T(8,128)(2,1)}), bf16[1024,2176]{1,0:T(8,128)(2,1)}) %all-gather.20.cloned.1.call-update) | async-done | bytes 4456464 | tf_op jit(solution)/shard_map/all_gather | solution.py:126
  562.6 9.2 shard_map.256
  585.2 11.4 %convolution_convert_fusion = bf16[2048,1408]{0,1:T(8,128)(2,1)S(1)} fusion(bf16[1024,2048]{1,0:T(8,128)(2,1)} %all-gather.14.cloned.1.call-done, bf16[1024,704]{1,0:T(8,128)(2,1)} %copy-done.46, bf16[1024,704]{1,0:T(8,128)(2,1)} %copy-done.45), kind=kOutput, calls=%fused_computation.5 | convolution fusion | flops 5914230784 | bytes 12845056 | tf_op jit(solution)/shard_map/dot_general | solution.py:145
  613.2 51.9 %all_to_all.43 = bf16[8,128,2048]{2,1,0:T(8,128)(2,1)} all-to-all(bf16[8,128,2048]{2,1,0:T(8,128)(2,1)S(1)} %bitcast.113), channel_id=1, replica_groups=mesh['g'=4,'p'=2,'c'=2,'x'=2] {'p','c','x'}, dimensions={0} | all-to-all | bytes 8388608 | tf_op jit(solution)/shard_map/all_to_all | solution.py:130
  668.8 11.8 %all-reduce.2 = f32[4,2,64]{2,1,0:T(2,128)S(1)} all-reduce(f32[4,2,64]{2,1,0:T(2,128)S(1)} %bitcast.132), channel_id=6, replica_groups=mesh['g'=4,'p'=2,'c'=2,'x'=2] {'g'}, use_global_device_ids=true, to_apply=%region_19.20.clone | all-reduce | flops 512 | bytes 4096
  684.3 136.2 %reduce-scatter.8.cloned.1.call-done = bf16[512,2112]{0,1:T(8,128)(2,1)} async-done(((bf16[2048,2112]{0,1:T(8,128)(2,1)}), bf16[512,2112]{0,1:T(8,128)(2,1)}) %reduce-scatter.8.cloned.1.call-update) | async-done | bytes 2162704 | tf_op jit(solution)/shard_map/reduce_scatter | solution.py:269
  833.5 57.1 %all-reduce.1 = f32[32,2,64]{2,1,0:T(2,128)S(1)} all-reduce(f32[32,2,64]{2,1,0:T(2,128)S(1)} %pad_maximum_fusion.7), channel_id=5, replica_groups=mesh['g'=4,'p'=2,'c'=2,'x'=2] {'g','p','c','x'}, use_global_device_ids=true, to_apply=%region_18.19.clone | all-reduce | flops 4096 | bytes 32768
  (241 shorter events, 173.6 us)
Async XLA Ops:
  7.2 248.7 %copy-start = (bf16[352,2048]{1,0:T(8,128)(2,1)S(1)}, bf16[352,2048]{1,0:T(8,128)(2,1)}, u32[]{:S(2)}) copy-start(bf16[352,2048]{1,0:T(8,128)(2,1)} %param.27) | copy-start | bytes 4325380
  7.2 84.6 %all-gather.10.cloned.1.call-start = ((), (), s32[]{:S(2)}) async-start(), calls=%async_computation.12 | async-start | bytes 3932160 | tf_op jit(solution)/shard_map/all_gather | solution.py:193
  27.6 119.7 %all-gather.8.cloned.1.call-start = ((), (), s32[]{:S(2)}) async-start(), calls=%async_computation.11 | async-start | bytes 9437184 | tf_op jit(solution)/shard_map/all_gather | solution.py:126
  29.4 148.1 %all-gather.12.cloned.1.call-start = ((), (), s32[]{:S(2)}) async-start(), calls=%async_computation.13 | async-start | bytes 1310720 | tf_op jit(solution)/shard_map/all_gather | solution.py:193
  31.2 254.6 %all-gather.16.cloned.1.call-start = ((), (), s32[]{:S(2)}) async-start(), calls=%async_computation.15 | async-start | bytes 7208960 | tf_op jit(solution)/shard_map/all_gather | solution.py:193
  37.1 23.1 %copy-start.23 = (s32[4096]{0:T(1024)S(1)}, s32[4096]{0:T(1024)}, u32[]{:S(2)}) copy-start(s32[4096]{0:T(1024)} %param.19) | copy-start | bytes 49156
  59.9 263.3 %all-gather.14.cloned.1.call-start = ((), (), s32[]{:S(2)}) async-start(), calls=%async_computation.14 | async-start | bytes 4718592 | tf_op jit(solution)/shard_map/all_gather | solution.py:126
  63.0 90.5 %copy-start.31 = (f32[24]{0:T(128)}, f32[24]{0:T(128)S(1)}, u32[]{:S(2)}) copy-start(f32[24]{0:T(128)S(1)} %and_convert_fusion) | copy-start | bytes 292
  63.0 90.5 %copy-start.27 = (f32[64]{0:T(128)}, f32[64]{0:T(128)S(1)}, u32[]{:S(2)}) copy-start(f32[64]{0:T(128)S(1)} %fusion.37) | copy-start | bytes 772
  255.6 128.7 %all-gather.18.cloned.1.call-start = ((), (), s32[]{:S(2)}) async-start(), calls=%async_computation.16 | async-start | bytes 3604480 | tf_op jit(solution)/shard_map/all_gather | solution.py:193
  403.0 53.2 %all-to-all-start.4 = ((bf16[8,128,2048]{2,1,0:T(8,128)(2,1)}), bf16[8,128,2048]{2,1,0:T(8,128)(2,1)}, u32[]{:S(2)}, u32[]{:S(2)}) async-start(bf16[8,128,2048]{2,1,0:T(8,128)(2,1)} %bitcast.112), calls=%async_computation.4 | async-start | bytes 8388608 | tf_op jit(solution)/shard_map/all_to_all | solution.py:130
  456.2 53.4 %all-to-all-start.3 = ((bf16[8,128,2048]{2,1,0:T(8,128)(2,1)}), bf16[8,128,2048]{2,1,0:T(8,128)(2,1)}, u32[]{:S(2)}, u32[]{:S(2)}) async-start(bf16[8,128,2048]{2,1,0:T(8,128)(2,1)} %bitcast.111), calls=%async_computation.3 | async-start | bytes 8388608 | tf_op jit(solution)/shard_map/all_to_all | solution.py:130
  461.0 91.1 %all-gather.20.cloned.1.call-start = ((), (), s32[]{:S(2)}) async-start(), calls=%async_computation.17 | async-start | bytes 5013504 | tf_op jit(solution)/shard_map/all_gather | solution.py:126
  466.1 46.7 %copy-start.40 = (f32[128]{0:T(128)S(1)}, f32[128]{0:T(128)}, u32[]{:S(2)}) copy-start(f32[128]{0:T(128)} %copy-done.39) | copy-start | bytes 1540
  516.8 148.3 %reduce-scatter.4.cloned.1.call-start = ((), (), s32[]{:S(2)}) async-start(), calls=%async_computation.18 | async-start | bytes 3932160 | tf_op jit(solution)/shard_map/reduce_scatter | solution.py:269
  580.5 102.1 %reduce-scatter.6.cloned.1.call-start = ((), (), s32[]{:S(2)}) async-start(), calls=%async_computation.19 | async-start | bytes 1310720 | tf_op jit(solution)/shard_map/reduce_scatter | solution.py:269
  585.0 235.6 %reduce-scatter.8.cloned.1.call-start = ((), (), s32[]{:S(2)}) async-start(), calls=%async_computation.20 | async-start | bytes 10813440 | tf_op jit(solution)/shard_map/reduce_scatter | solution.py:269
  613.2 68.6 %copy-start.19 = (f32[24,64]{1,0:T(8,128)S(1)}, f32[24,64]{1,0:T(8,128)}, u32[]{:S(2)}) copy-start(f32[24,64]{1,0:T(8,128)} %param.31) | copy-start | bytes 18436
  613.2 68.6 %copy-start.25 = (f32[64]{0:T(128)S(1)}, f32[64]{0:T(128)}, u32[]{:S(2)}) copy-start(f32[64]{0:T(128)} %copy-done.24) | copy-start | bytes 772
  613.2 68.6 %copy-start.28 = (f32[64]{0:T(128)S(1)}, f32[64]{0:T(128)}, u32[]{:S(2)}) copy-start(f32[64]{0:T(128)} %copy-done.27) | copy-start | bytes 772
  613.2 68.6 %copy-start.32 = (f32[24]{0:T(128)S(1)}, f32[24]{0:T(128)}, u32[]{:S(2)}) copy-start(f32[24]{0:T(128)} %copy-done.31) | copy-start | bytes 292
  665.1 159.5 %all-to-all-start.6 = ((bf16[8,64,768]{2,1,0:T(8,128)(2,1)}), bf16[8,64,768]{2,1,0:T(8,128)(2,1)S(1)}, u32[]{:S(2)}, u32[]{:S(2)}) async-start(bf16[8,64,768]{2,1,0:T(8,128)(2,1)} %bitcast.129), calls=%async_computation.7 | async-start | bytes 1572864 | tf_op jit(solution)/shard_map/all_to_all | solution.py:324
  825.5 75.0 %all-to-all-start.7 = ((bf16[8,64,2112]{2,1,0:T(8,128)(2,1)}), bf16[8,64,2112]{2,1,0:T(8,128)(2,1)}, u32[]{:S(2)}, u32[]{:S(2)}) async-start(bf16[8,64,2112]{2,1,0:T(8,128)(2,1)} %bitcast.106), calls=%async_computation.10 | async-start | bytes 4456448 | tf_op jit(solution)/shard_map/all_to_all | solution.py:324
  829.9 61.3 %copy-start.13 = (f32[128,2048]{1,0:T(8,128)S(1)}, f32[128,2048]{1,0:T(8,128)}, u32[]{:S(2)}) copy-start(f32[128,2048]{1,0:T(8,128)} %get-tuple-element.44) | copy-start | bytes 3145732
  (37 other events, 233.0 us)
Sparse Core Ops, SparseCore 0:
  27.8 64.0 all-gather.9
  94.3 53.0 all-gather.7
  149.5 28.0 all-gather.11
  179.5 106.2 all-gather.15
  288.1 35.0 all-gather.13
  325.2 59.1 all-gather.17
  516.9 35.0 all-gather.19
  580.6 60.2 reduce-scatter.3
  643.7 27.1 reduce-scatter.5
  673.3 147.2 reduce-scatter.7

commit v2 on v1

--- a/solution.py
+++ b/solution.py
@@ -67,7 +67,7 @@
     blocks = proj_ref.shape[0] // ROWS
 
     def step(j, carried):
-        later, sum_lower, sum_gain = carried
+        later, sum_lower = carried
         i = blocks - 1 - j
         rows = pl.ds(pl.multiple_of(i * ROWS, ROWS), ROWS)
         proj = proj_ref[rows, :]
@@ -85,7 +85,6 @@
         gate_act = gate * sig_gate
         do = do_ref[rows, :]
         o_ref[rows, :] = (hn * gain * gate_act).astype(bf16)
-        sum_gain = sum_gain + jnp.sum(do * hn * gate_act, axis=0, keepdims=True)
         dgp = do * hn * gain * (sig_gate * (1.0 + gate * (1.0 - sig_gate)))
         dhb = scale * (do * gain * gate_act - hn * mean)
         d = dhb.astype(bf16).astype(f32)
@@ -104,11 +103,11 @@
         dfp = tail * (1.0 - lower) * sf
         grad_ref[rows, :] = jnp.concatenate([dip, dfp, dgp], axis=1).astype(bf16)
         sum_lower = sum_lower + jnp.sum(tail, axis=0, keepdims=True)
-        return (e * dh)[0:1, :], sum_lower, sum_gain
+        return (e * dh)[0:1, :], sum_lower
 
     zero = jnp.zeros((1, chan), f32)
-    _, sum_lower, sum_gain = lax.fori_loop(0, blocks, step, (zero, zero, zero))
-    sums_ref[...] = jnp.concatenate([sum_lower, sum_gain], axis=0)
+    _, sum_lower = lax.fori_loop(0, blocks, step, (zero, zero))
+    sums_ref[...] = sum_lower
 
 
 def kernel_call(kernel, outs, *args):
@@ -122,15 +121,157 @@
     )(*args)
 
 
-def gather_plane(v):
-    return lax.all_gather(v, PLANE, axis=0, tiled=True)
-
-
-def scatter_plane(part, n):
-    got = lax.all_to_all(
-        part.reshape(n, part.shape[0] // n, part.shape[1]), PLANE, split_axis=0, concat_axis=0, tiled=True
-    )
-    return jnp.sum(got.astype(f32), axis=0)
+MESH = pl.DeviceIdType.MESH
+
+
+def places():
+    g, p, c, x = (lax.axis_index(a) for a in ALL)
+    flips = ((1, 1), (0, 1), (1, 0), (0, 0))
+    chips = [(g, p + dp * (1 - 2 * p), x + dx * (1 - 2 * x)) for dp, dx in flips]
+    return chips, c
+
+
+def device_at(chip, core):
+    return (chip[0], chip[1], core, chip[2])
+
+
+def rank_at(chip, core):
+    return (chip[1] * 2 + core) * 2 + chip[2]
+
+
+def greet(partners):
+    barrier = pltpu.get_barrier_semaphore()
+    for partner in partners:
+        pl.semaphore_signal(barrier, inc=1, device_id=partner, device_id_type=MESH)
+    pl.semaphore_wait(barrier, len(partners))
+
+
+def remote(src, dst, send_sem, recv_sem, device):
+    copy = pltpu.make_async_remote_copy(
+        src_ref=src, dst_ref=dst, send_sem=send_sem, recv_sem=recv_sem, device_id=device, device_id_type=MESH
+    )
+    copy.start()
+    return copy
+
+
+def gather_kernel(own_ref, out_ref, local_sem, send_sem, recv_sem):
+    chips, core = places()
+    here = chips[3]
+    sibling = device_at(here, 1 - core)
+    greet([device_at(chip, core) for chip in chips[:3]] + [sibling])
+    slot = out_ref.at[rank_at(here, core)]
+    local = pltpu.make_async_copy(own_ref, slot, local_sem)
+    local.start()
+    direct = [
+        remote(own_ref, slot, send_sem.at[i], recv_sem.at[i], device_at(chips[i], core)) for i in range(3)
+    ]
+    passed = [remote(own_ref, slot, send_sem.at[3], recv_sem.at[3], sibling)]
+    for i in (1, 2, 0):
+        direct[i].wait_recv()
+        got = out_ref.at[rank_at(chips[i], core)]
+        passed.append(remote(got, got, send_sem.at[4 + i], recv_sem.at[4 + i], sibling))
+    for copy in direct:
+        copy.wait_send()
+    for copy in passed:
+        copy.wait()
+    local.wait()
+
+
+def scatter_kernel(part_ref, out_ref, mine, theirs, outgoing, landing, local_sem, send_sem, recv_sem):
+    chips, core = places()
+    sibling = device_at(chips[3], 1 - core)
+    greet([device_at(chip, core) for chip in chips[:3]] + [sibling])
+    swaps, locals_ = [], []
+    for j, chip in enumerate(chips):
+        swaps.append(
+            remote(
+                part_ref.at[rank_at(chip, 1 - core)], theirs.at[j], send_sem.at[j], recv_sem.at[j], sibling
+            )
+        )
+        local = pltpu.make_async_copy(part_ref.at[rank_at(chip, core)], mine.at[j], local_sem.at[j])
+        local.start()
+        locals_.append(local)
+    steps = out_ref.shape[0] // ROWS
+    sent = []
+    for j in range(4):
+        locals_[j].wait()
+        swaps[j].wait_recv()
+
+        def add(i, _, j=j):
+            rows = pl.ds(pl.multiple_of(i * ROWS, ROWS), ROWS)
+            total = mine[j, rows, :].astype(f32) + theirs[j, rows, :].astype(f32)
+            if j < 3:
+                outgoing[j, rows, :] = total.astype(bf16)
+            else:
+                out_ref[rows, :] = total
+            return 0
+
+        lax.fori_loop(0, steps, add, 0)
+        if j < 3:
+            sent.append(
+                remote(
+                    outgoing.at[j],
+                    landing.at[j],
+                    send_sem.at[4 + j],
+                    recv_sem.at[4 + j],
+                    device_at(chips[j], core),
+                )
+            )
+    for copy in sent:
+        copy.wait_recv()
+
+    def finish(i, _):
+        rows = pl.ds(pl.multiple_of(i * ROWS, ROWS), ROWS)
+        total = out_ref[rows, :]
+        for j in range(3):
+            total = total + landing[j, rows, :].astype(f32)
+        out_ref[rows, :] = total
+        return 0
+
+    lax.fori_loop(0, steps, finish, 0)
+    for copy in swaps + sent:
+        copy.wait_send()
+
+
+def gather_plane(v, ident):
+    hbm = pl.BlockSpec(memory_space=pl.ANY)
+    out = pl.pallas_call(
+        gather_kernel,
+        out_shape=jax.ShapeDtypeStruct((8,) + v.shape, v.dtype),
+        in_specs=[hbm],
+        out_specs=hbm,
+        scratch_shapes=[
+            pltpu.SemaphoreType.DMA,
+            pltpu.SemaphoreType.DMA((7,)),
+            pltpu.SemaphoreType.DMA((7,)),
+        ],
+        compiler_params=pltpu.CompilerParams(
+            collective_id=ident, has_side_effects=True, vmem_limit_bytes=48 * 2**20
+        ),
+    )(v)
+    return out.reshape(-1, v.shape[1])
+
+
+def scatter_plane(part, ident):
+    rows, wide = part.shape[0] // 8, part.shape[1]
+    return pl.pallas_call(
+        scatter_kernel,
+        out_shape=jax.ShapeDtypeStruct((rows, wide), f32),
+        in_specs=[pl.BlockSpec(memory_space=pl.ANY)],
+        out_specs=pl.BlockSpec(memory_space=pltpu.VMEM),
+        scratch_shapes=[
+            pltpu.VMEM((4, rows, wide), bf16),
+            pltpu.VMEM((4, rows, wide), bf16),
+            pltpu.VMEM((3, rows, wide), bf16),
+            pltpu.VMEM((3, rows, wide), bf16),
+            pltpu.SemaphoreType.DMA((4,)),
+            pltpu.SemaphoreType.DMA((7,)),
+            pltpu.SemaphoreType.DMA((7,)),
+        ],
+        compiler_params=pltpu.CompilerParams(
+            collective_id=ident, has_side_effects=True, vmem_limit_bytes=48 * 2**20
+        ),
+    )(part.reshape(8, rows, wide))
 
 
 def dot(a, b):
@@ -195,18 +336,31 @@
     mix = jnp.concatenate([columns(w_in, ce), columns(w_forget, ce), columns(w_gate_out, ce)], axis=2)
     mix = lax.all_to_all(mix, ("p", "c"), split_axis=0, concat_axis=0, tiled=True)
     mix_w = gather_rows(mix.reshape(-1, 3 * chan))
-    out_w = gather_rows(half_rows(w_out))
+    layer_count = bound_logits.shape[0]
+    layer_probs = jax.nn.softmax(bound_logits, axis=0)
+    layer_index = jnp.arange(layer_count, dtype=jnp.int32)
+    layer_pick = ((layer_index >= 1) & (layer_index <= LAYER_AT)).astype(f32)[:, None]
+    own_lower = jnp.sum(layer_probs * layer_pick, axis=0)[:, None]
+    top, rest = split_hi_lo(own_lower)
+    out_ext = gather_rows(
+        jnp.concatenate(
+            [
+                half_rows(w_out),
+                top,
+                rest,
+                (own_lower - top.astype(f32) - rest.astype(f32)).astype(bf16),
+                jnp.zeros((ce, 125), bf16),
+            ],
+            axis=1,
+        )
+    )
+    out_w = out_ext[:, :width]
+    lower = jnp.sum(out_ext[:, width : width + 3].astype(f32), axis=1).reshape(1, chan)
     ffn = jnp.concatenate([columns(ffn_gate, fe), columns(ffn_up, fe)], axis=2)
     ffn = lax.all_to_all(ffn, ("p", "c"), split_axis=0, concat_axis=0, tiled=True)
     ffn_w = gather_rows(ffn.reshape(-1, 2 * unit))
     down_w = gather_rows(half_rows(ffn_down))
 
-    layer_count = bound_logits.shape[0]
-    layer_probs = jax.nn.softmax(bound_logits, axis=0)
-    layer_index = jnp.arange(layer_count, dtype=jnp.int32)
-    layer_pick = ((layer_index >= 1) & (layer_index <= LAYER_AT)).astype(f32)[:, None]
-    lower = jnp.sum(layer_probs * layer_pick, axis=0)
-    lower = lax.all_gather(lower, "g", axis=0, tiled=True).reshape(1, chan)
     gain = own_columns(out_gain, ce)
 
     places = jnp.arange(doc_ids.shape[0], dtype=jnp.int32)
@@ -225,7 +379,7 @@
     seq_total = doc_ids.shape[0] // SEQ_LEN
     grad_z = cotangent.astype(f32) * (seq_total / (domain_count * per_token))[:, None]
 
-    both = gather_plane(jnp.concatenate([act_one_own, grad_z.astype(bf16)], axis=1))
+    both = gather_plane(jnp.concatenate([act_one_own, grad_z.astype(bf16)], axis=1), 0)
     act_one, grad_m = both[:, :width], both[:, width:]
 
     proj = dot(act_one, mix_w)
@@ -245,13 +399,13 @@
     part = jnp.concatenate(
         [dot(mixed_raw, out_w).astype(bf16), *split_hi_lo(squares), pad], axis=1
     )
-    total = scatter_plane(part, ranks)
+    total = scatter_plane(part, 1)
     state_scale = lax.rsqrt((total[:, width : width + 1] + total[:, width + 1 : width + 2]) / width + EPS)
     branch = total[:, :width] * state_scale
     residual = token_f + branch
     scale_two = lax.rsqrt(jnp.mean(residual * residual, axis=-1, keepdims=True) + EPS)
     normed_two = residual * scale_two
-    act_two = gather_plane((normed_two * ffn_gain).astype(bf16))
+    act_two = gather_plane((normed_two * ffn_gain).astype(bf16), 2)
 
     pre = dot(act_two, ffn_w)
     gate_ffn, up_ffn = pre[:, :unit], pre[:, unit:]
@@ -268,10 +422,11 @@
     def scatter_rows(v):
         return lax.psum_scatter(v.astype(bf16), "g", scatter_dimension=0, tiled=True)
 
-    ffn_sum = scatter_rows(jnp.concatenate([dot_tn(act_two, grad_pre), dot_tn(grad_m, hidden)], axis=1))
-
-    back_term = scatter_plane(back_part, ranks)
-    gain_two = jnp.sum(back_term * normed_two, axis=0)
+    ffn_grads = jnp.concatenate([dot_tn(act_two, grad_pre), dot_tn(grad_m, hidden)], axis=1).astype(bf16)
+    ffn_grads, back_part = lax.optimization_barrier((ffn_grads, back_part))
+    ffn_sum = scatter_rows(ffn_grads)
+
+    back_term = scatter_plane(back_part, 3)
     scaled_two = back_term * ffn_gain
     grad_resid = grad_z + scale_two * (
         scaled_two - normed_two * jnp.mean(scaled_two * normed_two, axis=-1, keepdims=True)
@@ -287,7 +442,7 @@
         ],
         axis=1,
     )
-    got = gather_plane(sent)
+    got = gather_plane(sent, 4)
     grad_branch = got[:, :width]
     info = got[:, width:].astype(f32)
     info = jnp.concatenate([info[:, 0:1] + info[:, 1:2], info[:, 2:3] + info[:, 3:4]], axis=1)
@@ -297,7 +452,7 @@
         [
             jax.ShapeDtypeStruct((plane_rows, 3 * chan), bf16),
             jax.ShapeDtypeStruct((plane_rows, chan), bf16),
-            jax.ShapeDtypeStruct((2, chan), f32),
+            jax.ShapeDtypeStruct((1, chan), f32),
         ],
         proj,
         states,
@@ -308,13 +463,27 @@
         gain,
     )
     in_part = dot_nt(grad_proj, mix_w).astype(bf16)
-    mix_sum = scatter_rows(dot_tn(act_one, grad_proj))
-    summed_wout = scatter_rows(dot_tn(mixed_out, grad_branch)).astype(f32)
-    down_term = scatter_plane(down_part, ranks)
+    mix_grads = dot_tn(act_one, grad_proj).astype(bf16).reshape(groups, -1, 3 * chan)
+    top, rest = split_hi_lo(sums.reshape(chan, 1))
+    out_grads = jnp.concatenate(
+        [dot_tn(mixed_out, grad_branch).astype(bf16), top, rest, jnp.zeros((chan, 3 * chan - 2), bf16)],
+        axis=1,
+    )
+    folds = out_grads.shape[1] // (3 * chan)
+    out_grads = out_grads[:, : folds * 3 * chan].reshape(groups, ce, folds, 3 * chan)
+    out_grads = jnp.moveaxis(out_grads, 2, 1).reshape(groups, folds * ce, 3 * chan)
+    late_grads = jnp.concatenate([mix_grads, out_grads], axis=1).reshape(-1, 3 * chan)
+    late_grads, ffn_sum = lax.optimization_barrier((late_grads, ffn_sum))
+    late_sum = scatter_rows(late_grads)
+    mix_sum = late_sum[: width // groups]
+    out_sum = jnp.moveaxis(late_sum[width // groups :].reshape(folds, ce, 3 * chan), 1, 0)
+    out_sum = out_sum.reshape(ce, -1).astype(f32)
+    summed_wout = out_sum[:, :width]
+    grad_lower = out_sum[:, width] + out_sum[:, width + 1]
+    down_term = scatter_plane(down_part, 5)
     output_rows = (residual + down_term).astype(bf16)
 
-    grad_act = scatter_plane(in_part, ranks)
-    gain_one = jnp.sum(grad_act * normed_one, axis=0)
+    grad_act = scatter_plane(in_part, 6)
     scaled_one = grad_act * norm_gain
     grad_tokens = grad_resid + scale_one * (
         scaled_one - normed_one * jnp.mean(scaled_one * normed_one, axis=-1, keepdims=True)
@@ -339,15 +508,21 @@
     summed_wforget = whole_columns(mix_rows[:, :, chan : 2 * chan], ce)
     summed_wgate = whole_columns(mix_rows[:, :, 2 * chan :], ce)
 
-    sums = sums.reshape(2, groups, ce).transpose(1, 0, 2)
-    sums = lax.psum_scatter(sums, "g", scatter_dimension=0, tiled=True)[0]
-    grad_lower, summed_outg = sums[0], sums[1]
+    first = (g * ranks + rank) * ce
+
+    def own_gain(gain, pairs):
+        total = sum(jnp.sum(grad * half_rows(w).astype(f32), axis=1) for grad, w in pairs)
+        return total / lax.dynamic_slice_in_dim(gain, first, ce, axis=0)
+
+    summed_norm = own_gain(
+        norm_gain, ((summed_win, w_in), (summed_wforget, w_forget), (summed_wgate, w_gate_out))
+    )
+    summed_outg = own_gain(out_gain, ((summed_wout, w_out),))
+    summed_ffng = own_gain(ffn_gain, ((summed_fgate, ffn_gate), (summed_fup, ffn_up)))
     grad_probs = layer_pick * grad_lower[None, :]
     grad_bounds = layer_probs * (
         grad_probs - jnp.sum(layer_probs * grad_probs, axis=0, keepdims=True)
     )
-    gains = jnp.stack([gain_one.reshape(-1, ce), gain_two.reshape(-1, ce)], axis=1)
-    gains = lax.psum_scatter(gains, ALL, scatter_dimension=0, tiled=True)[0]
     return (
         output_rows,
         grad_tokens,
@@ -358,9 +533,9 @@
         summed_fgate,
         summed_fup,
         summed_fdown,
-        gains[0],
+        summed_norm,
         summed_outg,
-        gains[1],
+        summed_ffng,
         grad_bounds,
     )
 

time: 947 us -> 601 us (0.63)
  waiting for transfers between devices: 454 us -> 73.4 us
  Pallas kernels: 20 us -> 265 us
  blocking collectives: 225 us -> 36.9 us
  starting transfers between devices: 18.4 us -> 8.35 us
    pallas_call x0 -> x7, Pallas kernels: none -> 246 us  [the longest x4 132 us: scatter_plane(): pl.pallas_call(scatter_kernel, out_shape=jax.ShapeDtypeStruct((rows, wide...]
    all_gather x3 -> x0, waiting for transfers between devices: 128 us -> none  [gather_plane(): return lax.all_gather(v, PLANE, axis=0, tiled=True)]
    reduce_scatter x3 -> x2, waiting for transfers between devices: 136 us -> 13.9 us  [scatter_rows(): lax.psum_scatter(v.astype(bf16), 'g', scatter_dimension=0, tiled=True)]
    all_to_all x2 -> x0, blocking collectives: 107 us -> none  [scatter_plane(): lax.all_to_all(part.reshape(n, part.shape[0] // n, part.shape[1]), PLANE,...]
    all_to_all x2 -> x0, waiting for transfers between devices: 84.5 us -> none  [scatter_plane(): lax.all_to_all(part.reshape(n, part.shape[0] // n, part.shape[1]), PLANE,...]
    unnamed x3 -> x0, blocking collectives: 81.3 us -> none
    all_gather x4, waiting for transfers between devices: 105 us -> 50.7 us  [gather_rows(): return lax.all_gather(v, 'g', axis=0, tiled=True)]
    unnamed x106 -> x98, local copies, waits for them, and re-layouts: 20.4 us -> 14.4 us
  transfers between devices with their start and end apart: 14 -> 8, of which waited for: 10 -> 4; matrix products, arithmetic and copies ran while one was open for 12% -> 22% of each run, Pallas kernels for 1% -> 45%
where the time goes in v2:
time: 601 us; the launch traced here: 592 us
  Pallas kernels  265 us (44%)
  matrix products  83 us (14%)
  local copies, waits for them, and re-layouts  78.2 us (13%)
  waiting for transfers between devices  73.4 us (12%)
  blocking collectives  36.9 us (6%)
  other arithmetic  31.7 us (5%)
  between operations  15.5 us (3%)
  starting transfers between devices  8.35 us (1%)
    pallas_call x4, Pallas kernels, scatter_plane(): pl.pallas_call(scatter_kernel, out_shape=jax.ShapeDtypeStruct((rows, wide...  132 us
    pallas_call x3, Pallas kernels, gather_plane(): pl.pallas_call(gather_kernel, out_shape=jax.ShapeDtypeStruct((8,) + v.sha...  114 us
    all_gather x4, waiting for transfers between devices, gather_rows(): return lax.all_gather(v, 'g', axis=0, tiled=True)  50.7 us
    dot_general x4, matrix products, dot_nt(): lax.dot_general(a, b, (((1,), (1,)), ((), ())), preferred_element_type=f32)  30 us
    dot_general x4, matrix products, dot(): return jnp.dot(a, b, preferred_element_type=f32)  27.4 us
    dot_general x4, matrix products, dot_tn(): lax.dot_general(a, b, (((0,), (0,)), ((), ())), preferred_element_type=f32)  25.6 us
    convert_element_type x15, local copies, waits for them, and re-layouts, whole_columns(): return v.transpose(1, 2, 0, 3).reshape(v.shape[1], -1).astype(f32)  21.1 us
    all_to_all x1, blocking collectives, body(): lax.all_to_all(ffn, ('p', 'c'), split_axis=0, concat_axis=0, tiled=True)  21.1 us
  transfers between devices with their start and end apart: 8, of which 4 were waited for; matrix products, arithmetic and copies ran while one was open for 22% of the time, Pallas kernels for 45%

profile of v2, /device:TPU:0, one launch (start us, length us, event | category | flops | bytes accessed | tf_op | source)
XLA Modules:
  0.0 592.5 jit_solution(7749516159143514532)
XLA Ops:
  14.1 15.8 %all_to_all.20 = bf16[4,128,768]{1,2,0:T(8,128)(2,1)} all-to-all(bf16[4,128,768]{1,2,0:T(8,128)(2,1)S(1)} %pad_maximum_fusion.7), channel_id=1, replica_groups=mesh['g'=4,'p'=2,'c'=2,'x'=2] {'p','c'}, dimensions={0} | all-to-all | bytes 1572864 | tf_op jit(solution)/shard_map/all_to_all | solution.py:337
  38.1 21.1 %all_to_all.21 = bf16[4,128,1408]{1,2,0:T(8,128)(2,1)S(1)} all-to-all(bf16[4,128,1408]{1,2,0:T(8,128)(2,1)S(1)} %pad_maximum_fusion.5), channel_id=1, replica_groups=mesh['g'=4,'p'=2,'c'=2,'x'=2] {'p','c'}, dimensions={0} | all-to-all | bytes 2883584 | tf_op jit(solution)/shard_map/all_to_all | solution.py:360
  64.3 54.2 %shard_map.255 = bf16[8,128,4096]{2,1,0:T(8,128)(2,1)} custom-call(bf16[128,4096]{1,0:T(8,128)(2,1)S(1)} %pad_maximum_fusion.6.own_ref), custom_call_target="tpu_custom_call" | custom-call | tf_op jit(solution)/shard_map/pallas_call | solution.py:238
  119.5 6.5 %fusion.10.proj_ref = f32[1024,768]{1,0:T(8,128)S(1)} fusion(bf16[2048,768]{1,0:T(8,128)(2,1)} %all-gather.5.cloned.1.call-done, bf16[1024,4096]{1,0:T(8,128)(2,1)} %bitcast.126), kind=kOutput, calls=%fused_computation.17 | convolution fusion | flops 3221225472 | bytes 10485760 | tf_op jit(solution)/shard_map/dot_general | solution.py:278
  126.0 10.8 %shard_map.256 = (f32[1024,256]{1,0:T(8,128)S(1)}, bf16[1024,256]{1,0:T(8,128)(2,1)S(1)}, f32[1024,1]{1,0:T(8,128)S(1)}) custom-call(f32[1024,768]{1,0:T(8,128)S(1)} %fusion.10.proj_ref, f32[1024,1]{1,0:T(8,128)S(1)} %copy.176.keep_ref, f32[1,256]{1,0:T(1,128)S(1)} %bitcast.122, f32[1,256]{1,0:T(1,128)S(1)} %reshape.327.gain_ref), custom_call_target="tpu_custom_call" | custom-call | tf_op jit(solution)/shard_map/pallas_call | solution.py:115
  140.3 7.8 %concatenate.41 = bf16[1024,2176]{1,0:T(8,128)(2,1)} concatenate(bf16[1024,2048]{1,0:T(8,128)(2,1)} %convolution_convert_fusion.3, bf16[1024,1]{1,0:T(8,128)(2,1)S(1)} %get-tuple-element.43, bf16[1024,1]{1,0:T(8,128)(2,1)S(1)} %get-tuple-element.42, bf16[1024,126]{1,0:T(8,128)(2,1)S(1)} %broadcast_in_dim.23), dimensions={1} | concatenate | bytes 8912896 | tf_op jit(solution)/shard_map/concatenate | solution.py:399
  150.4 30.2 %shard_map.257 = f32[128,2176]{1,0:T(8,128)S(1)} custom-call(bf16[8,128,2176]{2,1,0:T(8,128)(2,1)S(1)} %bitcast.113), custom_call_target="tpu_custom_call" | custom-call | tf_op jit(solution)/shard_map/pallas_call | solution.py:257
  182.3 29.1 %shard_map.258 = bf16[8,128,2048]{2,1,0:T(8,128)(2,1)S(1)} custom-call(bf16[128,2048]{1,0:T(8,128)(2,1)S(1)} %multiply_convert_fusion.3.own_ref), custom_call_target="tpu_custom_call" | custom-call | tf_op jit(solution)/shard_map/pallas_call | solution.py:238
  216.5 11.9 %fusion.53 = f32[1024,1408]{1,0:T(8,128)} fusion(bf16[1024,2048]{1,0:T(8,128)(2,1)} %bitcast.120, bf16[2048,1408]{1,0:T(8,128)(2,1)} %all-gather.9.cloned.1.call-done), kind=kOutput, calls=%fused_computation.127 | convolution fusion | flops 5905580032 | bytes 15728640 | tf_op jit(solution)/shard_map/dot_general | solution.py:278
  228.3 47.7 %all-gather.11.cloned.1.call-done = bf16[704,2048]{1,0:T(8,128)(2,1)} async-done(((bf16[176,2048]{1,0:T(8,128)(2,1)}), bf16[704,2048]{1,0:T(8,128)(2,1)}) %all-gather.11.cloned.1.call-update) | async-done | bytes 2883600 | tf_op jit(solution)/shard_map/all_gather | solution.py:334
  276.0 9.0 %multiply_convert_fusion.1 = (bf16[1024,704]{1,0:T(8,128)(2,1)S(1)}, bf16[1024,704]{1,0:T(8,128)(2,1)S(1)}, bf16[1024,704]{1,0:T(8,128)(2,1)S(1)}) fusion(f32[1024,1408]{1,0:T(8,128)} %fusion.53, bf16[704,2048]{1,0:T(8,128)(2,1)} %all-gather.11.cloned.1.call-done, bf16[1024,4096]{1,0:T(8,128)(2,1)} %bitcast.127), kind=kOutput, calls=%fused_computation.22 | convolution fusion | flops 2963603456 | bytes 17694720 | tf_op jit(solution)/shard_map/dot_general | solution.py:282
  285.0 7.1 %fusion.15 = bf16[2048,704]{0,1:T(8,128)(2,1)S(1)} fusion(bf16[1024,704]{1,0:T(8,128)(2,1)S(1)} %get-tuple-element.46, bf16[1024,4096]{1,0:T(8,128)(2,1)} %bitcast.128), kind=kOutput, calls=%fused_computation.20 | convolution fusion | flops 2954231808 | bytes 8519680 | tf_op jit(solution)/shard_map/dot_general | solution.py:286
  292.2 8.3 %convolution_convert_fusion = bf16[2048,1408]{0,1:T(8,128)(2,1)S(1)} fusion(bf16[1024,2048]{1,0:T(8,128)(2,1)S(1)} %bitcast.121, bf16[1024,704]{1,0:T(8,128)(2,1)S(1)} %get-tuple-element.45, bf16[1024,704]{1,0:T(8,128)(2,1)S(1)} %get-tuple-element.44), kind=kOutput, calls=%fused_computation.1 | convolution fusion | flops 5914230784 | bytes 12845056 | tf_op jit(solution)/shard_map/dot_general | solution.py:286
  304.6 11.5 %convolution_convert_fusion.1 = bf16[1024,2048]{1,0:T(8,128)(2,1)} fusion(bf16[2048,1408]{1,0:T(8,128)(2,1)} %all-gather.9.cloned.1.call-done, bf16[1024,704]{1,0:T(8,128)(2,1)} %copy-done.45, bf16[1024,704]{1,0:T(8,128)(2,1)} %copy-done.44), kind=kOutput, calls=%fused_computation.3 | convolution fusion | flops 5913444352 | bytes 12845056 | tf_op jit(solution)/shard_map/dot_general | solution.py:282
  316.2 5.7 convolution_convert_fusion.2
  321.9 28.7 %shard_map.259 = f32[128,2048]{1,0:T(8,128)S(1)} custom-call(bf16[8,128,2048]{2,1,0:T(8,128)(2,1)S(1)} %bitcast.118), custom_call_target="tpu_custom_call" | custom-call | tf_op jit(solution)/shard_map/pallas_call | solution.py:257
  350.7 28.8 %shard_map.260 = f32[128,2048]{1,0:T(8,128)S(1)} custom-call(bf16[8,128,2048]{2,1,0:T(8,128)(2,1)S(1)} %bitcast.117), custom_call_target="tpu_custom_call" | custom-call | tf_op jit(solution)/shard_map/pallas_call | solution.py:257
  382.1 30.8 %shard_map.261 = bf16[8,128,2176]{2,1,0:T(8,128)(2,1)S(1)} custom-call(bf16[128,2176]{1,0:T(8,128)(2,1)S(1)} %concatenate.45.own_ref), custom_call_target="tpu_custom_call" | custom-call | tf_op jit(solution)/shard_map/pallas_call | solution.py:238
  419.1 9.0 %shard_map.262 = (bf16[1024,768]{1,0:T(8,128)(2,1)S(1)}, bf16[1024,256]{1,0:T(8,128)(2,1)S(1)}, f32[1,256]{1,0:T(1,128)S(1)}) custom-call(f32[1024,768]{1,0:T(8,128)} %copy-done.3, f32[1024,256]{1,0:T(8,128)S(1)} %copy-done.9, f32[1024,256]{1,0:T(8,128)S(1)} %fusion.2.do_ref, f32[1024,2]{1,0:T(8,128)S(1)} %copy.188.info_ref, f32[1024,1]{1,0:T(8,128)S(1)} %copy.176.keep_ref, ...), custom_call_target="tpu_custom_call" | custom-call | tf_op jit(solution)/shard_map/pallas_call | solution.py:115
  441.7 5.7 fusion.12
  449.7 13.9 %reduce-scatter.3.cloned.1.call-done = bf16[512,2112]{0,1:T(8,128)(2,1)} async-done(((bf16[2048,2112]{0,1:T(8,128)(2,1)}), bf16[512,2112]{0,1:T(8,128)(2,1)}) %reduce-scatter.3.cloned.1.call-update) | async-done | bytes 2162704 | tf_op jit(solution)/shard_map/reduce_scatter | solution.py:423
  472.3 6.0 %convolution_convert_fusion.4 = bf16[1024,2048]{1,0:T(8,128)(2,1)S(1)} fusion(bf16[1024,768]{1,0:T(8,128)(2,1)S(1)} %get-tuple-element.27, bf16[2048,768]{1,0:T(8,128)(2,1)} %all-gather.5.cloned.1.call-done), kind=kOutput, calls=%fused_computation.6 | convolution fusion | flops 3223322624 | bytes 8912896 | tf_op jit(solution)/shard_map/dot_general | solution.py:282
  478.3 43.8 %shard_map.263 = f32[128,2048]{1,0:T(8,128)S(1)} custom-call(bf16[8,128,2048]{2,1,0:T(8,128)(2,1)S(1)} %bitcast.119), custom_call_target="tpu_custom_call" | custom-call | tf_op jit(solution)/shard_map/pallas_call | solution.py:257
  567.0 8.7 %all-to-all-done.2 = bf16[8,64,768]{2,1,0:T(8,128)(2,1)S(1)} async-done(((bf16[8,64,768]{2,1,0:T(8,128)(2,1)}), bf16[8,64,768]{2,1,0:T(8,128)(2,1)S(1)}, u32[]{:S(2)}, u32[]{:S(2)}) %all-to-all-start.2) | async-done | bytes 786464 | tf_op jit(solution)/shard_map/all_to_all | solution.py:493
  (232 shorter events, 124.9 us)
Async XLA Ops:
  7.2 53.7 %copy-start = (bf16[352,2048]{1,0:T(8,128)(2,1)S(1)}, bf16[352,2048]{1,0:T(8,128)(2,1)}, u32[]{:S(2)}) copy-start(bf16[352,2048]{1,0:T(8,128)(2,1)} %param.27) | copy-start | bytes 4325380
  7.2 111.3 %all-gather.7.cloned.1.call-start = ((), (), s32[]{:S(2)}) async-start(), calls=%async_computation.7 | async-start | bytes 1392640 | tf_op jit(solution)/shard_map/all_gather | solution.py:334
  11.9 107.6 %all-gather.5.cloned.1.call-start = ((), (), s32[]{:S(2)}) async-start(), calls=%async_computation.6 | async-start | bytes 3932160 | tf_op jit(solution)/shard_map/all_gather | solution.py:334
  32.3 184.2 %all-gather.9.cloned.1.call-start = ((), (), s32[]{:S(2)}) async-start(), calls=%async_computation.8 | async-start | bytes 7208960 | tf_op jit(solution)/shard_map/all_gather | solution.py:334
  60.8 215.2 %all-gather.11.cloned.1.call-start = ((), (), s32[]{:S(2)}) async-start(), calls=%async_computation.9 | async-start | bytes 3604480 | tf_op jit(solution)/shard_map/all_gather | solution.py:334
  61.8 401.8 %reduce-scatter.3.cloned.1.call-start = ((), (), s32[]{:S(2)}) async-start(), calls=%async_computation.10 | async-start | bytes 10813440 | tf_op jit(solution)/shard_map/reduce_scatter | solution.py:423
  62.7 55.8 %copy-start.39 = (f32[128]{0:T(128)}, f32[128]{0:T(128)S(1)}, u32[]{:S(2)}) copy-start(f32[128]{0:T(128)S(1)} %add_rsqrt_fusion.2) | copy-start | bytes 1540
  126.0 14.2 %copy-start.3 = (f32[1024,768]{1,0:T(8,128)}, f32[1024,768]{1,0:T(8,128)S(1)}, u32[]{:S(2)}) copy-start(f32[1024,768]{1,0:T(8,128)S(1)} %fusion.10.proj_ref) | copy-start | bytes 9437188
  126.0 10.9 %copy-start.25 = (bf16[256,2176]{1,0:T(8,128)(2,1)S(1)}, bf16[256,2176]{1,0:T(8,128)(2,1)}, u32[]{:S(2)}) copy-start(bf16[256,2176]{1,0:T(8,128)(2,1)} %all-gather.7.cloned.1.call-done) | copy-start | bytes 3342340
  150.4 31.7 %copy-start.29 = (f32[2048]{0:T(1024)S(1)}, f32[2048]{0:T(1024)}, u32[]{:S(2)}) copy-start(f32[2048]{0:T(1024)} %param.30) | copy-start | bytes 24580
  285.0 7.2 %copy-start.43 = (bf16[1024,704]{1,0:T(8,128)(2,1)}, bf16[1024,704]{1,0:T(8,128)(2,1)S(1)}, u32[]{:S(2)}) copy-start(bf16[1024,704]{1,0:T(8,128)(2,1)S(1)} %get-tuple-element.46) | copy-start | bytes 4325380
  285.0 7.2 %copy-start.44 = (bf16[1024,704]{1,0:T(8,128)(2,1)}, bf16[1024,704]{1,0:T(8,128)(2,1)S(1)}, u32[]{:S(2)}) copy-start(bf16[1024,704]{1,0:T(8,128)(2,1)S(1)} %get-tuple-element.44) | copy-start | bytes 4325380
  285.0 7.2 %copy-start.45 = (bf16[1024,704]{1,0:T(8,128)(2,1)}, bf16[1024,704]{1,0:T(8,128)(2,1)S(1)}, u32[]{:S(2)}) copy-start(bf16[1024,704]{1,0:T(8,128)(2,1)S(1)} %get-tuple-element.45) | copy-start | bytes 4325380
  316.1 241.9 %reduce-scatter.5.cloned.1.call-start = ((), (), s32[]{:S(2)}) async-start(), calls=%async_computation.11 | async-start | bytes 5406720 | tf_op jit(solution)/shard_map/reduce_scatter | solution.py:423
  321.9 28.8 %copy-start.5 = (bf16[1024,2048]{1,0:T(8,128)(2,1)S(1)}, bf16[1024,2048]{1,0:T(8,128)(2,1)}, u32[]{:S(2)}) copy-start(bf16[1024,2048]{1,0:T(8,128)(2,1)} %convolution_convert_fusion.1) | copy-start | bytes 12582916
  350.7 28.8 %copy-start.11 = (f32[128,2048]{1,0:T(8,128)S(1)}, f32[128,2048]{1,0:T(8,128)}, u32[]{:S(2)}) copy-start(f32[128,2048]{1,0:T(8,128)} %copy-done.10) | copy-start | bytes 3145732
  350.7 29.1 %copy-start.22 = (bf16[128,2048]{1,0:T(8,128)(2,1)S(1)}, bf16[128,2048]{1,0:T(8,128)(2,1)}, u32[]{:S(2)}) copy-start(bf16[128,2048]{1,0:T(8,128)(2,1)} %param.17) | copy-start | bytes 1572868
  382.1 33.3 %copy-start.26 = (bf16[256,2176]{1,0:T(8,128)(2,1)S(1)}, bf16[256,2176]{1,0:T(8,128)(2,1)}, u32[]{:S(2)}) copy-start(bf16[256,2176]{1,0:T(8,128)(2,1)} %all-gather.7.cloned.1.call-done) | copy-start | bytes 3342340
  467.7 56.2 %all-to-all-start.3 = ((bf16[8,64,2112]{2,1,0:T(8,128)(2,1)}), bf16[8,64,2112]{2,1,0:T(8,128)(2,1)}, u32[]{:S(2)}, u32[]{:S(2)}) async-start(bf16[8,64,2112]{2,1,0:T(8,128)(2,1)} %bitcast.125), calls=%async_computation.5 | async-start | bytes 4456448 | tf_op jit(solution)/shard_map/all_to_all | solution.py:493
  478.3 43.9 %copy-start.13 = (bf16[128,2048]{1,0:T(8,128)(2,1)S(1)}, bf16[128,2048]{1,0:T(8,128)(2,1)}, u32[]{:S(2)}) copy-start(bf16[128,2048]{1,0:T(8,128)(2,1)} %param.16) | copy-start | bytes 1572868
  478.3 43.9 %copy-start.40 = (f32[128]{0:T(128)S(1)}, f32[128]{0:T(128)}, u32[]{:S(2)}) copy-start(f32[128]{0:T(128)} %copy-done.39) | copy-start | bytes 1540
  478.3 44.2 %copy-start.16 = (f32[128,2048]{1,0:T(8,128)S(1)}, f32[128,2048]{1,0:T(8,128)}, u32[]{:S(2)}) copy-start(f32[128,2048]{1,0:T(8,128)} %get-tuple-element.37) | copy-start | bytes 3145732
  545.3 8.8 %copy-start.14 = (f32[64,5632]{1,0:T(8,128)}, f32[64,5632]{1,0:T(8,128)S(1)}, u32[]{:S(2)}) copy-start(f32[64,5632]{1,0:T(8,128)S(1)} %reshape.351) | copy-start | bytes 4325380
  560.2 15.6 %all-to-all-start.2 = ((bf16[8,64,768]{2,1,0:T(8,128)(2,1)}), bf16[8,64,768]{2,1,0:T(8,128)(2,1)S(1)}, u32[]{:S(2)}, u32[]{:S(2)}) async-start(bf16[8,64,768]{2,1,0:T(8,128)(2,1)} %bitcast.38), calls=%async_computation.4 | async-start | bytes 1572864 | tf_op jit(solution)/shard_map/all_to_all | solution.py:493
  (31 other events, 116.7 us)
Sparse Core Ops, SparseCore 0:
  12.0 31.6 all-gather.6
  45.9 62.9 all-gather.4
  111.1 105.3 all-gather.8
  218.5 57.4 all-gather.10
  316.2 147.2 reduce-scatter.2
  465.7 79.6 reduce-scatter.4

commit v3 on v2

--- a/solution.py
+++ b/solution.py
@@ -12,6 +12,7 @@
 SEQ_LEN = 1024
 EPS = 1e-06
 ROWS = 16
+HALVES = 2
 PLANE = ("p", "c", "x")
 ALL = ("g", "p", "c", "x")
 f32 = jnp.float32
@@ -177,6 +178,211 @@
     local.wait()
 
 
+class Line:
+    def __init__(self, groups, own_ref, out_ref, send_sem, recv_sem):
+        self.groups, self.own, self.out = groups, own_ref, out_ref
+        self.send_sem, self.recv_sem = send_sem, recv_sem
+        self.g, self.p, self.c, self.x = (lax.axis_index(a) for a in ALL)
+
+    def at_step(self, way, k):
+        block = self.g - (k - 1) if way == 0 else self.g + (k - 1)
+        return pltpu.make_async_remote_copy(
+            src_ref=self.own if k == 1 else self.out.at[block],
+            dst_ref=self.out.at[block],
+            send_sem=self.send_sem.at[way, k - 1],
+            recv_sem=self.recv_sem.at[way, k - 1],
+            device_id=(self.g + (1 if way == 0 else -1), self.p, self.c, self.x),
+            device_id_type=MESH,
+        )
+
+    def behind(self, way, k):
+        return self.g >= k if way == 0 else self.g + k < self.groups
+
+    def sends(self, way, k):
+        return self.behind(way, k - 1) & self.behind(1 - way, 1)
+
+    def send(self, k):
+        for way in (0, 1):
+
+            @pl.when(self.sends(way, k))
+            def _(way=way):
+                self.at_step(way, k).start()
+
+    def step(self, k):
+        for way in (0, 1):
+
+            @pl.when(self.behind(way, k))
+            def _(way=way):
+                block = self.g - k if way == 0 else self.g + k
+                got = self.out.at[block]
+                pltpu.make_async_remote_copy(
+                    src_ref=got,
+                    dst_ref=got,
+                    send_sem=self.send_sem.at[way, k - 1],
+                    recv_sem=self.recv_sem.at[way, k - 1],
+                    device_id=(self.g, self.p, self.c, self.x),
+                    device_id_type=MESH,
+                ).wait_recv()
+
+        if k + 1 < self.groups:
+            self.send(k + 1)
+
+    def finish(self):
+        for k in range(1, self.groups):
+            for way in (0, 1):
+
+                @pl.when(self.sends(way, k))
+                def _(way=way, k=k):
+                    self.at_step(way, k).wait_send()
+
+
+def line_partners(groups):
+    g, p, c, x = (lax.axis_index(a) for a in ALL)
+    offsets = sorted({1 % groups, -1 % groups} - {0})
+    return [(lax.rem(g + k, groups), p, c, x) for k in offsets]
+
+
+class Plane:
+    def __init__(self, own_ref, out_ref, local_sem, send_sem, recv_sem):
+        self.own, self.out = own_ref, out_ref
+        self.send_sem, self.recv_sem = send_sem, recv_sem
+        self.chips, self.core = places()
+        self.slot = out_ref.at[rank_at(self.chips[3], self.core)]
+        self.sibling = device_at(self.chips[3], 1 - self.core)
+        self.local = pltpu.make_async_copy(own_ref, self.slot, local_sem)
+        self.direct, self.passed = {}, []
+
+    def start_own(self):
+        self.local.start()
+        self.passed.append(
+            remote(self.own, self.slot, self.send_sem.at[3], self.recv_sem.at[3], self.sibling)
+        )
+
+    def start(self, i):
+        self.direct[i] = remote(
+            self.own, self.slot, self.send_sem.at[i], self.recv_sem.at[i], device_at(self.chips[i], self.core)
+        )
+
+    def hand_on(self, i):
+        self.direct[i].wait_recv()
+        got = self.out.at[rank_at(self.chips[i], self.core)]
+        self.passed.append(remote(got, got, self.send_sem.at[4 + i], self.recv_sem.at[4 + i], self.sibling))
+
+    def finish(self):
+        for copy in self.direct.values():
+            copy.wait_send()
+        for copy in self.passed:
+            copy.wait()
+        self.local.wait()
+
+
+def spread_kernel(
+    groups,
+    mix_ref,
+    ffn_ref,
+    out_ref,
+    act_ref,
+    grad_ref,
+    mix_all,
+    ffn_all,
+    out_all,
+    act_all,
+    grad_all,
+    local_sem,
+    swap_send,
+    swap_recv,
+    mix_send,
+    mix_recv,
+    out_send,
+    out_recv,
+    act_send,
+    act_recv,
+    grad_send,
+    grad_recv,
+):
+    chips, core = places()
+    here, other = chips[3], chips[2]
+    g = here[0]
+    swaps = [device_at(here, 1 - core), device_at(other, core), device_at(other, 1 - core)]
+    greet([device_at(chip, core) for chip in chips[:3]] + [swaps[0], swaps[2]] + line_partners(groups))
+    own = here[1] * 2 + core
+    targets = [here[1] * 2 + 1 - core, other[1] * 2 + core, other[1] * 2 + 1 - core]
+
+    def swap(src, dst, first):
+        return [
+            remote(
+                src.at[targets[i]], dst, swap_send.at[first + i], swap_recv.at[first + i], swaps[i]
+            )
+            for i in range(3)
+        ]
+
+    mix_copies = swap(mix_ref, mix_all.at[g, own], 0)
+    locals_ = [
+        pltpu.make_async_copy(mix_ref.at[own], mix_all.at[g, own], local_sem.at[0]),
+        pltpu.make_async_copy(ffn_ref.at[own], ffn_all.at[own], local_sem.at[1]),
+        pltpu.make_async_copy(out_ref, out_all.at[g], local_sem.at[2]),
+    ]
+    for copy in locals_:
+        copy.start()
+    out_line = Line(groups, out_ref, out_all, out_send, out_recv)
+    mix_line = Line(groups, mix_all.at[g], mix_all, mix_send, mix_recv)
+    out_line.send(1)
+    act = Plane(act_ref, act_all, local_sem.at[3], act_send, act_recv)
+    grad = Plane(grad_ref, grad_all, local_sem.at[4], grad_send, grad_recv)
+    act.start_own()
+    grad.start_own()
+    act.start(1)
+    for copy in mix_copies:
+        copy.wait()
+    locals_[0].wait()
+    mix_line.send(1)
+    act.start(2)
+    act.start(0)
+    ffn_copies = swap(ffn_ref, ffn_all.at[own], 3)
+    out_line.step(1)
+    for i in (1, 2, 0):
+        grad.start(i)
+    mix_line.step(1)
+    for i in (1, 2, 0):
+        act.hand_on(i)
+    for k in range(2, groups):
+        out_line.step(k)
+        mix_line.step(k)
+    for i in (1, 2, 0):
+        grad.hand_on(i)
+    for copy in ffn_copies:
+        copy.wait()
+    locals_[1].wait()
+    locals_[2].wait()
+    out_line.finish()
+    mix_line.finish()
+    act.finish()
+    grad.finish()
+
+
+def spread(groups, mix, ffn, out, act, grad, ident):
+    hbm = pl.BlockSpec(memory_space=pl.ANY)
+    dma = pltpu.SemaphoreType.DMA
+    return pl.pallas_call(
+        functools.partial(spread_kernel, groups),
+        out_shape=[
+            jax.ShapeDtypeStruct((groups,) + mix.shape, bf16),
+            jax.ShapeDtypeStruct(ffn.shape, bf16),
+            jax.ShapeDtypeStruct((groups,) + out.shape, bf16),
+            jax.ShapeDtypeStruct((8,) + act.shape, bf16),
+            jax.ShapeDtypeStruct((8,) + grad.shape, bf16),
+        ],
+        in_specs=[hbm] * 5,
+        out_specs=[hbm] * 5,
+        scratch_shapes=[dma((5,)), dma((6,)), dma((6,))]
+        + [dma((2, groups - 1))] * 4
+        + [dma((7,))] * 4,
+        compiler_params=pltpu.CompilerParams(
+            collective_id=ident, has_side_effects=True, vmem_limit_bytes=48 * 2**20
+        ),
+    )(mix, ffn, out, act, grad)
+
+
 def scatter_kernel(part_ref, out_ref, mine, theirs, outgoing, landing, local_sem, send_sem, recv_sem):
     chips, core = places()
     sibling = device_at(chips[3], 1 - core)
@@ -231,6 +437,63 @@
     lax.fori_loop(0, steps, finish, 0)
     for copy in swaps + sent:
         copy.wait_send()
+
+
+def collect_kernel(count, size, *refs):
+    parts, outs = refs[:count], refs[count : count + 3]
+    landing = refs[count + 3 : 2 * count + 3]
+    local_sem, send_sem, recv_sem = refs[2 * count + 3 :]
+    chips, core = places()
+    others = [(j, chips[j], other) for j in range(4) for other in (core, 1 - core)]
+    own = rank_at(chips[3], core)
+    targets = [(chip, other) for j, chip, other in others if not (j == 3 and other is core)]
+    greet([device_at(chip, other) for chip, other in targets])
+    copies, locals_ = [], []
+    for n in range(count):
+        for i, (chip, other) in enumerate(targets):
+            copies.append(
+                remote(
+                    parts[n].at[rank_at(chip, other)],
+                    landing[n].at[own],
+                    send_sem.at[n, i],
+                    recv_sem.at[n, i],
+                    device_at(chip, other),
+                )
+            )
+        local = pltpu.make_async_copy(parts[n].at[own], landing[n].at[own], local_sem.at[n])
+        local.start()
+        locals_.append(local)
+    for copy in locals_:
+        copy.wait()
+    for copy in copies:
+        copy.wait_recv()
+    span = landing[0].shape[2] // 3
+    groups = span // size
+    for which in range(3):
+        for n in range(count):
+            for k in range(8):
+                for g in range(groups):
+                    start = which * span + g * size
+                    place = ((n * groups + g) * 8 + k) * size
+                    outs[which][:, place : place + size] = landing[n][k, :, start : start + size].astype(f32)
+    for copy in copies:
+        copy.wait_send()
+
+
+def collect(parts, size, ident):
+    count, rows, wide = len(parts), parts[0].shape[1], parts[0].shape[2]
+    vmem = pl.BlockSpec(memory_space=pltpu.VMEM)
+    dma = pltpu.SemaphoreType.DMA
+    return pl.pallas_call(
+        functools.partial(collect_kernel, count, size),
+        out_shape=[jax.ShapeDtypeStruct((rows, count * 8 * wide // 3), f32)] * 3,
+        in_specs=[pl.BlockSpec(memory_space=pl.ANY)] * count,
+        out_specs=[vmem] * 3,
+        scratch_shapes=[pltpu.VMEM((8, rows, wide), bf16)] * count + [dma((count,)), dma((count, 7)), dma((count, 7))],
+        compiler_params=pltpu.CompilerParams(
+            collective_id=ident, has_side_effects=True, vmem_limit_bytes=48 * 2**20
+        ),
+    )(*parts)
 
 
 def gather_plane(v, ident):
@@ -315,13 +578,18 @@
     rank = (lax.axis_index("p") * lax.axis_size("c") + lax.axis_index("c")) * copies + x
     ce = width // (groups * ranks)
     fe = units // (groups * ranks)
-    chan, unit = ce * groups, fe * groups
+    chan, part_unit = ce * groups, fe * groups // HALVES
 
     def columns(w, size):
         w = w.reshape(w.shape[0], groups, members, copies, size)
         w = lax.dynamic_index_in_dim(w, x, axis=3, keepdims=False)
         return jnp.moveaxis(w, 2, 0).reshape(members, w.shape[0], groups * size)
 
+    def ffn_columns(w):
+        w = w.reshape(w.shape[0], HALVES, groups // HALVES, members, copies, fe)
+        w = lax.dynamic_index_in_dim(w, x, axis=4, keepdims=False)
+        return w.transpose(3, 1, 0, 2, 4).reshape(members, HALVES, w.shape[0], part_unit)
+
     def half_rows(w):
         half = w.shape[0] // copies
         return lax.dynamic_slice_in_dim(w, x * half, half, axis=0)
@@ -333,34 +601,23 @@
     def gather_rows(v):
         return lax.all_gather(v, "g", axis=0, tiled=True)
 
-    mix = jnp.concatenate([columns(w_in, ce), columns(w_forget, ce), columns(w_gate_out, ce)], axis=2)
-    mix = lax.all_to_all(mix, ("p", "c"), split_axis=0, concat_axis=0, tiled=True)
-    mix_w = gather_rows(mix.reshape(-1, 3 * chan))
     layer_count = bound_logits.shape[0]
     layer_probs = jax.nn.softmax(bound_logits, axis=0)
     layer_index = jnp.arange(layer_count, dtype=jnp.int32)
     layer_pick = ((layer_index >= 1) & (layer_index <= LAYER_AT)).astype(f32)[:, None]
     own_lower = jnp.sum(layer_probs * layer_pick, axis=0)[:, None]
     top, rest = split_hi_lo(own_lower)
-    out_ext = gather_rows(
-        jnp.concatenate(
-            [
-                half_rows(w_out),
-                top,
-                rest,
-                (own_lower - top.astype(f32) - rest.astype(f32)).astype(bf16),
-                jnp.zeros((ce, 125), bf16),
-            ],
-            axis=1,
-        )
-    )
-    out_w = out_ext[:, :width]
-    lower = jnp.sum(out_ext[:, width : width + 3].astype(f32), axis=1).reshape(1, chan)
-    ffn = jnp.concatenate([columns(ffn_gate, fe), columns(ffn_up, fe)], axis=2)
-    ffn = lax.all_to_all(ffn, ("p", "c"), split_axis=0, concat_axis=0, tiled=True)
-    ffn_w = gather_rows(ffn.reshape(-1, 2 * unit))
+    out_own = jnp.concatenate(
+        [
+            half_rows(w_out),
+            top,
+            rest,
+            (own_lower - top.astype(f32) - rest.astype(f32)).astype(bf16),
+            jnp.zeros((ce, 125), bf16),
+        ],
+        axis=1,
+    )
     down_w = gather_rows(half_rows(ffn_down))
-
     gain = own_columns(out_gain, ce)
 
     places = jnp.arange(doc_ids.shape[0], dtype=jnp.int32)
@@ -379,8 +636,22 @@
     seq_total = doc_ids.shape[0] // SEQ_LEN
     grad_z = cotangent.astype(f32) * (seq_total / (domain_count * per_token))[:, None]
 
-    both = gather_plane(jnp.concatenate([act_one_own, grad_z.astype(bf16)], axis=1), 0)
-    act_one, grad_m = both[:, :width], both[:, width:]
+    mix_w, ffn, out_ext, act_one, grad_m = spread(
+        groups,
+        jnp.concatenate([columns(w_in, ce), columns(w_forget, ce), columns(w_gate_out, ce)], axis=2),
+        jnp.concatenate([ffn_columns(ffn_gate), ffn_columns(ffn_up)], axis=3),
+        out_own,
+        act_one_own,
+        grad_z.astype(bf16),
+        0,
+    )
+    mix_w = mix_w.reshape(width, 3 * chan)
+    ffn, down_w = lax.optimization_barrier((ffn, down_w))
+    ffn_w = [gather_rows(ffn[:, h].reshape(-1, 2 * part_unit)) for h in range(HALVES)]
+    act_one, grad_m = act_one.reshape(plane_rows, width), grad_m.reshape(plane_rows, width)
+    out_ext = out_ext.reshape(chan, -1)
+    out_w = out_ext[:, :width]
+    lower = jnp.sum(out_ext[:, width : width + 3].astype(f32), axis=1).reshape(1, chan)
 
     proj = dot(act_one, mix_w)
     states, mixed_raw, squares = kernel_call(
@@ -407,24 +678,29 @@
     normed_two = residual * scale_two
     act_two = gather_plane((normed_two * ffn_gain).astype(bf16), 2)
 
-    pre = dot(act_two, ffn_w)
-    gate_ffn, up_ffn = pre[:, :unit], pre[:, unit:]
-    sig = jax.nn.sigmoid(gate_ffn)
-    gate_silu = gate_ffn * sig
-    hidden = (gate_silu * up_ffn).astype(bf16)
-    down_part = dot(hidden, down_w).astype(bf16)
-    grad_hidden = dot_nt(grad_m, down_w)
-    grad_gate = (grad_hidden * up_ffn * (sig * (1.0 + gate_ffn * (1.0 - sig)))).astype(bf16)
-    grad_up = (grad_hidden * gate_silu).astype(bf16)
-    grad_pre = jnp.concatenate([grad_gate, grad_up], axis=1)
-    back_part = dot_nt(grad_pre, ffn_w).astype(bf16)
-
     def scatter_rows(v):
-        return lax.psum_scatter(v.astype(bf16), "g", scatter_dimension=0, tiled=True)
-
-    ffn_grads = jnp.concatenate([dot_tn(act_two, grad_pre), dot_tn(grad_m, hidden)], axis=1).astype(bf16)
-    ffn_grads, back_part = lax.optimization_barrier((ffn_grads, back_part))
-    ffn_sum = scatter_rows(ffn_grads)
+        return lax.psum_scatter(v, "g", scatter_dimension=0, tiled=True)
+
+    down_part, back_part, ffn_sums = 0.0, 0.0, []
+    for h in range(HALVES):
+        down = down_w[h * part_unit : (h + 1) * part_unit]
+        grad_hidden = dot_nt(grad_m, down)
+        pre = dot(act_two, ffn_w[h])
+        gate_ffn, up_ffn = pre[:, :part_unit], pre[:, part_unit:]
+        sig = jax.nn.sigmoid(gate_ffn)
+        gate_silu = gate_ffn * sig
+        hidden = (gate_silu * up_ffn).astype(bf16)
+        grad_gate = (grad_hidden * up_ffn * (sig * (1.0 + gate_ffn * (1.0 - sig)))).astype(bf16)
+        grad_up = (grad_hidden * gate_silu).astype(bf16)
+        grad_pre = jnp.concatenate([grad_gate, grad_up], axis=1)
+        grads = jnp.concatenate(
+            [dot_tn(act_two, grad_pre).astype(bf16), dot_tn(grad_m, hidden).astype(bf16)], axis=1
+        )
+        grads, grad_pre, hidden = lax.optimization_barrier((grads, grad_pre, hidden))
+        ffn_sums.append(scatter_rows(grads))
+        down_part = down_part + dot(hidden, down)
+        back_part = back_part + dot_nt(grad_pre, ffn_w[h])
+    down_part, back_part = down_part.astype(bf16), back_part.astype(bf16)
 
     back_term = scatter_plane(back_part, 3)
     scaled_two = back_term * ffn_gain
@@ -473,7 +749,7 @@
     out_grads = out_grads[:, : folds * 3 * chan].reshape(groups, ce, folds, 3 * chan)
     out_grads = jnp.moveaxis(out_grads, 2, 1).reshape(groups, folds * ce, 3 * chan)
     late_grads = jnp.concatenate([mix_grads, out_grads], axis=1).reshape(-1, 3 * chan)
-    late_grads, ffn_sum = lax.optimization_barrier((late_grads, ffn_sum))
+    late_grads, ffn_sums = lax.optimization_barrier((late_grads, ffn_sums))
     late_sum = scatter_rows(late_grads)
     mix_sum = late_sum[: width // groups]
     out_sum = jnp.moveaxis(late_sum[width // groups :].reshape(folds, ce, 3 * chan), 1, 0)
@@ -489,25 +765,9 @@
         scaled_one - normed_one * jnp.mean(scaled_one * normed_one, axis=-1, keepdims=True)
     )
 
-    def spread_rows(v):
-        v = lax.all_to_all(
-            v.reshape(ranks, -1, v.shape[1]), PLANE, split_axis=0, concat_axis=0, tiled=True
-        )
-        return v
-
-    def whole_columns(v, size):
-        v = v.reshape(ranks, v.shape[1], groups, size)
-        return v.transpose(1, 2, 0, 3).reshape(v.shape[1], -1).astype(f32)
-
-    ffn_rows = spread_rows(ffn_sum)
-    summed_fgate = whole_columns(ffn_rows[:, :, :unit], fe)
-    summed_fup = whole_columns(ffn_rows[:, :, unit : 2 * unit], fe)
-    summed_fdown = whole_columns(ffn_rows[:, :, 2 * unit :], fe).T
-    mix_rows = spread_rows(mix_sum)
-    summed_win = whole_columns(mix_rows[:, :, :chan], ce)
-    summed_wforget = whole_columns(mix_rows[:, :, chan : 2 * chan], ce)
-    summed_wgate = whole_columns(mix_rows[:, :, 2 * chan :], ce)
-
+    summed_fgate, summed_fup, fdown = collect([v.reshape(ranks, -1, 3 * part_unit) for v in ffn_sums], fe, 7)
+    summed_fdown = fdown.T
+    summed_win, summed_wforget, summed_wgate = collect([mix_sum.reshape(ranks, -1, 3 * chan)], ce, 8)
     first = (g * ranks + rank) * ce
 
     def own_gain(gain, pairs):

time: 601 us -> 553 us (0.920)
  Pallas kernels: 265 us -> 349 us
  waiting for transfers between devices: 73.4 us -> 15.6 us
  blocking collectives: 36.9 us -> 0 us
  local copies, waits for them, and re-layouts: 78.2 us -> 64.1 us
  matrix products: 83 us -> 71.5 us
  starting transfers between devices: 8.35 us -> 0.88 us
    pallas_call x0 -> x3, Pallas kernels: none -> 152 us  [the longest x1 108 us: spread(): pl.pallas_call(functools.partial(spread_kernel, groups), out_shape=[jax.S...]
    pallas_call x3 -> x2, Pallas kernels: 114 us -> 60.1 us  [gather_plane(): pl.pallas_call(gather_kernel, out_shape=jax.ShapeDtypeStruct((8,) + v.sha...]
    all_gather x4 -> x3, waiting for transfers between devices: 50.7 us -> 12 us  [gather_rows(): return lax.all_gather(v, 'g', axis=0, tiled=True)]
    all_to_all x2 -> x0, blocking collectives: 36.9 us -> none  [the longest x1 21.1 us: body(): lax.all_to_all(ffn, ('p', 'c'), split_axis=0, concat_axis=0, tiled=True)]
    convert_element_type x16 -> x0, local copies, waits for them, and re-layouts: 21.3 us -> none  [the longest x15 21.1 us: whole_columns(): return v.transpose(1, 2, 0, 3).reshape(v.shape[1], -1).astype(f32)]
    pallas_call x4, Pallas kernels: 132 us -> 117 us  [scatter_plane(): pl.pallas_call(scatter_kernel, out_shape=jax.ShapeDtypeStruct((rows, wide...]
    unnamed x98 -> x136, local copies, waits for them, and re-layouts: 14.4 us -> 25.2 us
    reduce_scatter x2 -> x3, waiting for transfers between devices: 13.9 us -> 3.49 us  [scatter_rows(): return lax.psum_scatter(v, 'g', scatter_dimension=0, tiled=True)]
  transfers between devices with their start and end apart: 8 -> 6, of which waited for: 4 -> 3; matrix products, arithmetic and copies ran while one was open for 22% -> 25% of each run, Pallas kernels for 45% -> 62%
where the time goes in v3:
time: 553 us; the launch traced here: 545 us
  Pallas kernels  349 us (63%)
  matrix products  71.5 us (13%)
  local copies, waits for them, and re-layouts  64.1 us (12%)
  other arithmetic  29 us (5%)
  between operations  15.7 us (3%)
  waiting for transfers between devices  15.6 us (3%)
    pallas_call x4, Pallas kernels, scatter_plane(): pl.pallas_call(scatter_kernel, out_shape=jax.ShapeDtypeStruct((rows, wide...  117 us
    pallas_call x1, Pallas kernels, spread(): pl.pallas_call(functools.partial(spread_kernel, groups), out_shape=[jax.S...  108 us
    pallas_call x2, Pallas kernels, gather_plane(): pl.pallas_call(gather_kernel, out_shape=jax.ShapeDtypeStruct((8,) + v.sha...  60.1 us
    pallas_call x2, Pallas kernels, collect(): pl.pallas_call(functools.partial(collect_kernel, count, size), out_shape=...  44.3 us
    dot_general x6, matrix products, dot(): return jnp.dot(a, b, preferred_element_type=f32)  26.6 us
    unnamed x136, local copies, waits for them, and re-layouts  25.2 us
    dot_general x6, matrix products, dot_nt(): lax.dot_general(a, b, (((1,), (1,)), ((), ())), preferred_element_type=f32)  23.5 us
    dot_general x6, matrix products, dot_tn(): lax.dot_general(a, b, (((0,), (0,)), ((), ())), preferred_element_type=f32)  21.4 us
  transfers between devices with their start and end apart: 6, of which 3 were waited for; matrix products, arithmetic and copies ran while one was open for 25% of the time, Pallas kernels for 62%

profile of v3, /device:TPU:0, one launch (start us, length us, event | category | flops | bytes accessed | tf_op | source)
XLA Modules:
  0.0 545.3 jit_solution(2836211217642018019)
XLA Ops:
  34.1 107.8 %shard_map.255 = (bf16[4,4,128,768]{3,2,1,0:T(8,128)(2,1)}, bf16[4,2,128,704]{3,2,1,0:T(8,128)(2,1)S(1)}, bf16[4,64,2176]{2,1,0:T(8,128)(2,1)S(1)}, bf16[8,128,2048]{2,1,0:T(8,128)(2,1)}, bf16[8,128,2048]{2,1,0:T(8,128)(2,1)}) custom-call(bf16[4,128,768]{2,1,0:T(8,128)(2,1)S(1)} %pad_maximum_fusion.6.mix_ref, ...), custom_call_target="tpu_custom_call" | custom-call | tf_op jit(solution)/shard_map/pallas_call | solution.py:366
  146.2 6.1 %fusion.46.proj_ref = f32[1024,768]{1,0:T(8,128)S(1)} fusion(bf16[1024,2048]{1,0:T(8,128)(2,1)} %bitcast.144, bf16[2048,768]{1,0:T(8,128)(2,1)} %bitcast.150), kind=kOutput, calls=%fused_computation.127 | convolution fusion | flops 3221225472 | bytes 10485760 | tf_op jit(solution)/shard_map/dot_general | solution.py:541
  152.3 10.8 %shard_map.256 = (f32[1024,256]{1,0:T(8,128)S(1)}, bf16[1024,256]{1,0:T(8,128)(2,1)S(1)}, f32[1024,1]{1,0:T(8,128)S(1)}) custom-call(f32[1024,768]{1,0:T(8,128)S(1)} %fusion.46.proj_ref, f32[1024,1]{1,0:T(8,128)S(1)} %copy.165.keep_ref, f32[1,256]{1,0:T(1,128)S(1)} %bitcast.119, f32[1,256]{1,0:T(1,128)S(1)} %reshape.302.gain_ref), custom_call_target="tpu_custom_call" | custom-call | tf_op jit(solution)/shard_map/pallas_call | solution.py:116
  166.5 7.8 %concatenate.43 = bf16[1024,2176]{1,0:T(8,128)(2,1)} concatenate(bf16[1024,2048]{1,0:T(8,128)(2,1)} %convolution_convert_fusion, bf16[1024,1]{1,0:T(8,128)(2,1)S(1)} %get-tuple-element.79, bf16[1024,1]{1,0:T(8,128)(2,1)S(1)} %get-tuple-element.78, bf16[1024,126]{1,0:T(8,128)(2,1)S(1)} %broadcast_in_dim.23), dimensions={1} | concatenate | bytes 8912896 | tf_op jit(solution)/shard_map/concatenate | solution.py:670
  176.6 30.3 %shard_map.257 = f32[128,2176]{1,0:T(8,128)S(1)} custom-call(bf16[8,128,2176]{2,1,0:T(8,128)(2,1)S(1)} %bitcast.102), custom_call_target="tpu_custom_call" | custom-call | tf_op jit(solution)/shard_map/pallas_call | solution.py:520
  209.1 29.4 %shard_map.258 = bf16[8,128,2048]{2,1,0:T(8,128)(2,1)S(1)} custom-call(bf16[128,2048]{1,0:T(8,128)(2,1)S(1)} %multiply_convert_fusion.6.own_ref), custom_call_target="tpu_custom_call" | custom-call | tf_op jit(solution)/shard_map/pallas_call | solution.py:501
  240.5 6.1 %fusion.48 = f32[1024,704]{0,1:T(8,128)S(1)} fusion(bf16[1024,2048]{1,0:T(8,128)(2,1)} %bitcast.111, bf16[2048,704]{1,0:T(8,128)(2,1)} %all-gather.8.cloned.1.call-done), kind=kOutput, calls=%fused_computation.129 | convolution fusion | flops 2952790016 | bytes 9961472 | tf_op jit(solution)/shard_map/dot_general | solution.py:541
  252.3 3.9 convolution_convert_fusion.3
  258.9 12.0 %all-gather.6.cloned.1.call-done = bf16[2048,704]{1,0:T(8,128)(2,1)} async-done(((bf16[512,704]{1,0:T(8,128)(2,1)}), bf16[2048,704]{1,0:T(8,128)(2,1)}) %all-gather.6.cloned.1.call-update) | async-done | bytes 2883600 | tf_op jit(solution)/shard_map/all_gather | solution.py:602
  270.9 6.1 %fusion.47 = f32[1024,704]{0,1:T(8,128)S(1)} fusion(bf16[1024,2048]{1,0:T(8,128)(2,1)} %bitcast.112, bf16[2048,704]{1,0:T(8,128)(2,1)} %all-gather.6.cloned.1.call-done), kind=kOutput, calls=%fused_computation.128 | convolution fusion | flops 2952790016 | bytes 9961472 | tf_op jit(solution)/shard_map/dot_general | solution.py:541
  282.6 3.9 convolution_convert_fusion.4
  289.1 6.0 %fusion.49 = f32[1024,2048]{1,0:T(8,128)S(1)} fusion(bf16[1024,704]{0,1:T(8,128)(2,1)} %pad_maximum_fusion.4, bf16[2048,704]{1,0:T(8,128)(2,1)} %all-gather.6.cloned.1.call-done), kind=kOutput, calls=%fused_computation.130 | convolution fusion | flops 2952790016 | bytes 12713984 | tf_op jit(solution)/shard_map/dot_general | solution.py:545
  295.1 4.0 add_convert_fusion
  299.1 28.7 %shard_map.260 = f32[128,2048]{1,0:T(8,128)S(1)} custom-call(bf16[8,128,2048]{2,1,0:T(8,128)(2,1)S(1)} %bitcast.109), custom_call_target="tpu_custom_call" | custom-call | tf_op jit(solution)/shard_map/pallas_call | solution.py:520
  332.8 28.8 %shard_map.259 = f32[128,2048]{1,0:T(8,128)S(1)} custom-call(bf16[8,128,2048]{2,1,0:T(8,128)(2,1)S(1)} %bitcast.103), custom_call_target="tpu_custom_call" | custom-call | tf_op jit(solution)/shard_map/pallas_call | solution.py:520
  364.3 30.7 %shard_map.261 = bf16[8,128,2176]{2,1,0:T(8,128)(2,1)S(1)} custom-call(bf16[128,2176]{1,0:T(8,128)(2,1)S(1)} %concatenate.48.own_ref), custom_call_target="tpu_custom_call" | custom-call | tf_op jit(solution)/shard_map/pallas_call | solution.py:501
  401.1 9.0 %shard_map.262 = (bf16[1024,768]{1,0:T(8,128)(2,1)S(1)}, bf16[1024,256]{1,0:T(8,128)(2,1)S(1)}, f32[1,256]{1,0:T(1,128)S(1)}) custom-call(f32[1024,768]{1,0:T(8,128)} %copy-done.3, f32[1024,256]{1,0:T(8,128)S(1)} %copy-done.16, f32[1024,256]{1,0:T(8,128)S(1)} %fusion.2.do_ref, f32[1024,2]{1,0:T(8,128)S(1)} %copy.170.info_ref, f32[1024,1]{1,0:T(8,128)S(1)} %copy.165.keep_ref, ...), custom_call_target="tpu_custom_call" | custom-call | tf_op jit(solution)/shard_map/pallas_call | solution.py:116
  410.4 4.4 fusion.4
  418.4 3.9 reshape.312
  423.9 5.7 %convolution_convert_fusion.2 = bf16[2048,768]{1,0:T(8,128)(2,1)S(1)} fusion(bf16[1024,2048]{1,0:T(8,128)(2,1)} %bitcast.145, bf16[1024,768]{1,0:T(8,128)(2,1)S(1)} %get-tuple-element.55), kind=kOutput, calls=%fused_computation.11 | convolution fusion | flops 3222798336 | bytes 8912896 | tf_op jit(solution)/shard_map/dot_general | solution.py:549
  432.2 5.6 %convolution_convert_fusion.1 = bf16[1024,2048]{1,0:T(8,128)(2,1)S(1)} fusion(bf16[1024,768]{1,0:T(8,128)(2,1)S(1)} %get-tuple-element.55, bf16[2048,768]{1,0:T(8,128)(2,1)} %bitcast.151), kind=kOutput, calls=%fused_computation.6 | convolution fusion | flops 3223322624 | bytes 8912896 | tf_op jit(solution)/shard_map/dot_general | solution.py:545
  437.9 28.8 %shard_map.263 = f32[128,2048]{1,0:T(8,128)S(1)} custom-call(bf16[8,128,2048]{2,1,0:T(8,128)(2,1)S(1)} %bitcast.110), custom_call_target="tpu_custom_call" | custom-call | tf_op jit(solution)/shard_map/pallas_call | solution.py:520
  474.7 31.4 %shard_map.265 = (f32[64,5632]{1,0:T(8,128)S(1)}, f32[64,5632]{1,0:T(8,128)S(1)}, f32[64,5632]{1,0:T(8,128)}) custom-call(bf16[8,64,1056]{2,1,0:T(8,128)(2,1)S(1)} %bitcast.107, bf16[8,64,1056]{2,1,0:T(8,128)(2,1)S(1)} %bitcast.108), custom_call_target="tpu_custom_call" | custom-call | tf_op jit(solution)/shard_map/pallas_call | solution.py:487
  516.3 12.9 %shard_map.264 = (f32[64,2048]{1,0:T(8,128)S(1)}, f32[64,2048]{1,0:T(8,128)S(1)}, f32[64,2048]{1,0:T(8,128)S(1)}) custom-call(bf16[8,64,768]{2,1,0:T(8,128)(2,1)S(1)} %bitcast.115), custom_call_target="tpu_custom_call" | custom-call | tf_op jit(solution)/shard_map/pallas_call | solution.py:487
  (258 shorter events, 105.4 us)
Async XLA Ops:
  7.2 9.1 %copy-start.33 = (bf16[128,2048]{1,0:T(8,128)(2,1)S(1)}, bf16[128,2048]{1,0:T(8,128)(2,1)}, u32[]{:S(2)}) copy-start(bf16[128,2048]{1,0:T(8,128)(2,1)} %param.22) | copy-start | bytes 1572868
  7.2 134.8 %all-gather.4.cloned.1.call-start = ((), (), s32[]{:S(2)}) async-start(), calls=%async_computation.3 | async-start | bytes 3604480 | tf_op jit(solution)/shard_map/all_gather | solution.py:602
  8.5 8.0 %copy-start.35 = (bf16[128,2048]{1,0:T(8,128)(2,1)S(1)}, bf16[128,2048]{1,0:T(8,128)(2,1)}, u32[]{:S(2)}) copy-start(bf16[128,2048]{1,0:T(8,128)(2,1)} %param.23) | copy-start | bytes 1572868
  9.5 231.0 %all-gather.8.cloned.1.call-start = ((), (), s32[]{:S(2)}) async-start(), calls=%async_computation.5 | async-start | bytes 3932160 | tf_op jit(solution)/shard_map/all_gather | solution.py:602
  143.5 127.4 %all-gather.6.cloned.1.call-start = ((), (), s32[]{:S(2)}) async-start(), calls=%async_computation.4 | async-start | bytes 3932160 | tf_op jit(solution)/shard_map/all_gather | solution.py:602
  152.3 14.2 %copy-start.3 = (f32[1024,768]{1,0:T(8,128)}, f32[1024,768]{1,0:T(8,128)S(1)}, u32[]{:S(2)}) copy-start(f32[1024,768]{1,0:T(8,128)S(1)} %fusion.46.proj_ref) | copy-start | bytes 9437188
  152.3 10.9 %copy-start.13 = (bf16[4,64,2176]{2,1,0:T(8,128)(2,1)S(1)}, bf16[4,64,2176]{2,1,0:T(8,128)(2,1)}, u32[]{:S(2)}) copy-start(bf16[4,64,2176]{2,1,0:T(8,128)(2,1)} %copy-done.12) | copy-start | bytes 3342340
  207.2 224.8 %reduce-scatter.6.cloned.1.call-start = ((), (), s32[]{:S(2)}) async-start(), calls=%async_computation.7 | async-start | bytes 5406720 | tf_op jit(solution)/shard_map/reduce_scatter | solution.py:682
  258.7 173.6 %reduce-scatter.4.cloned.1.call-start = ((), (), s32[]{:S(2)}) async-start(), calls=%async_computation.6 | async-start | bytes 5406720 | tf_op jit(solution)/shard_map/reduce_scatter | solution.py:682
  289.0 224.8 %reduce-scatter.8.cloned.1.call-start = ((), (), s32[]{:S(2)}) async-start(), calls=%async_computation.8 | async-start | bytes 5406720 | tf_op jit(solution)/shard_map/reduce_scatter | solution.py:682
  299.1 28.8 %copy-start.27 = (bf16[704,2048]{1,0:T(8,128)(2,1)S(1)}, bf16[704,2048]{1,0:T(8,128)(2,1)}, u32[]{:S(2)}) copy-start(bf16[704,2048]{1,0:T(8,128)(2,1)} %all-gather.4.cloned.1.call-done) | copy-start | bytes 8650756
  332.8 28.8 %copy-start.18 = (f32[128,2048]{1,0:T(8,128)S(1)}, f32[128,2048]{1,0:T(8,128)}, u32[]{:S(2)}) copy-start(f32[128,2048]{1,0:T(8,128)} %copy-done.17) | copy-start | bytes 3145732
  332.8 29.1 %copy-start.29 = (bf16[128,2048]{1,0:T(8,128)(2,1)S(1)}, bf16[128,2048]{1,0:T(8,128)(2,1)}, u32[]{:S(2)}) copy-start(bf16[128,2048]{1,0:T(8,128)(2,1)} %param.17) | copy-start | bytes 1572868
  364.3 33.2 %copy-start.14 = (bf16[4,64,2176]{2,1,0:T(8,128)(2,1)S(1)}, bf16[4,64,2176]{2,1,0:T(8,128)(2,1)}, u32[]{:S(2)}) copy-start(bf16[4,64,2176]{2,1,0:T(8,128)(2,1)} %copy-done.12) | copy-start | bytes 3342340
  437.8 28.8 %copy-start.20 = (bf16[128,2048]{1,0:T(8,128)(2,1)S(1)}, bf16[128,2048]{1,0:T(8,128)(2,1)}, u32[]{:S(2)}) copy-start(bf16[128,2048]{1,0:T(8,128)(2,1)} %param.16) | copy-start | bytes 1572868
  437.9 28.8 %copy-start.56 = (f32[128]{0:T(128)S(1)}, f32[128]{0:T(128)}, u32[]{:S(2)}) copy-start(f32[128]{0:T(128)} %copy-done.55) | copy-start | bytes 1540
  437.9 29.1 %copy-start.21 = (f32[128,2048]{1,0:T(8,128)S(1)}, f32[128,2048]{1,0:T(8,128)}, u32[]{:S(2)}) copy-start(f32[128,2048]{1,0:T(8,128)} %get-tuple-element.73) | copy-start | bytes 3145732
  514.9 14.3 %copy-start.32 = (bf16[128,2048]{1,0:T(8,128)(2,1)S(1)}, bf16[128,2048]{1,0:T(8,128)(2,1)}, u32[]{:S(2)}) copy-start(bf16[128,2048]{1,0:T(8,128)(2,1)} %param.21) | copy-start | bytes 1572868
  515.0 14.4 %copy-start.34 = (bf16[128,2048]{1,0:T(8,128)(2,1)S(1)}, bf16[128,2048]{1,0:T(8,128)(2,1)}, u32[]{:S(2)}) copy-start(bf16[128,2048]{1,0:T(8,128)(2,1)} %param.22) | copy-start | bytes 1572868
  515.0 14.5 %copy-start.36 = (bf16[128,2048]{1,0:T(8,128)(2,1)S(1)}, bf16[128,2048]{1,0:T(8,128)(2,1)}, u32[]{:S(2)}) copy-start(bf16[128,2048]{1,0:T(8,128)(2,1)} %param.23) | copy-start | bytes 1572868
  515.2 15.7 %copy-start.41 = (f32[24,64]{1,0:T(8,128)S(1)}, f32[24,64]{1,0:T(8,128)}, u32[]{:S(2)}) copy-start(f32[24,64]{1,0:T(8,128)} %param.31) | copy-start | bytes 18436
  515.2 15.7 %copy-start.49 = (f32[64]{0:T(128)S(1)}, f32[64]{0:T(128)}, u32[]{:S(2)}) copy-start(f32[64]{0:T(128)} %copy-done.48) | copy-start | bytes 772
  515.2 15.7 %copy-start.52 = (f32[64]{0:T(128)S(1)}, f32[64]{0:T(128)}, u32[]{:S(2)}) copy-start(f32[64]{0:T(128)} %copy-done.51) | copy-start | bytes 772
  515.2 15.7 %copy-start.54 = (f32[24]{0:T(128)S(1)}, f32[24]{0:T(128)}, u32[]{:S(2)}) copy-start(f32[24]{0:T(128)} %copy-done.53) | copy-start | bytes 292
  (44 other events, 143.1 us)
Sparse Core Ops, SparseCore 0:
  9.6 80.6 all-gather.3
  143.6 63.6 all-gather.7
  208.8 62.0 all-gather.5
  273.1 77.5 reduce-scatter.5
  352.8 79.3 reduce-scatter.3
  434.4 79.3 reduce-scatter.7

commit v4 on v3

--- a/solution.py
+++ b/solution.py
@@ -12,7 +12,7 @@
 SEQ_LEN = 1024
 EPS = 1e-06
 ROWS = 16
-HALVES = 2
+QUARTERS = 4
 PLANE = ("p", "c", "x")
 ALL = ("g", "p", "c", "x")
 f32 = jnp.float32
@@ -57,6 +57,134 @@
         return h[ROWS - 1 : ROWS, :]
 
     lax.fori_loop(0, proj_ref.shape[0] // ROWS, step, jnp.zeros((1, chan), f32))
+
+
+def mixer_kernel(
+    chan,
+    act_ref,
+    mix_ref,
+    out_w_ref,
+    keep_ref,
+    lower_ref,
+    gain_ref,
+    token_ref,
+    ffn_gain_ref,
+    proj_ref,
+    h_ref,
+    residual_ref,
+    scale_ref,
+    act_two_ref,
+    raw,
+    squares,
+    part,
+    theirs,
+    outgoing,
+    landing,
+    own_two,
+    swap_send,
+    swap_recv,
+    send_sem,
+    recv_sem,
+    local_sem,
+    act_send,
+    act_recv,
+):
+    chips, core = places()
+    sibling = device_at(chips[3], 1 - core)
+    greet([device_at(chip, core) for chip in chips[:3]] + [sibling])
+    rows, width = token_ref.shape
+    block = 2 * rows
+
+    def project(i, _):
+        at = pl.ds(pl.multiple_of(i * block, block), block)
+        proj_ref[at, :] = dot(act_ref[at, :], mix_ref[...])
+        return 0
+
+    lax.fori_loop(0, act_ref.shape[0] // block, project, 0)
+    forward_scan(chan, proj_ref, keep_ref, lower_ref, gain_ref, h_ref, raw, squares)
+
+    lane = lax.broadcasted_iota(jnp.int32, (rows, part.shape[1] - width), 1)
+
+    def mixed(rank):
+        at = pl.ds(pl.multiple_of(rank * rows, rows), rows)
+        part[at, :width] = dot(raw[at, :], out_w_ref[:, :width]).astype(bf16)
+        top, rest = split_hi_lo(squares[at, :])
+        side = jnp.where(lane == 0, top.astype(f32), jnp.where(lane == 1, rest.astype(f32), 0.0))
+        part[at, width:] = side.astype(bf16)
+        return part.at[at]
+
+    swaps = []
+    for j, chip in enumerate(chips):
+        swaps.append(
+            remote(
+                mixed(rank_at(chip, 1 - core)), theirs.at[j], swap_send.at[j], swap_recv.at[j], sibling
+            )
+        )
+    scatter = Scatter([], theirs, outgoing, landing, send_sem, recv_sem)
+    for j, chip in enumerate(chips):
+        scatter.mine.append(mixed(rank_at(chip, core)))
+        swaps[j].wait_recv()
+        if j < 3:
+            scatter.first(j)
+    scatter.second()
+
+    def finish(at, total):
+        scale = lax.rsqrt((total[:, width : width + 1] + total[:, width + 1 : width + 2]) / width + EPS)
+        scale_ref[at, :] = scale
+        residual = token_ref[at, :].astype(f32) + total[:, :width] * scale
+        residual_ref[at, :] = residual
+        norm = lax.rsqrt(jnp.mean(residual * residual, axis=-1, keepdims=True) + EPS)
+        own_two[at, :] = (residual * norm * ffn_gain_ref[...]).astype(bf16)
+
+    scatter.totals(finish)
+    plane = Plane(own_two, act_two_ref, local_sem.at[0], act_send, act_recv)
+    plane.start(1)
+    plane.start(2)
+    plane.start_own()
+    for copy in swaps:
+        copy.wait_send()
+    scatter.finish()
+    for i in (1, 2, 0):
+        plane.hand_on(i)
+    plane.finish()
+
+
+def mixer(chan, act, mix_w, out_ext, keep, lower, gain, tokens, ffn_gain, ident):
+    total, (rows, width) = act.shape[0], tokens.shape
+    vmem, hbm = pl.BlockSpec(memory_space=pltpu.VMEM), pl.BlockSpec(memory_space=pl.ANY)
+    dma = pltpu.SemaphoreType.DMA
+    wide = width + 128
+    return pl.pallas_call(
+        functools.partial(mixer_kernel, chan),
+        out_shape=[
+            jax.ShapeDtypeStruct((total, 3 * chan), f32),
+            jax.ShapeDtypeStruct((total, chan), f32),
+            jax.ShapeDtypeStruct((rows, width), f32),
+            jax.ShapeDtypeStruct((rows, 1), f32),
+            jax.ShapeDtypeStruct((8, rows, width), bf16),
+        ],
+        in_specs=[vmem] * 8,
+        out_specs=[vmem] * 4 + [hbm],
+        scratch_shapes=[
+            pltpu.VMEM((total, chan), bf16),
+            pltpu.VMEM((total, 1), f32),
+            pltpu.VMEM((total, wide), bf16),
+            pltpu.VMEM((4, rows, wide), bf16),
+            pltpu.VMEM((6, rows // 2, wide), bf16),
+            pltpu.VMEM((6, rows // 2, wide), bf16),
+            pltpu.VMEM((rows, width), bf16),
+            dma((4,)),
+            dma((4,)),
+            dma((6,)),
+            dma((6,)),
+            dma((1,)),
+            dma((8,)),
+            dma((8,)),
+        ],
+        compiler_params=pltpu.CompilerParams(
+            collective_id=ident, has_side_effects=True, vmem_limit_bytes=56 * 2**20
+        ),
+    )(act, mix_w, out_ext, keep, lower, gain, tokens, ffn_gain)
 
 
 def backward_scan(
@@ -155,34 +283,15 @@
     return copy
 
 
-def gather_kernel(own_ref, out_ref, local_sem, send_sem, recv_sem):
-    chips, core = places()
-    here = chips[3]
-    sibling = device_at(here, 1 - core)
-    greet([device_at(chip, core) for chip in chips[:3]] + [sibling])
-    slot = out_ref.at[rank_at(here, core)]
-    local = pltpu.make_async_copy(own_ref, slot, local_sem)
-    local.start()
-    direct = [
-        remote(own_ref, slot, send_sem.at[i], recv_sem.at[i], device_at(chips[i], core)) for i in range(3)
-    ]
-    passed = [remote(own_ref, slot, send_sem.at[3], recv_sem.at[3], sibling)]
-    for i in (1, 2, 0):
-        direct[i].wait_recv()
-        got = out_ref.at[rank_at(chips[i], core)]
-        passed.append(remote(got, got, send_sem.at[4 + i], recv_sem.at[4 + i], sibling))
-    for copy in direct:
-        copy.wait_send()
-    for copy in passed:
-        copy.wait()
-    local.wait()
-
-
 class Line:
-    def __init__(self, groups, own_ref, out_ref, send_sem, recv_sem):
+    def __init__(self, groups, own_ref, out_ref, send_sem, recv_sem, local_sem=None):
         self.groups, self.own, self.out = groups, own_ref, out_ref
         self.send_sem, self.recv_sem = send_sem, recv_sem
         self.g, self.p, self.c, self.x = (lax.axis_index(a) for a in ALL)
+        self.kept = None
+        if local_sem is not None:
+            self.kept = pltpu.make_async_copy(own_ref, out_ref.at[self.g], local_sem)
+            self.kept.start()
 
     def at_step(self, way, k):
         block = self.g - (k - 1) if way == 0 else self.g + (k - 1)
@@ -208,26 +317,30 @@
             def _(way=way):
                 self.at_step(way, k).start()
 
+    def arrived(self, way, k):
+        got = self.out.at[self.g - k if way == 0 else self.g + k]
+        pltpu.make_async_remote_copy(
+            src_ref=got,
+            dst_ref=got,
+            send_sem=self.send_sem.at[way, k - 1],
+            recv_sem=self.recv_sem.at[way, k - 1],
+            device_id=(self.g, self.p, self.c, self.x),
+            device_id_type=MESH,
+        ).wait_recv()
+
     def step(self, k):
         for way in (0, 1):
 
             @pl.when(self.behind(way, k))
             def _(way=way):
-                block = self.g - k if way == 0 else self.g + k
-                got = self.out.at[block]
-                pltpu.make_async_remote_copy(
-                    src_ref=got,
-                    dst_ref=got,
-                    send_sem=self.send_sem.at[way, k - 1],
-                    recv_sem=self.recv_sem.at[way, k - 1],
-                    device_id=(self.g, self.p, self.c, self.x),
-                    device_id_type=MESH,
-                ).wait_recv()
+                self.arrived(way, k)
 
         if k + 1 < self.groups:
             self.send(k + 1)
 
     def finish(self):
+        if self.kept is not None:
+            self.kept.wait()
         for k in range(1, self.groups):
             for way in (0, 1):
 
@@ -247,33 +360,119 @@
         self.own, self.out = own_ref, out_ref
         self.send_sem, self.recv_sem = send_sem, recv_sem
         self.chips, self.core = places()
+        self.half = own_ref.shape[0] // 2
         self.slot = out_ref.at[rank_at(self.chips[3], self.core)]
         self.sibling = device_at(self.chips[3], 1 - self.core)
         self.local = pltpu.make_async_copy(own_ref, self.slot, local_sem)
-        self.direct, self.passed = {}, []
+        self.sent, self.passed = {}, []
+
+    def send(self, n, src, dst, device):
+        return remote(src, dst, self.send_sem.at[n], self.recv_sem.at[n], device)
 
     def start_own(self):
         self.local.start()
-        self.passed.append(
-            remote(self.own, self.slot, self.send_sem.at[3], self.recv_sem.at[3], self.sibling)
-        )
+        self.passed.append(self.send(3, self.own, self.slot, self.sibling))
 
     def start(self, i):
-        self.direct[i] = remote(
-            self.own, self.slot, self.send_sem.at[i], self.recv_sem.at[i], device_at(self.chips[i], self.core)
-        )
+        self.sent[i] = self.send(i, self.own, self.slot, device_at(self.chips[i], self.core))
 
     def hand_on(self, i):
-        self.direct[i].wait_recv()
         got = self.out.at[rank_at(self.chips[i], self.core)]
-        self.passed.append(remote(got, got, self.send_sem.at[4 + i], self.recv_sem.at[4 + i], self.sibling))
+        if i:
+            self.sent[i].wait_recv()
+            n, first = (0, 0) if i == 1 else (7, self.half)
+            part = got.at[pl.ds(first, self.half)]
+            self.sent[n] = self.send(n, part, part, device_at(self.chips[3 - i], self.core))
+        else:
+            self.sent[0].wait_recv()
+            self.sent[7].wait_recv()
+        self.passed.append(self.send(4 + i, got, got, self.sibling))
 
     def finish(self):
-        for copy in self.direct.values():
+        for copy in self.sent.values():
             copy.wait_send()
         for copy in self.passed:
             copy.wait()
         self.local.wait()
+
+
+class Scatter:
+    def __init__(self, mine, theirs, outgoing, landing, send_sem, recv_sem):
+        self.mine, self.theirs, self.outgoing, self.landing = mine, theirs, outgoing, landing
+        self.send_sem, self.recv_sem = send_sem, recv_sem
+        self.chips, self.core = places()
+        self.half = outgoing.shape[1]
+        self.sent = []
+
+    def both(self, j, at):
+        return self.mine[j][at, :].astype(f32) + self.theirs[j, at, :].astype(f32)
+
+    def send(self, n, j, bottom, to, arrived=None):
+        def add(i, _):
+            near = pl.ds(pl.multiple_of(i * ROWS, ROWS), ROWS)
+            at = pl.ds(pl.multiple_of(i * ROWS + bottom * self.half, ROWS), ROWS)
+            total = self.both(j, at)
+            if arrived is not None:
+                total = total + self.landing[arrived, near, :].astype(f32)
+            self.outgoing[n, near, :] = total.astype(bf16)
+            return 0
+
+        lax.fori_loop(0, self.half // ROWS, add, 0)
+        self.sent.append(
+            remote(
+                self.outgoing.at[n],
+                self.landing.at[n],
+                self.send_sem.at[n],
+                self.recv_sem.at[n],
+                device_at(self.chips[to], self.core),
+            )
+        )
+
+    def first(self, j):
+        if j in (0, 1):
+            self.send(j, j, 0, 1)
+        if j in (0, 2):
+            self.send(2 if j == 0 else 3, j, 1, 2)
+
+    def second(self):
+        arrived = [self.sent[n].wait_recv for n in (0, 2, 1, 3)]
+        arrived[0]()
+        self.send(4, 2, 0, 2, 0)
+        arrived[2]()
+        self.send(5, 1, 1, 1, 2)
+        arrived[1]()
+        arrived[3]()
+        self.sent[4].wait_recv()
+        self.sent[5].wait_recv()
+
+    def totals(self, use):
+        for bottom in (0, 1):
+
+            def one(i, _, bottom=bottom):
+                near = pl.ds(pl.multiple_of(i * ROWS, ROWS), ROWS)
+                at = pl.ds(pl.multiple_of(i * ROWS + bottom * self.half, ROWS), ROWS)
+                total = self.both(3, at)
+                for n in (1 + 2 * bottom, 4 + bottom):
+                    total = total + self.landing[n, near, :].astype(f32)
+                use(at, total)
+                return 0
+
+            lax.fori_loop(0, self.half // ROWS, one, 0)
+
+    def finish(self):
+        for copy in self.sent:
+            copy.wait_send()
+
+
+def gather_kernel(own_ref, out_ref, local_sem, send_sem, recv_sem):
+    plane = Plane(own_ref, out_ref, local_sem, send_sem, recv_sem)
+    greet([device_at(chip, plane.core) for chip in plane.chips[:3]] + [plane.sibling])
+    plane.start(1)
+    plane.start(2)
+    plane.start_own()
+    for i in (1, 2, 0):
+        plane.hand_on(i)
+    plane.finish()
 
 
 def spread_kernel(
@@ -284,10 +483,10 @@
     act_ref,
     grad_ref,
     mix_all,
-    ffn_all,
     out_all,
     act_all,
     grad_all,
+    ffn_all,
     local_sem,
     swap_send,
     swap_recv,
@@ -337,23 +536,25 @@
     locals_[0].wait()
     mix_line.send(1)
     act.start(2)
-    act.start(0)
     ffn_copies = swap(ffn_ref, ffn_all.at[own], 3)
     out_line.step(1)
-    for i in (1, 2, 0):
-        grad.start(i)
+    act.hand_on(1)
+    act.hand_on(2)
+    grad.start(1)
+    grad.start(2)
     mix_line.step(1)
-    for i in (1, 2, 0):
-        act.hand_on(i)
+    act.hand_on(0)
     for k in range(2, groups):
         out_line.step(k)
         mix_line.step(k)
-    for i in (1, 2, 0):
-        grad.hand_on(i)
+        if k == 2:
+            grad.hand_on(1)
+            grad.hand_on(2)
+    grad.hand_on(0)
     for copy in ffn_copies:
         copy.wait()
-    locals_[1].wait()
-    locals_[2].wait()
+    for copy in locals_[1:]:
+        copy.wait()
     out_line.finish()
     mix_line.finish()
     act.finish()
@@ -367,82 +568,79 @@
         functools.partial(spread_kernel, groups),
         out_shape=[
             jax.ShapeDtypeStruct((groups,) + mix.shape, bf16),
-            jax.ShapeDtypeStruct(ffn.shape, bf16),
             jax.ShapeDtypeStruct((groups,) + out.shape, bf16),
             jax.ShapeDtypeStruct((8,) + act.shape, bf16),
             jax.ShapeDtypeStruct((8,) + grad.shape, bf16),
+            jax.ShapeDtypeStruct(ffn.shape, bf16),
         ],
         in_specs=[hbm] * 5,
         out_specs=[hbm] * 5,
         scratch_shapes=[dma((5,)), dma((6,)), dma((6,))]
         + [dma((2, groups - 1))] * 4
-        + [dma((7,))] * 4,
+        + [dma((8,))] * 4,
         compiler_params=pltpu.CompilerParams(
             collective_id=ident, has_side_effects=True, vmem_limit_bytes=48 * 2**20
         ),
     )(mix, ffn, out, act, grad)
 
 
-def scatter_kernel(part_ref, out_ref, mine, theirs, outgoing, landing, local_sem, send_sem, recv_sem):
+def scatter_kernel(count, *refs):
+    parts, outs = refs[:count], refs[count : 2 * count]
+    mine, theirs, outgoing, landing, local_sem, send_sem, recv_sem = refs[2 * count :]
     chips, core = places()
     sibling = device_at(chips[3], 1 - core)
     greet([device_at(chip, core) for chip in chips[:3]] + [sibling])
-    swaps, locals_ = [], []
-    for j, chip in enumerate(chips):
-        swaps.append(
-            remote(
-                part_ref.at[rank_at(chip, 1 - core)], theirs.at[j], send_sem.at[j], recv_sem.at[j], sibling
-            )
-        )
-        local = pltpu.make_async_copy(part_ref.at[rank_at(chip, core)], mine.at[j], local_sem.at[j])
-        local.start()
-        locals_.append(local)
-    steps = out_ref.shape[0] // ROWS
-    sent = []
-    for j in range(4):
-        locals_[j].wait()
-        swaps[j].wait_recv()
-
-        def add(i, _, j=j):
-            rows = pl.ds(pl.multiple_of(i * ROWS, ROWS), ROWS)
-            total = mine[j, rows, :].astype(f32) + theirs[j, rows, :].astype(f32)
-            if j < 3:
-                outgoing[j, rows, :] = total.astype(bf16)
-            else:
-                out_ref[rows, :] = total
-            return 0
-
-        lax.fori_loop(0, steps, add, 0)
-        if j < 3:
-            sent.append(
+    swaps, locals_, sent = [], [], []
+    for n in range(count):
+        for j, chip in enumerate(chips):
+            swaps.append(
                 remote(
-                    outgoing.at[j],
-                    landing.at[j],
-                    send_sem.at[4 + j],
-                    recv_sem.at[4 + j],
-                    device_at(chips[j], core),
+                    parts[n].at[rank_at(chip, 1 - core)],
+                    theirs.at[n, j],
+                    send_sem.at[n, j],
+                    recv_sem.at[n, j],
+                    sibling,
                 )
             )
-    for copy in sent:
-        copy.wait_recv()
-
-    def finish(i, _):
-        rows = pl.ds(pl.multiple_of(i * ROWS, ROWS), ROWS)
-        total = out_ref[rows, :]
-        for j in range(3):
-            total = total + landing[j, rows, :].astype(f32)
-        out_ref[rows, :] = total
-        return 0
-
-    lax.fori_loop(0, steps, finish, 0)
-    for copy in swaps + sent:
+            local = pltpu.make_async_copy(
+                parts[n].at[rank_at(chip, core)], mine.at[n, j], local_sem.at[n, j]
+            )
+            local.start()
+            locals_.append(local)
+    scatters = []
+    for n in range(count):
+        scatter = Scatter(
+            [mine.at[n, j] for j in range(4)],
+            theirs.at[n],
+            outgoing.at[n],
+            landing.at[n],
+            send_sem.at[n, pl.ds(4, 6)],
+            recv_sem.at[n, pl.ds(4, 6)],
+        )
+        for j in range(4):
+            locals_[4 * n + j].wait()
+            swaps[4 * n + j].wait_recv()
+            if j < 3:
+                scatter.first(j)
+        scatters.append(scatter)
+    for n, scatter in enumerate(scatters):
+        scatter.second()
+
+        def store(at, total, n=n):
+            outs[n][at, :] = total
+
+        scatter.totals(store)
+    for scatter in scatters:
+        scatter.finish()
+    for copy in swaps:
         copy.wait_send()
 
 
-def collect_kernel(count, size, *refs):
+def collect_kernel(count, splits, size, *refs):
     parts, outs = refs[:count], refs[count : count + 3]
     landing = refs[count + 3 : 2 * count + 3]
-    local_sem, send_sem, recv_sem = refs[2 * count + 3 :]
+    wholes = refs[2 * count + 3 : 2 * count + 6]
+    local_sem, send_sem, recv_sem = refs[2 * count + 6 :]
     chips, core = places()
     others = [(j, chips[j], other) for j in range(4) for other in (core, 1 - core)]
     own = rank_at(chips[3], core)
@@ -467,29 +665,39 @@
         copy.wait()
     for copy in copies:
         copy.wait_recv()
-    span = landing[0].shape[2] // 3
-    groups = span // size
-    for which in range(3):
-        for n in range(count):
+    edges = [0]
+    for n in range(count):
+        edges.append(edges[-1] + landing[n].shape[2])
+    for first, last in zip(splits[:-1], splits[1:]):
+        for which in range(3):
             for k in range(8):
-                for g in range(groups):
-                    start = which * span + g * size
-                    place = ((n * groups + g) * 8 + k) * size
-                    outs[which][:, place : place + size] = landing[n][k, :, start : start + size].astype(f32)
+                for group in range(first // size, last // size):
+                    start = 3 * first + which * (last - first) + group * size - first
+                    place = (group * 8 + k) * size
+                    for n in range(count):
+                        low, high = max(start, edges[n]), min(start + size, edges[n + 1])
+                        if low < high:
+                            wholes[which][:, place + low - start : place + high - start] = landing[n][
+                                k, :, low - edges[n] : high - edges[n]
+                            ].astype(f32)
+    for out, whole in zip(outs, wholes):
+        out[...] = whole[...].astype(bf16)
     for copy in copies:
         copy.wait_send()
 
 
-def collect(parts, size, ident):
-    count, rows, wide = len(parts), parts[0].shape[1], parts[0].shape[2]
+def collect(parts, splits, size, ident):
+    count, rows, wide = len(parts), parts[0].shape[1], 8 * splits[-1]
     vmem = pl.BlockSpec(memory_space=pltpu.VMEM)
     dma = pltpu.SemaphoreType.DMA
     return pl.pallas_call(
-        functools.partial(collect_kernel, count, size),
-        out_shape=[jax.ShapeDtypeStruct((rows, count * 8 * wide // 3), f32)] * 3,
+        functools.partial(collect_kernel, count, splits, size),
+        out_shape=[jax.ShapeDtypeStruct((rows, wide), bf16)] * 3,
         in_specs=[pl.BlockSpec(memory_space=pl.ANY)] * count,
         out_specs=[vmem] * 3,
-        scratch_shapes=[pltpu.VMEM((8, rows, wide), bf16)] * count + [dma((count,)), dma((count, 7)), dma((count, 7))],
+        scratch_shapes=[pltpu.VMEM(part.shape, bf16) for part in parts]
+        + [pltpu.VMEM((rows, wide), f32)] * 3
+        + [dma((count,)), dma((count, 7)), dma((count, 7))],
         compiler_params=pltpu.CompilerParams(
             collective_id=ident, has_side_effects=True, vmem_limit_bytes=48 * 2**20
         ),
@@ -505,8 +713,8 @@
         out_specs=hbm,
         scratch_shapes=[
             pltpu.SemaphoreType.DMA,
-            pltpu.SemaphoreType.DMA((7,)),
-            pltpu.SemaphoreType.DMA((7,)),
+            pltpu.SemaphoreType.DMA((8,)),
+            pltpu.SemaphoreType.DMA((8,)),
         ],
         compiler_params=pltpu.CompilerParams(
             collective_id=ident, has_side_effects=True, vmem_limit_bytes=48 * 2**20
@@ -515,26 +723,26 @@
     return out.reshape(-1, v.shape[1])
 
 
-def scatter_plane(part, ident):
-    rows, wide = part.shape[0] // 8, part.shape[1]
+def scatter_plane(parts, ident):
+    count, rows, wide = len(parts), parts[0].shape[0] // 8, parts[0].shape[1]
     return pl.pallas_call(
-        scatter_kernel,
-        out_shape=jax.ShapeDtypeStruct((rows, wide), f32),
-        in_specs=[pl.BlockSpec(memory_space=pl.ANY)],
-        out_specs=pl.BlockSpec(memory_space=pltpu.VMEM),
+        functools.partial(scatter_kernel, count),
+        out_shape=[jax.ShapeDtypeStruct((rows, wide), f32)] * count,
+        in_specs=[pl.BlockSpec(memory_space=pl.ANY)] * count,
+        out_specs=[pl.BlockSpec(memory_space=pltpu.VMEM)] * count,
         scratch_shapes=[
-            pltpu.VMEM((4, rows, wide), bf16),
-            pltpu.VMEM((4, rows, wide), bf16),
-            pltpu.VMEM((3, rows, wide), bf16),
-            pltpu.VMEM((3, rows, wide), bf16),
-            pltpu.SemaphoreType.DMA((4,)),
-            pltpu.SemaphoreType.DMA((7,)),
-            pltpu.SemaphoreType.DMA((7,)),
+            pltpu.VMEM((count, 4, rows, wide), bf16),
+            pltpu.VMEM((count, 4, rows, wide), bf16),
+            pltpu.VMEM((count, 6, rows // 2, wide), bf16),
+            pltpu.VMEM((count, 6, rows // 2, wide), bf16),
+            pltpu.SemaphoreType.DMA((count, 4)),
+            pltpu.SemaphoreType.DMA((count, 10)),
+            pltpu.SemaphoreType.DMA((count, 10)),
         ],
         compiler_params=pltpu.CompilerParams(
             collective_id=ident, has_side_effects=True, vmem_limit_bytes=48 * 2**20
         ),
-    )(part.reshape(8, rows, wide))
+    )(*[part.reshape(8, rows, wide) for part in parts])
 
 
 def dot(a, b):
@@ -578,28 +786,24 @@
     rank = (lax.axis_index("p") * lax.axis_size("c") + lax.axis_index("c")) * copies + x
     ce = width // (groups * ranks)
     fe = units // (groups * ranks)
-    chan, part_unit = ce * groups, fe * groups // HALVES
+    chan, unit = ce * groups, fe * groups
+    splits = (0, unit // QUARTERS, unit)
 
     def columns(w, size):
         w = w.reshape(w.shape[0], groups, members, copies, size)
         w = lax.dynamic_index_in_dim(w, x, axis=3, keepdims=False)
         return jnp.moveaxis(w, 2, 0).reshape(members, w.shape[0], groups * size)
 
-    def ffn_columns(w):
-        w = w.reshape(w.shape[0], HALVES, groups // HALVES, members, copies, fe)
-        w = lax.dynamic_index_in_dim(w, x, axis=4, keepdims=False)
-        return w.transpose(3, 1, 0, 2, 4).reshape(members, HALVES, w.shape[0], part_unit)
-
     def half_rows(w):
         half = w.shape[0] // copies
         return lax.dynamic_slice_in_dim(w, x * half, half, axis=0)
 
+    def gather_rows(v):
+        return lax.all_gather(v, "g", axis=0, tiled=True)
+
     def own_columns(v, size):
         v = v.reshape(groups, ranks, size)
         return lax.dynamic_index_in_dim(v, rank, axis=1, keepdims=False).reshape(1, groups * size)
-
-    def gather_rows(v):
-        return lax.all_gather(v, "g", axis=0, tiled=True)
 
     layer_count = bound_logits.shape[0]
     layer_probs = jax.nn.softmax(bound_logits, axis=0)
@@ -617,7 +821,6 @@
         ],
         axis=1,
     )
-    down_w = gather_rows(half_rows(ffn_down))
     gain = own_columns(out_gain, ce)
 
     places = jnp.arange(doc_ids.shape[0], dtype=jnp.int32)
@@ -636,73 +839,83 @@
     seq_total = doc_ids.shape[0] // SEQ_LEN
     grad_z = cotangent.astype(f32) * (seq_total / (domain_count * per_token))[:, None]
 
-    mix_w, ffn, out_ext, act_one, grad_m = spread(
+    ffn_own = jnp.concatenate(
+        [
+            columns(w, fe)[:, :, first:last]
+            for first, last in zip(splits[:-1], splits[1:])
+            for w in (ffn_gate, ffn_up)
+        ],
+        axis=2,
+    )
+    mix_w, out_ext, act_one, grad_m, ffn = spread(
         groups,
         jnp.concatenate([columns(w_in, ce), columns(w_forget, ce), columns(w_gate_out, ce)], axis=2),
-        jnp.concatenate([ffn_columns(ffn_gate), ffn_columns(ffn_up)], axis=3),
+        ffn_own,
         out_own,
         act_one_own,
         grad_z.astype(bf16),
         0,
     )
     mix_w = mix_w.reshape(width, 3 * chan)
-    ffn, down_w = lax.optimization_barrier((ffn, down_w))
-    ffn_w = [gather_rows(ffn[:, h].reshape(-1, 2 * part_unit)) for h in range(HALVES)]
+    down_w = gather_rows(half_rows(ffn_down))
+    ffn, down_w = lax.optimization_barrier((ffn.reshape(-1, 2 * unit), down_w))
+    ffn_all = gather_rows(ffn)
     act_one, grad_m = act_one.reshape(plane_rows, width), grad_m.reshape(plane_rows, width)
     out_ext = out_ext.reshape(chan, -1)
     out_w = out_ext[:, :width]
     lower = jnp.sum(out_ext[:, width : width + 3].astype(f32), axis=1).reshape(1, chan)
 
-    proj = dot(act_one, mix_w)
-    states, mixed_raw, squares = kernel_call(
-        functools.partial(forward_scan, chan),
-        [
-            jax.ShapeDtypeStruct((plane_rows, chan), f32),
-            jax.ShapeDtypeStruct((plane_rows, chan), bf16),
-            jax.ShapeDtypeStruct((plane_rows, 1), f32),
-        ],
-        proj,
+    proj, states, residual, state_scale, act_two = mixer(
+        chan,
+        act_one,
+        mix_w,
+        out_ext,
         keep,
         lower,
         gain,
-    )
-    pad = jnp.zeros((plane_rows, 126), bf16)
-    part = jnp.concatenate(
-        [dot(mixed_raw, out_w).astype(bf16), *split_hi_lo(squares), pad], axis=1
-    )
-    total = scatter_plane(part, 1)
-    state_scale = lax.rsqrt((total[:, width : width + 1] + total[:, width + 1 : width + 2]) / width + EPS)
-    branch = total[:, :width] * state_scale
-    residual = token_f + branch
+        tokens,
+        ffn_gain.reshape(1, width),
+        1,
+    )
+    act_two = act_two.reshape(plane_rows, width)
+    branch = residual - token_f
     scale_two = lax.rsqrt(jnp.mean(residual * residual, axis=-1, keepdims=True) + EPS)
     normed_two = residual * scale_two
-    act_two = gather_plane((normed_two * ffn_gain).astype(bf16), 2)
 
     def scatter_rows(v):
         return lax.psum_scatter(v, "g", scatter_dimension=0, tiled=True)
 
-    down_part, back_part, ffn_sums = 0.0, 0.0, []
-    for h in range(HALVES):
-        down = down_w[h * part_unit : (h + 1) * part_unit]
-        grad_hidden = dot_nt(grad_m, down)
-        pre = dot(act_two, ffn_w[h])
-        gate_ffn, up_ffn = pre[:, :part_unit], pre[:, part_unit:]
+    backs = [dot_nt(grad_m, down_w[first:last]) for first, last in zip(splits[:-1], splits[1:])]
+    backs, ffn_all = lax.optimization_barrier((backs, ffn_all))
+    grads, pre_grads, hiddens, ffn_sums = [], [], [], []
+    for first, last in zip(splits[:-1], splits[1:]):
+        some = last - first
+        pre = dot(act_two, ffn_all[:, 2 * first : 2 * last])
+        gate_ffn, up_ffn = pre[:, :some], pre[:, some:]
         sig = jax.nn.sigmoid(gate_ffn)
         gate_silu = gate_ffn * sig
         hidden = (gate_silu * up_ffn).astype(bf16)
-        grad_gate = (grad_hidden * up_ffn * (sig * (1.0 + gate_ffn * (1.0 - sig)))).astype(bf16)
-        grad_up = (grad_hidden * gate_silu).astype(bf16)
-        grad_pre = jnp.concatenate([grad_gate, grad_up], axis=1)
-        grads = jnp.concatenate(
-            [dot_tn(act_two, grad_pre).astype(bf16), dot_tn(grad_m, hidden).astype(bf16)], axis=1
+        back = backs[first > 0]
+        grad_gate = (back * up_ffn * (sig * (1.0 + gate_ffn * (1.0 - sig)))).astype(bf16)
+        grad_up = (back * gate_silu).astype(bf16)
+        pre_grads.append(jnp.concatenate([grad_gate, grad_up], axis=1))
+        hiddens.append(hidden)
+        grads.append(
+            jnp.concatenate(
+                [dot_tn(act_two, pre_grads[-1]).astype(bf16), dot_tn(grad_m, hidden).astype(bf16)], axis=1
+            )
         )
-        grads, grad_pre, hidden = lax.optimization_barrier((grads, grad_pre, hidden))
-        ffn_sums.append(scatter_rows(grads))
-        down_part = down_part + dot(hidden, down)
-        back_part = back_part + dot_nt(grad_pre, ffn_w[h])
-    down_part, back_part = down_part.astype(bf16), back_part.astype(bf16)
-
-    back_term = scatter_plane(back_part, 3)
+        if first == 0:
+            kept = grads[0].shape[1] // 128 * 128
+            ffn_sums.append(scatter_rows(grads[0][:, :kept]))
+            grads[0], act_two = lax.optimization_barrier((grads[0][:, kept:], act_two))
+    far_grads = jnp.concatenate(grads, axis=1)
+    pre_grads, hiddens, far_grads = lax.optimization_barrier((pre_grads, hiddens, far_grads))
+    ffn_sums.append(scatter_rows(far_grads))
+    down_part = dot(jnp.concatenate(hiddens, axis=1), down_w).astype(bf16)
+    back_part = dot_nt(jnp.concatenate(pre_grads, axis=1), ffn_all).astype(bf16)
+
+    (back_term,) = scatter_plane([back_part], 3)
     scaled_two = back_term * ffn_gain
     grad_resid = grad_z + scale_two * (
         scaled_two - normed_two * jnp.mean(scaled_two * normed_two, axis=-1, keepdims=True)
@@ -749,25 +962,31 @@
     out_grads = out_grads[:, : folds * 3 * chan].reshape(groups, ce, folds, 3 * chan)
     out_grads = jnp.moveaxis(out_grads, 2, 1).reshape(groups, folds * ce, 3 * chan)
     late_grads = jnp.concatenate([mix_grads, out_grads], axis=1).reshape(-1, 3 * chan)
-    late_grads, ffn_sums = lax.optimization_barrier((late_grads, ffn_sums))
+    late_grads, ffn_sums, in_part, down_part = lax.optimization_barrier(
+        (late_grads, ffn_sums, in_part, down_part)
+    )
     late_sum = scatter_rows(late_grads)
     mix_sum = late_sum[: width // groups]
     out_sum = jnp.moveaxis(late_sum[width // groups :].reshape(folds, ce, 3 * chan), 1, 0)
     out_sum = out_sum.reshape(ce, -1).astype(f32)
     summed_wout = out_sum[:, :width]
     grad_lower = out_sum[:, width] + out_sum[:, width + 1]
-    down_term = scatter_plane(down_part, 5)
+    grad_act, down_term = scatter_plane([in_part, down_part], 6)
     output_rows = (residual + down_term).astype(bf16)
 
-    grad_act = scatter_plane(in_part, 6)
     scaled_one = grad_act * norm_gain
     grad_tokens = grad_resid + scale_one * (
         scaled_one - normed_one * jnp.mean(scaled_one * normed_one, axis=-1, keepdims=True)
     )
 
-    summed_fgate, summed_fup, fdown = collect([v.reshape(ranks, -1, 3 * part_unit) for v in ffn_sums], fe, 7)
+    summed_fgate, summed_fup, fdown = [
+        v.astype(f32)
+        for v in collect([v.reshape(ranks, -1, v.shape[1]) for v in ffn_sums], splits, fe, 7)
+    ]
     summed_fdown = fdown.T
-    summed_win, summed_wforget, summed_wgate = collect([mix_sum.reshape(ranks, -1, 3 * chan)], ce, 8)
+    summed_win, summed_wforget, summed_wgate = [
+        v.astype(f32) for v in collect([mix_sum.reshape(ranks, -1, 3 * chan)], (0, chan), ce, 8)
+    ]
     first = (g * ranks + rank) * ce
 
     def own_gain(gain, pairs):

time: 553 us -> 536 us (0.969)
  waiting for transfers between devices: 15.6 us -> 39.7 us
  Pallas kernels: 349 us -> 327 us
  local copies, waits for them, and re-layouts: 64.1 us -> 44.2 us
  other arithmetic: 29 us -> 37.1 us
    pallas_call x2 -> x1, Pallas kernels: 60.1 us -> 24.4 us  [gather_plane(): pl.pallas_call(gather_kernel, out_shape=jax.ShapeDtypeStruct((8,) + v.sha...]
    pallas_call x6 -> x5, Pallas kernels: 161 us -> 178 us  [the longest x1 70.2 us: mixer(): pl.pallas_call(functools.partial(mixer_kernel, chan), out_shape=[jax.Shap...]
    all_gather x3 -> x2, waiting for transfers between devices: 12 us -> 25.7 us  [gather_rows(): return lax.all_gather(v, 'g', axis=0, tiled=True)]
    pallas_call x2 -> x1, Pallas kernels: 19.8 us -> 9.11 us  [kernel_call(): pl.pallas_call(kernel, out_shape=outs, in_specs=[vmem] * len(args), out_s...]
    reduce_scatter x3, waiting for transfers between devices: 3.49 us -> 13.9 us  [scatter_rows(): return lax.psum_scatter(v, 'g', scatter_dimension=0, tiled=True)]
    unnamed x136 -> x134, local copies, waits for them, and re-layouts: 25.2 us -> 17.4 us
    pallas_call x1, Pallas kernels: 108 us -> 115 us  [spread(): pl.pallas_call(functools.partial(spread_kernel, groups), out_shape=[jax.S...]
    concatenate x1, local copies, waits for them, and re-layouts: 7.81 us -> 1.3 us  [body(): jnp.concatenate([columns(w, fe)[:, :, first:last] for first, last in zip(...]
  transfers between devices with their start and end apart: 6 -> 5, of which waited for: 3 -> 2; matrix products, arithmetic and copies ran while one was open for 25% -> 22% of each run, Pallas kernels for 62% -> 59%
where the time goes in v4:
time: 536 us; the launch traced here: 531 us
  Pallas kernels  327 us (61%)
  matrix products  67.1 us (13%)
  local copies, waits for them, and re-layouts  44.2 us (8%)
  waiting for transfers between devices  39.7 us (7%)
  other arithmetic  37.1 us (7%)
  between operations  15.4 us (3%)
    pallas_call x1, Pallas kernels, spread(): pl.pallas_call(functools.partial(spread_kernel, groups), out_shape=[jax.S...  115 us
    pallas_call x1, Pallas kernels, mixer(): pl.pallas_call(functools.partial(mixer_kernel, chan), out_shape=[jax.Shap...  70.2 us
    pallas_call x2, Pallas kernels, scatter_plane(): pl.pallas_call(functools.partial(scatter_kernel, count), out_shape=[jax.S...  66.5 us
    pallas_call x2, Pallas kernels, collect(): pl.pallas_call(functools.partial(collect_kernel, count, splits, size), ou...  41.3 us
    all_gather x2, waiting for transfers between devices, gather_rows(): return lax.all_gather(v, 'g', axis=0, tiled=True)  25.7 us
    dot_general x5, matrix products, dot_nt(): lax.dot_general(a, b, (((1,), (1,)), ((), ())), preferred_element_type=f32)  24.8 us
    pallas_call x1, Pallas kernels, gather_plane(): pl.pallas_call(gather_kernel, out_shape=jax.ShapeDtypeStruct((8,) + v.sha...  24.4 us
    dot_general x3, matrix products, dot(): return jnp.dot(a, b, preferred_element_type=f32)  21.2 us
  transfers between devices with their start and end apart: 5, of which 2 were waited for; matrix products, arithmetic and copies ran while one was open for 22% of the time, Pallas kernels for 59%

profile of v4, /device:TPU:0, one launch (start us, length us, event | category | flops | bytes accessed | tf_op | source)
XLA Modules:
  0.0 530.9 jit_solution(14744298693293896115)
XLA Ops:
  26.0 115.0 %shard_map.255 = (bf16[4,4,128,768]{3,2,1,0:T(8,128)(2,1)}, bf16[4,64,2176]{2,1,0:T(8,128)(2,1)S(1)}, bf16[8,128,2048]{2,1,0:T(8,128)(2,1)}, bf16[8,128,2048]{2,1,0:T(8,128)(2,1)}, bf16[4,128,1408]{2,1,0:T(8,128)(2,1)}) custom-call(bf16[4,128,768]{2,1,0:T(8,128)(2,1)S(1)} %pad_maximum_fusion.4.mix_ref, bf16[4,128,1408]{2,1,0:T(8,128)(2,1)S(1)} %concatenate.43.ffn_ref, ...), custom_call_target="tpu_custom_call" | custom-call | tf_op jit(solution)/shard_map/pallas_call | solution.py:567
  145.3 70.2 %shard_map.256 = (f32[1024,768]{1,0:T(8,128)}, f32[1024,256]{1,0:T(8,128)}, f32[128,2048]{1,0:T(8,128)}, f32[128,1]{1,0:T(8,128)}, bf16[8,128,2048]{2,1,0:T(8,128)(2,1)}) custom-call(bf16[1024,2048]{1,0:T(8,128)(2,1)} %bitcast.112, bf16[2048,768]{1,0:T(8,128)(2,1)} %bitcast.119, bf16[256,2176]{1,0:T(8,128)(2,1)} %bitcast.101, f32[1024,1]{1,0:T(8,128)} %copy.175.keep_ref, ...), custom_call_target="tpu_custom_call" | custom-call | tf_op jit(solution)/shard_map/pallas_call | solution.py:157
  215.6 2.8 fusion.34
  218.4 3.9 fusion.13
  222.3 25.7 %all-gather.5.cloned.1.call-done = bf16[2048,1408]{1,0:T(8,128)(2,1)} async-done(((bf16[512,1408]{1,0:T(8,128)(2,1)}), bf16[2048,1408]{1,0:T(8,128)(2,1)}) %all-gather.5.cloned.1.call-update) | async-done | bytes 5767184 | tf_op jit(solution)/shard_map/all_gather | solution.py:802
  247.9 4.4 fusion.15
  259.8 11.8 %fusion = f32[1024,1056]{0,1:T(8,128)S(1)} fusion(bf16[1024,2048]{1,0:T(8,128)(2,1)} %bitcast.139, bf16[2048,1408]{1,0:T(8,128)(2,1)} %all-gather.5.cloned.1.call-done), kind=kOutput, calls=%fused_computation.2 | convolution fusion | flops 4429185024 | bytes 13238272 | tf_op jit(solution)/shard_map/dot_general | solution.py:749
  279.0 5.8 %convolution_convert_fusion = bf16[2048,1056]{0,1:T(8,128)(2,1)S(1)} fusion(bf16[1024,2048]{1,0:T(8,128)(2,1)S(1)} %bitcast.141, bf16[1024,528]{0,1:T(8,128)(2,1)S(1)} %get-tuple-element.107, bf16[1024,528]{0,1:T(8,128)(2,1)S(1)} %get-tuple-element.106), kind=kOutput, calls=%fused_computation | convolution fusion | flops 4435673088 | bytes 10682368 | tf_op jit(solution)/shard_map/dot_general | solution.py:757
  284.8 8.9 %pad_maximum_fusion = bf16[2048,1600]{0,1:T(8,128)(2,1)} fusion(bf16[2048,528]{0,1:T(8,128)(2,1)S(1)} %convolution_convert_fusion.5, bf16[2048,1056]{0,1:T(8,128)(2,1)S(1)} %convolution_convert_fusion, bf16[2048,16]{0,1:T(8,128)(2,1)S(1)} %slice-done), kind=kLoop, calls=%fused_computation.1 | loop fusion | flops 19660800 | bytes 13107200 | tf_op jit(solution)/shard_map/concatenate | solution.py:912
  295.2 9.5 %convolution_convert_fusion.2 = bf16[1024,2048]{1,0:T(8,128)(2,1)S(1)} fusion(bf16[2048,1408]{1,0:T(8,128)(2,1)} %all-gather.5.cloned.1.call-done, bf16[1024,1056]{0,1:T(8,128)(2,1)} %pad_maximum_fusion.2, bf16[1024,352]{0,1:T(8,128)(2,1)S(1)} %copy-done.40), kind=kOutput, calls=%fused_computation.6 | convolution fusion | flops 5913444352 | bytes 12845056 | tf_op jit(solution)/shard_map/dot_general | solution.py:753
  304.7 23.2 %shard_map.257 = f32[128,2048]{1,0:T(8,128)S(1)} custom-call(bf16[8,128,2048]{2,1,0:T(8,128)(2,1)S(1)} %bitcast.97), custom_call_target="tpu_custom_call" | custom-call | tf_op jit(solution)/shard_map/pallas_call | solution.py:728
  331.2 24.4 %shard_map.258 = bf16[8,128,2176]{2,1,0:T(8,128)(2,1)S(1)} custom-call(bf16[128,2176]{1,0:T(8,128)(2,1)S(1)} %concatenate.50.own_ref), custom_call_target="tpu_custom_call" | custom-call | tf_op jit(solution)/shard_map/pallas_call | solution.py:709
  358.3 3.6 fusion.4.do_ref
  361.9 9.1 %shard_map.259 = (bf16[1024,768]{1,0:T(8,128)(2,1)S(1)}, bf16[1024,256]{1,0:T(8,128)(2,1)S(1)}, f32[1,256]{1,0:T(1,128)S(1)}) custom-call(f32[1024,768]{1,0:T(8,128)} %get-tuple-element.55.proj_ref, f32[1024,256]{1,0:T(8,128)S(1)} %copy-done.7, f32[1024,256]{1,0:T(8,128)S(1)} %fusion.4.do_ref, f32[1024,2]{1,0:T(8,128)S(1)} %copy.180.info_ref, ...), custom_call_target="tpu_custom_call" | custom-call | tf_op jit(solution)/shard_map/pallas_call | solution.py:244
  371.4 4.5 fusion.9
  379.4 3.9 reshape.318
  385.0 5.7 %convolution_convert_fusion.4 = bf16[2048,768]{1,0:T(8,128)(2,1)S(1)} fusion(bf16[1024,2048]{1,0:T(8,128)(2,1)} %bitcast.113, bf16[1024,768]{1,0:T(8,128)(2,1)S(1)} %get-tuple-element.70), kind=kOutput, calls=%fused_computation.12 | convolution fusion | flops 3222798336 | bytes 8912896 | tf_op jit(solution)/shard_map/dot_general | solution.py:757
  394.5 5.1 convolution_convert_fusion.1
  399.6 5.0 convolution_convert_fusion.3
  404.6 13.9 %reduce-scatter.6.cloned.1.call-done = bf16[512,1600]{0,1:T(8,128)(2,1)} async-done(((bf16[2048,1600]{0,1:T(8,128)(2,1)}), bf16[512,1600]{0,1:T(8,128)(2,1)}) %reduce-scatter.6.cloned.1.call-update) | async-done | bytes 1638416 | tf_op jit(solution)/shard_map/reduce_scatter | solution.py:886
  420.6 2.7 copy.187
  423.3 43.3 %shard_map.260 = (f32[128,2048]{1,0:T(8,128)S(1)}, f32[128,2048]{1,0:T(8,128)S(1)}) custom-call(bf16[8,128,2048]{2,1,0:T(8,128)(2,1)} %bitcast.115, bf16[8,128,2048]{2,1,0:T(8,128)(2,1)} %bitcast.114), custom_call_target="tpu_custom_call" | custom-call | tf_op jit(solution)/shard_map/pallas_call | solution.py:728
  466.7 28.1 %shard_map.262 = (bf16[64,5632]{1,0:T(8,128)(2,1)S(1)}, bf16[64,5632]{1,0:T(8,128)(2,1)S(1)}, bf16[64,5632]{1,0:T(8,128)(2,1)S(1)}) custom-call(bf16[8,64,512]{2,1,0:T(8,128)(2,1)S(1)} %bitcast.99, bf16[8,64,1600]{2,1,0:T(8,128)(2,1)S(1)} %bitcast.93), custom_call_target="tpu_custom_call" | custom-call | tf_op jit(solution)/shard_map/pallas_call | solution.py:693
  505.1 13.2 %shard_map.261 = (bf16[64,2048]{1,0:T(8,128)(2,1)S(1)}, bf16[64,2048]{1,0:T(8,128)(2,1)S(1)}, bf16[64,2048]{1,0:T(8,128)(2,1)S(1)}) custom-call(bf16[8,64,768]{2,1,0:T(8,128)(2,1)S(1)} %bitcast.98), custom_call_target="tpu_custom_call" | custom-call | tf_op jit(solution)/shard_map/pallas_call | solution.py:693
  (249 shorter events, 71.7 us)
Async XLA Ops:
  7.2 133.8 %all-gather.3.cloned.1.call-start = ((), (), s32[]{:S(2)}) async-start(), calls=%async_computation.3 | async-start | bytes 3604480 | tf_op jit(solution)/shard_map/all_gather | solution.py:802
  9.5 238.4 %all-gather.5.cloned.1.call-start = ((), (), s32[]{:S(2)}) async-start(), calls=%async_computation.4 | async-start | bytes 7208960 | tf_op jit(solution)/shard_map/all_gather | solution.py:802
  26.0 115.6 %copy-start.48 = (s32[4096]{0:T(1024)S(1)}, s32[4096]{0:T(1024)}, u32[]{:S(2)}) copy-start(s32[4096]{0:T(1024)} %param.19) | copy-start | bytes 49156
  26.0 116.1 %copy-start.49 = (f32[2048]{0:T(1024)S(1)}, f32[2048]{0:T(1024)}, u32[]{:S(2)}) copy-start(f32[2048]{0:T(1024)} %param.29) | copy-start | bytes 24580
  141.0 4.3 copy-start.5
  141.1 263.6 %reduce-scatter.4.cloned.1.call-start = ((), (), s32[]{:S(2)}) async-start(), calls=%async_computation.5 | async-start | bytes 2621440 | tf_op jit(solution)/shard_map/reduce_scatter | solution.py:886
  145.3 70.2 %copy-start.15 = (bf16[8,128,2048]{2,1,0:T(8,128)(2,1)S(1)}, bf16[8,128,2048]{2,1,0:T(8,128)(2,1)}, u32[]{:S(2)}) copy-start(bf16[8,128,2048]{2,1,0:T(8,128)(2,1)} %get-tuple-element.57) | copy-start | bytes 12582916
  259.6 158.9 %reduce-scatter.6.cloned.1.call-start = ((), (), s32[]{:S(2)}) async-start(), calls=%async_computation.6 | async-start | bytes 8192000 | tf_op jit(solution)/shard_map/reduce_scatter | solution.py:886
  259.8 11.8 %copy-start.26 = (f32[1024,528]{0,1:T(8,128)S(1)}, f32[1024,528]{0,1:T(8,128)}, u32[]{:S(2)}) copy-start(f32[1024,528]{0,1:T(8,128)} %fusion.13) | copy-start | bytes 6488068
  278.9 5.8 %slice-start = ((bf16[2048,176]{0,1:T(8,128)(2,1)}), bf16[2048,16]{0,1:T(8,128)(2,1)S(1)}, s32[]{:S(2)}) async-start(bf16[2048,176]{0,1:T(8,128)(2,1)} %copy-done.24), calls=%async_computation.8 | async-start | bytes 131072 | tf_op jit(solution)/shard_map/slice | solution.py:911
  293.8 208.9 %reduce-scatter.8.cloned.1.call-start = ((), (), s32[]{:S(2)}) async-start(), calls=%async_computation.7 | async-start | bytes 5406720 | tf_op jit(solution)/shard_map/reduce_scatter | solution.py:886
  304.7 23.2 %copy-start.44 = (f32[2048]{0:T(1024)S(1)}, f32[2048]{0:T(1024)}, u32[]{:S(2)}) copy-start(f32[2048]{0:T(1024)} %param.30) | copy-start | bytes 24580
  394.5 5.1 copy-start.25
  423.3 43.4 %copy-start.4 = (bf16[512,512]{1,0:T(8,128)(2,1)S(1)}, bf16[512,512]{1,0:T(8,128)(2,1)}, u32[]{:S(2)}) copy-start(bf16[512,512]{1,0:T(8,128)(2,1)} %copy.186) | copy-start | bytes 1572868
  466.6 28.1 %copy-start.12 = (bf16[128,2048]{1,0:T(8,128)(2,1)S(1)}, bf16[128,2048]{1,0:T(8,128)(2,1)}, u32[]{:S(2)}) copy-start(bf16[128,2048]{1,0:T(8,128)(2,1)} %token_ref.1) | copy-start | bytes 1572868
  466.6 28.1 %copy-start.46 = (f32[2048]{0:T(1024)S(1)}, f32[2048]{0:T(1024)}, u32[]{:S(2)}) copy-start(f32[2048]{0:T(1024)} %param.28) | copy-start | bytes 24580
  466.6 28.1 %copy-start.55 = (f32[128]{0:T(128)S(1)}, f32[128]{0:T(128)}, u32[]{:S(2)}) copy-start(f32[128]{0:T(128)} %copy-done.54) | copy-start | bytes 1540
  466.7 28.5 %copy-start.20 = (bf16[128,5632]{1,0:T(8,128)(2,1)S(1)}, bf16[128,5632]{1,0:T(8,128)(2,1)}, u32[]{:S(2)}) copy-start(bf16[128,5632]{1,0:T(8,128)(2,1)} %param.25) | copy-start | bytes 4325380
  503.9 14.5 %copy-start.31 = (bf16[128,2048]{1,0:T(8,128)(2,1)S(1)}, bf16[128,2048]{1,0:T(8,128)(2,1)}, u32[]{:S(2)}) copy-start(bf16[128,2048]{1,0:T(8,128)(2,1)} %param.21) | copy-start | bytes 1572868
  504.1 16.5 %copy-start.51 = (f32[64]{0:T(128)S(1)}, f32[64]{0:T(128)}, u32[]{:S(2)}) copy-start(f32[64]{0:T(128)} %copy-done.50) | copy-start | bytes 772
  504.1 16.5 %copy-start.53 = (f32[24]{0:T(128)S(1)}, f32[24]{0:T(128)}, u32[]{:S(2)}) copy-start(f32[24]{0:T(128)} %copy-done.52) | copy-start | bytes 292
  504.1 17.3 %copy-start.33 = (bf16[128,2048]{1,0:T(8,128)(2,1)S(1)}, bf16[128,2048]{1,0:T(8,128)(2,1)}, u32[]{:S(2)}) copy-start(bf16[128,2048]{1,0:T(8,128)(2,1)} %param.22) | copy-start | bytes 1572868
  505.1 17.3 %copy-start.35 = (bf16[128,2048]{1,0:T(8,128)(2,1)S(1)}, bf16[128,2048]{1,0:T(8,128)(2,1)}, u32[]{:S(2)}) copy-start(bf16[128,2048]{1,0:T(8,128)(2,1)} %param.23) | copy-start | bytes 1572868
  505.1 18.9 %copy-start.1 = (bf16[352,2048]{1,0:T(8,128)(2,1)S(1)}, bf16[352,2048]{1,0:T(8,128)(2,1)}, u32[]{:S(2)}) copy-start(bf16[352,2048]{1,0:T(8,128)(2,1)} %param.27) | copy-start | bytes 4325380
  (44 other events, 108.2 us)
Sparse Core Ops, SparseCore 0:
  10.2 80.6 all-gather.2
  141.2 106.7 all-gather.4
  259.7 42.1 reduce-scatter.3
  304.2 114.2 reduce-scatter.5
  420.8 79.3 reduce-scatter.7

commit v5 on v4

--- a/solution.py
+++ b/solution.py
@@ -13,6 +13,7 @@
 EPS = 1e-06
 ROWS = 16
 QUARTERS = 4
+TILES = 12
 PLANE = ("p", "c", "x")
 ALL = ("g", "p", "c", "x")
 f32 = jnp.float32
@@ -60,20 +61,45 @@
 
 
 def mixer_kernel(
+    groups,
     chan,
+    act_hbm,
+    mix_hbm,
+    grad_hbm,
+    down_hbm,
+    near_ref,
+    far_ref,
+    out_w_hbm,
+    keep_ref,
+    gain_ref,
+    token_hbm,
+    ffn_gain_ref,
+    proj_hbm,
+    h_hbm,
+    pre_grad_hbm,
+    kept_hbm,
+    near_hbm,
+    residual_hbm,
+    hidden_hbm,
+    rest_hbm,
+    act_two_ref,
+    far_all,
+    scale_ref,
+    lower_ref,
+    token_ref,
+    out_w_ref,
     act_ref,
     mix_ref,
-    out_w_ref,
-    keep_ref,
-    lower_ref,
-    gain_ref,
-    token_ref,
-    ffn_gain_ref,
+    grad_ref,
+    down_ref,
     proj_ref,
     h_ref,
+    pre_grad_ref,
+    kept_ref,
+    near_all,
     residual_ref,
-    scale_ref,
-    act_two_ref,
+    hidden_ref,
+    rest_ref,
     raw,
     squares,
     part,
@@ -81,19 +107,48 @@
     outgoing,
     landing,
     own_two,
+    two,
+    pre_ref,
+    grad_tmp,
     swap_send,
     swap_recv,
     send_sem,
     recv_sem,
     local_sem,
+    move_sem,
     act_send,
     act_recv,
+    line_send,
+    line_recv,
 ):
+    moves = []
+
+    def move(src, dst):
+        copy = pltpu.make_async_copy(src, dst, move_sem.at[len(moves)])
+        copy.start()
+        moves.append(copy)
+        return copy
+
+    loads = [
+        move(*pair)
+        for pair in ((act_hbm, act_ref), (mix_hbm, mix_ref), (grad_hbm, grad_ref), (out_w_hbm, out_w_ref), (token_hbm, token_ref))
+    ]
     chips, core = places()
     sibling = device_at(chips[3], 1 - core)
-    greet([device_at(chip, core) for chip in chips[:3]] + [sibling])
-    rows, width = token_ref.shape
+    greet([device_at(chip, core) for chip in chips[:3]] + [sibling] + line_partners(groups))
+    near = Line(groups, near_ref, near_all, line_send.at[0], line_recv.at[0], local_sem.at[1])
+    far = Line(groups, far_ref, far_all, line_send.at[1], line_recv.at[1], local_sem.at[2])
+    near.send(1)
+    far.send(1)
+    loads.append(move(down_hbm.at[pl.ds(0, down_ref.shape[0])], down_ref))
+    rows, width = token_hbm.shape
     block = 2 * rows
+    loads[3].wait()
+    loads[4].wait()
+    turned = jnp.transpose(out_w_ref[:, width:].astype(f32))
+    lower_ref[...] = turned[0:1, :] + turned[1:2, :] + turned[2:3, :]
+    loads[0].wait()
+    loads[1].wait()
 
     def project(i, _):
         at = pl.ds(pl.multiple_of(i * block, block), block)
@@ -102,6 +157,9 @@
 
     lax.fori_loop(0, act_ref.shape[0] // block, project, 0)
     forward_scan(chan, proj_ref, keep_ref, lower_ref, gain_ref, h_ref, raw, squares)
+    near.step(1)
+    move(proj_ref, proj_hbm)
+    move(h_ref, h_hbm)
 
     lane = lax.broadcasted_iota(jnp.int32, (rows, part.shape[1] - width), 1)
 
@@ -126,6 +184,7 @@
         swaps[j].wait_recv()
         if j < 3:
             scatter.first(j)
+    far.step(1)
     scatter.second()
 
     def finish(at, total):
@@ -137,35 +196,105 @@
         own_two[at, :] = (residual * norm * ffn_gain_ref[...]).astype(bf16)
 
     scatter.totals(finish)
-    plane = Plane(own_two, act_two_ref, local_sem.at[0], act_send, act_recv)
+    move(residual_ref, residual_hbm)
+    plane = Plane(own_two, two, local_sem.at[0], act_send, act_recv)
     plane.start(1)
     plane.start(2)
     plane.start_own()
     for copy in swaps:
         copy.wait_send()
     scatter.finish()
-    for i in (1, 2, 0):
-        plane.hand_on(i)
+    near.step(2)
+    plane.hand_on(1)
+    plane.hand_on(2)
+    far.step(2)
+    plane.hand_on(0)
+    for k in range(3, groups):
+        near.step(k)
     plane.finish()
-
-
-def mixer(chan, act, mix_w, out_ext, keep, lower, gain, tokens, ffn_gain, ident):
+    near.finish()
+    move(two, act_two_ref)
+    move(near_all, near_hbm)
+    loads[2].wait()
+    loads[5].wait()
+
+    some = hidden_ref.shape[1]
+    depth = near_all.shape[1]
+
+    def quarter(i, _):
+        at = pl.ds(pl.multiple_of(i * block, block), block)
+        act = two[pl.ds(2 * i, 2)].reshape(block, width)
+        pre = jnp.zeros((block, near_all.shape[2]), f32)
+        for g in range(groups):
+            pre += dot(act[:, g * depth : (g + 1) * depth], near_all[g])
+        pre_ref[...] = pre
+        gate, up = pre_ref[:, :some], pre_ref[:, some : 2 * some]
+        back = dot_nt(grad_ref[at, :], down_ref[...])
+        sig = jax.nn.sigmoid(gate)
+        gate_silu = gate * sig
+        hidden_ref[at, :] = (gate_silu * up).astype(bf16)
+        pre_ref[:, :some] = back * up * (sig * (1.0 + gate * (1.0 - sig)))
+        pre_ref[:, some : 2 * some] = back * gate_silu
+        pre_grad_ref[at, :] = pre_ref[:, : 2 * some].astype(bf16)
+        return 0
+
+    lax.fori_loop(0, act_ref.shape[0] // block, quarter, 0)
+
+    def weights(i, _):
+        at = pl.ds(pl.multiple_of(i * block, block), block)
+        act = two[:, :, at].reshape(act_ref.shape[0], block)
+        grad_tmp[:, : 2 * some] = dot_tn(act, pre_grad_ref[...])
+        grad_tmp[:, 2 * some : 3 * some] = dot_tn(grad_ref[:, at], hidden_ref[...])
+        kept = kept_ref.shape[1]
+        kept_ref[at, :] = grad_tmp[:, :kept].astype(bf16)
+        rest_ref[at, :] = grad_tmp[:, kept : 3 * some].astype(bf16)
+        return 0
+
+    lax.fori_loop(0, width // block, weights, 0)
+    move(pre_grad_ref, pre_grad_hbm)
+    move(kept_ref, kept_hbm)
+    move(hidden_ref, hidden_hbm)
+    move(rest_ref, rest_hbm)
+    for k in range(3, groups):
+        far.step(k)
+    far.finish()
+    for copy in moves[6:]:
+        copy.wait()
+
+
+def mixer(
+    groups, chan, act, mix_w, out_ext, keep, gain, tokens, ffn_gain, grad, down, some, near, far, ident
+):
     total, (rows, width) = act.shape[0], tokens.shape
     vmem, hbm = pl.BlockSpec(memory_space=pltpu.VMEM), pl.BlockSpec(memory_space=pl.ANY)
     dma = pltpu.SemaphoreType.DMA
     wide = width + 128
+    kept = 3 * some // 128 * 128
+    moved = [
+        jax.ShapeDtypeStruct((total, 3 * chan), f32),
+        jax.ShapeDtypeStruct((total, chan), f32),
+        jax.ShapeDtypeStruct((total, 2 * some), bf16),
+        jax.ShapeDtypeStruct((width, kept), bf16),
+        jax.ShapeDtypeStruct((groups,) + near.shape, bf16),
+        jax.ShapeDtypeStruct((rows, width), f32),
+        jax.ShapeDtypeStruct((total, some), bf16),
+        jax.ShapeDtypeStruct((width, 3 * some - kept), bf16),
+    ]
     return pl.pallas_call(
-        functools.partial(mixer_kernel, chan),
-        out_shape=[
-            jax.ShapeDtypeStruct((total, 3 * chan), f32),
-            jax.ShapeDtypeStruct((total, chan), f32),
-            jax.ShapeDtypeStruct((rows, width), f32),
+        functools.partial(mixer_kernel, groups, chan),
+        out_shape=moved
+        + [
+            jax.ShapeDtypeStruct((8, rows, width), bf16),
+            jax.ShapeDtypeStruct((groups,) + far.shape, bf16),
             jax.ShapeDtypeStruct((rows, 1), f32),
-            jax.ShapeDtypeStruct((8, rows, width), bf16),
+            jax.ShapeDtypeStruct((1, chan), f32),
         ],
-        in_specs=[vmem] * 8,
-        out_specs=[vmem] * 4 + [hbm],
-        scratch_shapes=[
+        in_specs=[hbm] * 7 + [vmem] * 2 + [hbm, vmem],
+        out_specs=[hbm] * 10 + [vmem] * 2,
+        scratch_shapes=[pltpu.VMEM(v.shape, v.dtype) for v in (tokens, out_ext, act, mix_w, grad)]
+        + [pltpu.VMEM((some, width), bf16)]
+        + [pltpu.VMEM(v.shape, v.dtype) for v in moved]
+        + [
             pltpu.VMEM((total, chan), bf16),
             pltpu.VMEM((total, 1), f32),
             pltpu.VMEM((total, wide), bf16),
@@ -173,18 +302,166 @@
             pltpu.VMEM((6, rows // 2, wide), bf16),
             pltpu.VMEM((6, rows // 2, wide), bf16),
             pltpu.VMEM((rows, width), bf16),
+            pltpu.VMEM((8, rows, width), bf16),
+            pltpu.VMEM((2 * rows, near.shape[1]), f32),
+            pltpu.VMEM((2 * rows, 3 * some), f32),
             dma((4,)),
             dma((4,)),
             dma((6,)),
             dma((6,)),
-            dma((1,)),
+            dma((3,)),
+            dma((15,)),
             dma((8,)),
             dma((8,)),
+            dma((2, 2, groups - 1)),
+            dma((2, 2, groups - 1)),
         ],
         compiler_params=pltpu.CompilerParams(
-            collective_id=ident, has_side_effects=True, vmem_limit_bytes=56 * 2**20
+            collective_id=ident, has_side_effects=True, vmem_limit_bytes=60 * 2**20
         ),
-    )(act, mix_w, out_ext, keep, lower, gain, tokens, ffn_gain)
+    )(act, mix_w, grad, down, near, far, out_ext, keep, gain, tokens, ffn_gain)
+
+
+def feed_kernel(
+    first,
+    act_hbm,
+    grad_hbm,
+    near_hbm,
+    far_hbm,
+    down_hbm,
+    pre_first_ref,
+    rest_ref,
+    weights_hbm,
+    pre_grad_hbm,
+    hidden_hbm,
+    act_ref,
+    grad_ref,
+    near_ref,
+    far_ref,
+    down_ref,
+    weights_ref,
+    pre_grad_ref,
+    hidden_ref,
+    wide_ref,
+    side_ref,
+    lead_ref,
+    fold_ref,
+    move_sem,
+    store_sem,
+):
+    moves = []
+
+    def move(src, dst):
+        copy = pltpu.make_async_copy(src, dst, move_sem.at[len(moves)])
+        copy.start()
+        moves.append(copy)
+
+    for pair in (
+        (act_hbm, act_ref),
+        (near_hbm, near_ref),
+        (far_hbm, far_ref),
+        (grad_hbm, grad_ref),
+        (down_hbm, down_ref),
+    ):
+        move(*pair)
+    loads = len(moves)
+    for copy in moves[:3]:
+        copy.wait()
+    near, width = near_ref.shape[1], act_ref.shape[1]
+    unit = down_ref.shape[0]
+    some, lead = unit - first, near - 2 * first
+    block = 256
+
+    def tokens(i, _):
+        at = pl.ds(pl.multiple_of(i * block, block), block)
+        wide_ref[:, :near] = dot(act_ref[at, :], near_ref[...])
+        wide_ref[:, near:] = dot(act_ref[at, :], far_ref[...])
+
+        @pl.when(i == 0)
+        def _():
+            moves[3].wait()
+            moves[4].wait()
+
+        gate = wide_ref[:, 2 * first : 2 * first + some]
+        up = wide_ref[:, 2 * first + some :]
+        back = dot_nt(grad_ref[at, :], down_ref[first:, :])
+        sig = jax.nn.sigmoid(gate)
+        gate_silu = gate * sig
+        hidden_ref[at, :] = (gate_silu * up).astype(bf16)
+        wide_ref[:, : 2 * first] = pre_first_ref[at, :].astype(f32)
+        wide_ref[:, 2 * first : 2 * first + some] = back * up * (sig * (1.0 + gate * (1.0 - sig)))
+        wide_ref[:, 2 * first + some :] = back * gate_silu
+        pre_grad_ref[at, :] = wide_ref[...].astype(bf16)
+        return 0
+
+    lax.fori_loop(0, act_ref.shape[0] // block, tokens, 0)
+    move(pre_grad_ref, pre_grad_hbm)
+    move(hidden_ref, hidden_hbm)
+
+    groups = weights_ref.shape[0]
+    part = width // groups
+    rows = part // 8
+    tail = 64
+
+    def weights(g, _):
+        at = pl.ds(pl.multiple_of(g * part, part), part)
+        act, grad = act_ref[:, at], grad_ref[:, at]
+        full = dot_tn(act, pre_grad_ref[:, near:]).astype(bf16)
+        lead_ref[...] = dot_tn(act, pre_grad_ref[:, near - 128 : near])
+        side_ref[:, :lead] = lead_ref[:, 128 - lead :]
+        side_ref[:, lead : lead + some] = dot_tn(grad, hidden_ref[...])
+        side_ref[:, lead + some :] = rest_ref[at, :].astype(f32)
+        side = side_ref[...].astype(bf16)
+        for k in range(8):
+            for t in range(TILES):
+                source, skipped = (full, 0) if t * 128 < 2 * unit - near else (side, 2 * unit - near)
+                column = t * 128 - skipped
+                place = (k * TILES + t) * rows
+                weights_ref[g, place : place + rows, :] = source[
+                    k * rows : (k + 1) * rows, column : column + 128
+                ]
+        last = side_ref.shape[1] - tail
+        fold_ref[:, :tail] = side_ref[: part // 2, last:]
+        fold_ref[:, tail:] = side_ref[part // 2 :, last:]
+        weights_ref[g, 8 * TILES * rows :, :] = fold_ref[...].astype(bf16)
+        store(g).start()
+        return 0
+
+    def store(g):
+        return pltpu.make_async_copy(weights_ref.at[g], weights_hbm.at[g], store_sem.at[g])
+
+    lax.fori_loop(0, groups, weights, 0)
+    for g in range(groups):
+        store(g).wait()
+    for copy in moves[loads:]:
+        copy.wait()
+
+
+def feed(groups, act, grad, near, far, down, pre_first, rest):
+    (total, width), unit, first = act.shape, down.shape[0], pre_first.shape[1] // 2
+    side = near.shape[1] - 2 * first + unit - first + rest.shape[1]
+    vmem, hbm = pl.BlockSpec(memory_space=pltpu.VMEM), pl.BlockSpec(memory_space=pl.ANY)
+    outs = [
+        jax.ShapeDtypeStruct((groups, (8 * TILES + 4) * (width // (8 * groups)), 128), bf16),
+        jax.ShapeDtypeStruct((total, 2 * unit), bf16),
+        jax.ShapeDtypeStruct((total, unit - first), bf16),
+    ]
+    return pl.pallas_call(
+        functools.partial(feed_kernel, first),
+        out_shape=outs,
+        in_specs=[hbm] * 5 + [vmem] * 2,
+        out_specs=[hbm] * 3,
+        scratch_shapes=[pltpu.VMEM(v.shape, bf16) for v in (act, grad, near, far, down, *outs)]
+        + [
+            pltpu.VMEM((256, 2 * unit), f32),
+            pltpu.VMEM((width // groups, side), f32),
+            pltpu.VMEM((width // groups, 128), f32),
+            pltpu.VMEM((width // (2 * groups), 128), f32),
+            pltpu.SemaphoreType.DMA((7,)),
+            pltpu.SemaphoreType.DMA((groups,)),
+        ],
+        compiler_params=pltpu.CompilerParams(vmem_limit_bytes=60 * 2**20),
+    )(act, grad, near, far, down, pre_first, rest)
 
 
 def backward_scan(
@@ -284,8 +561,8 @@
 
 
 class Line:
-    def __init__(self, groups, own_ref, out_ref, send_sem, recv_sem, local_sem=None):
-        self.groups, self.own, self.out = groups, own_ref, out_ref
+    def __init__(self, groups, own_ref, out_ref, send_sem, recv_sem, local_sem=None, part=None):
+        self.groups, self.own, self.out, self.part = groups, own_ref, out_ref, part
         self.send_sem, self.recv_sem = send_sem, recv_sem
         self.g, self.p, self.c, self.x = (lax.axis_index(a) for a in ALL)
         self.kept = None
@@ -293,11 +570,14 @@
             self.kept = pltpu.make_async_copy(own_ref, out_ref.at[self.g], local_sem)
             self.kept.start()
 
+    def view(self, block):
+        return self.out.at[block] if self.part is None else self.out.at[block, self.part]
+
     def at_step(self, way, k):
         block = self.g - (k - 1) if way == 0 else self.g + (k - 1)
         return pltpu.make_async_remote_copy(
-            src_ref=self.own if k == 1 else self.out.at[block],
-            dst_ref=self.out.at[block],
+            src_ref=self.own if k == 1 else self.view(block),
+            dst_ref=self.view(block),
             send_sem=self.send_sem.at[way, k - 1],
             recv_sem=self.recv_sem.at[way, k - 1],
             device_id=(self.g + (1 if way == 0 else -1), self.p, self.c, self.x),
@@ -318,7 +598,7 @@
                 self.at_step(way, k).start()
 
     def arrived(self, way, k):
-        got = self.out.at[self.g - k if way == 0 else self.g + k]
+        got = self.view(self.g - k if way == 0 else self.g + k)
         pltpu.make_async_remote_copy(
             src_ref=got,
             dst_ref=got,
@@ -477,28 +757,14 @@
 
 def spread_kernel(
     groups,
-    mix_ref,
-    ffn_ref,
-    out_ref,
-    act_ref,
-    grad_ref,
-    mix_all,
-    out_all,
-    act_all,
-    grad_all,
-    ffn_all,
-    local_sem,
-    swap_send,
-    swap_recv,
-    mix_send,
-    mix_recv,
-    out_send,
-    out_recv,
-    act_send,
-    act_recv,
-    grad_send,
-    grad_recv,
+    splits,
+    *refs,
 ):
+    mixers, units = refs[:3], refs[3:5]
+    out_ref, act_ref, grad_ref, mix_all, out_all, act_all, grad_all, near_all, far_all = refs[5:14]
+    mix_ref, near_ref, far_ref, wide_ref = refs[14:18]
+    local_sem, swap_send, swap_recv = refs[18:21]
+    mix_send, mix_recv, out_send, out_recv, act_send, act_recv, grad_send, grad_recv = refs[21:]
     chips, core = places()
     here, other = chips[3], chips[2]
     g = here[0]
@@ -515,28 +781,67 @@
             for i in range(3)
         ]
 
-    mix_copies = swap(mix_ref, mix_all.at[g, own], 0)
-    locals_ = [
-        pltpu.make_async_copy(mix_ref.at[own], mix_all.at[g, own], local_sem.at[0]),
-        pltpu.make_async_copy(ffn_ref.at[own], ffn_all.at[own], local_sem.at[1]),
-        pltpu.make_async_copy(out_ref, out_all.at[g], local_sem.at[2]),
-    ]
-    for copy in locals_:
-        copy.start()
     out_line = Line(groups, out_ref, out_all, out_send, out_recv)
-    mix_line = Line(groups, mix_all.at[g], mix_all, mix_send, mix_recv)
     out_line.send(1)
     act = Plane(act_ref, act_all, local_sem.at[3], act_send, act_recv)
     grad = Plane(grad_ref, grad_all, local_sem.at[4], grad_send, grad_recv)
     act.start_own()
     grad.start_own()
     act.start(1)
+
+    def gather_columns(pieces, m, x):
+        place = 0
+        for ref, size, first, last in pieces:
+            for group in range(first // size, last // size):
+                start = ((group * 4 + m) * 2 + x) * size
+                wide_ref[:, place : place + size] = ref[:, start : start + size].astype(f32)
+                place += size
+        return place
+
+    def fill(make):
+        for x in (0, 1):
+
+            @pl.when(here[2] == x)
+            def _(x=x):
+                for m in range(4):
+                    make(m, x)
+
+    def mix_columns(m, x):
+        size = mixers[0].shape[1] // (8 * groups)
+        place = gather_columns([(ref, size, 0, size * groups) for ref in mixers], m, x)
+        mix_ref[m] = wide_ref[:, :place].astype(bf16)
+
+    def unit_columns(m, x):
+        size = units[0].shape[1] // (8 * groups)
+        place = gather_columns(
+            [(ref, size, first, last) for first, last in zip(splits[:-1], splits[1:]) for ref in units], m, x
+        )
+        near = near_ref.shape[2]
+        near_ref[m] = wide_ref[:, :near].astype(bf16)
+        far_ref[m] = wide_ref[:, near:place].astype(bf16)
+
+    fill(mix_columns)
+    mix_copies = swap(mix_ref, mix_all.at[g, own], 0)
+    locals_ = [
+        pltpu.make_async_copy(mix_ref.at[own], mix_all.at[g, own], local_sem.at[0]),
+        pltpu.make_async_copy(out_ref, out_all.at[g], local_sem.at[2]),
+    ]
+    for copy in locals_:
+        copy.start()
+    mix_line = Line(groups, mix_all.at[g], mix_all, mix_send, mix_recv)
     for copy in mix_copies:
         copy.wait()
     locals_[0].wait()
     mix_line.send(1)
     act.start(2)
-    ffn_copies = swap(ffn_ref, ffn_all.at[own], 3)
+    fill(unit_columns)
+    ffn_copies = swap(near_ref, near_all.at[own], 3) + swap(far_ref, far_all.at[own], 6)
+    for copy in (
+        pltpu.make_async_copy(near_ref.at[own], near_all.at[own], local_sem.at[1]),
+        pltpu.make_async_copy(far_ref.at[own], far_all.at[own], local_sem.at[5]),
+    ):
+        copy.start()
+        locals_.append(copy)
     out_line.step(1)
     act.hand_on(1)
     act.hand_on(2)
@@ -561,27 +866,35 @@
     grad.finish()
 
 
-def spread(groups, mix, ffn, out, act, grad, ident):
-    hbm = pl.BlockSpec(memory_space=pl.ANY)
-    dma = pltpu.SemaphoreType.DMA
+def spread(groups, splits, near, mixers, units, out, act, grad, ident):
+    vmem, hbm, dma = (
+        pl.BlockSpec(memory_space=pltpu.VMEM),
+        pl.BlockSpec(memory_space=pl.ANY),
+        pltpu.SemaphoreType.DMA,
+    )
+    rows = mixers[0].shape[0]
+    mix = (4, rows, 3 * mixers[0].shape[1] // 8)
+    sides = [(4, rows, near), (4, rows, 2 * splits[-1] - near)]
     return pl.pallas_call(
-        functools.partial(spread_kernel, groups),
+        functools.partial(spread_kernel, groups, splits),
         out_shape=[
-            jax.ShapeDtypeStruct((groups,) + mix.shape, bf16),
+            jax.ShapeDtypeStruct((groups,) + mix, bf16),
             jax.ShapeDtypeStruct((groups,) + out.shape, bf16),
             jax.ShapeDtypeStruct((8,) + act.shape, bf16),
             jax.ShapeDtypeStruct((8,) + grad.shape, bf16),
-            jax.ShapeDtypeStruct(ffn.shape, bf16),
-        ],
-        in_specs=[hbm] * 5,
-        out_specs=[hbm] * 5,
-        scratch_shapes=[dma((5,)), dma((6,)), dma((6,))]
+        ]
+        + [jax.ShapeDtypeStruct(shape, bf16) for shape in sides],
+        in_specs=[vmem] * 5 + [hbm] * 3,
+        out_specs=[hbm] * 6,
+        scratch_shapes=[pltpu.VMEM(shape, bf16) for shape in (mix, *sides)]
+        + [pltpu.VMEM((rows, 2 * splits[-1]), f32)]
+        + [dma((6,)), dma((9,)), dma((9,))]
         + [dma((2, groups - 1))] * 4
         + [dma((8,))] * 4,
         compiler_params=pltpu.CompilerParams(
-            collective_id=ident, has_side_effects=True, vmem_limit_bytes=48 * 2**20
+            collective_id=ident, has_side_effects=True, vmem_limit_bytes=62 * 2**20
         ),
-    )(mix, ffn, out, act, grad)
+    )(*mixers, *units, out, act, grad)
 
 
 def scatter_kernel(count, *refs):
@@ -636,7 +949,8 @@
         copy.wait_send()
 
 
-def collect_kernel(count, splits, size, *refs):
+def collect_kernel(streams, segments, size, rows, *refs):
+    count = len(streams)
     parts, outs = refs[:count], refs[count : count + 3]
     landing = refs[count + 3 : 2 * count + 3]
     wholes = refs[2 * count + 3 : 2 * count + 6]
@@ -646,62 +960,95 @@
     own = rank_at(chips[3], core)
     targets = [(chip, other) for j, chip, other in others if not (j == 3 and other is core)]
     greet([device_at(chip, other) for chip, other in targets])
+
+    def source(n, rank):
+        base, among, step = streams[n]
+        return parts[n].at[pl.ds(pl.multiple_of(base + lax.rem(rank, among) * step, step), step)]
+
     copies, locals_ = [], []
     for n in range(count):
         for i, (chip, other) in enumerate(targets):
             copies.append(
                 remote(
-                    parts[n].at[rank_at(chip, other)],
+                    source(n, rank_at(chip, other)),
                     landing[n].at[own],
                     send_sem.at[n, i],
                     recv_sem.at[n, i],
                     device_at(chip, other),
                 )
             )
-        local = pltpu.make_async_copy(parts[n].at[own], landing[n].at[own], local_sem.at[n])
+        local = pltpu.make_async_copy(source(n, own), landing[n].at[own], local_sem.at[n])
         local.start()
         locals_.append(local)
     for copy in locals_:
         copy.wait()
     for copy in copies:
         copy.wait_recv()
-    edges = [0]
-    for n in range(count):
-        edges.append(edges[-1] + landing[n].shape[2])
-    for first, last in zip(splits[:-1], splits[1:]):
-        for which in range(3):
+
+    def lay(which, place, n, k, low, high):
+        if n == 0:
+            wholes[which][:, place : place + high - low] = landing[0][k, :, low:high].astype(f32)
+            return
+        while low < high:
+            tile = low // 128
+            end = min(high, (tile + 1) * 128)
+            at = slice(place, place + end - low)
+            first, last = low - tile * 128, end - tile * 128
+            if tile < TILES:
+                wholes[which][:, at] = landing[1][k, tile * rows : (tile + 1) * rows, first:last].astype(f32)
+            else:
+                for side in (0, 1):
+
+                    @pl.when(chips[3][1] == side)
+                    def _(side=side, at=at, first=first, last=last):
+                        wholes[which][:, at] = landing[2][k, :, 64 * side + first : 64 * side + last].astype(f32)
+
+            place, low = place + end - low, end
+
+    for n, column, which, first, length in segments:
+        for group in range(first // size, -(-(first + length) // size)):
+            low, high = max(first, group * size), min(first + length, (group + 1) * size)
             for k in range(8):
-                for group in range(first // size, last // size):
-                    start = 3 * first + which * (last - first) + group * size - first
-                    place = (group * 8 + k) * size
-                    for n in range(count):
-                        low, high = max(start, edges[n]), min(start + size, edges[n + 1])
-                        if low < high:
-                            wholes[which][:, place + low - start : place + high - start] = landing[n][
-                                k, :, low - edges[n] : high - edges[n]
-                            ].astype(f32)
+                lay(which, group * 7 * size + k * size + low, n, k, column + low - first, column + high - first)
     for out, whole in zip(outs, wholes):
         out[...] = whole[...].astype(bf16)
     for copy in copies:
         copy.wait_send()
 
 
-def collect(parts, splits, size, ident):
-    count, rows, wide = len(parts), parts[0].shape[1], 8 * splits[-1]
+def collect(parts, streams, rows, segments, size, wide, ident):
+    count = len(parts)
     vmem = pl.BlockSpec(memory_space=pltpu.VMEM)
     dma = pltpu.SemaphoreType.DMA
     return pl.pallas_call(
-        functools.partial(collect_kernel, count, splits, size),
+        functools.partial(collect_kernel, streams, segments, size, rows),
         out_shape=[jax.ShapeDtypeStruct((rows, wide), bf16)] * 3,
         in_specs=[pl.BlockSpec(memory_space=pl.ANY)] * count,
         out_specs=[vmem] * 3,
-        scratch_shapes=[pltpu.VMEM(part.shape, bf16) for part in parts]
+        scratch_shapes=[
+            pltpu.VMEM((8, stream[2], part.shape[1]), bf16) for part, stream in zip(parts, streams)
+        ]
         + [pltpu.VMEM((rows, wide), f32)] * 3
         + [dma((count,)), dma((count, 7)), dma((count, 7))],
         compiler_params=pltpu.CompilerParams(
             collective_id=ident, has_side_effects=True, vmem_limit_bytes=48 * 2**20
         ),
     )(*parts)
+
+
+def close_kernel(sum_ref, w_ref, gain_ref, prob_ref, out_ref, sums_ref, bound_ref):
+    width = w_ref.shape[1]
+    out = sum_ref[:, :width].astype(f32)
+    out_ref[...] = out
+    gains = jnp.sum(out * w_ref[...].astype(f32), axis=1, keepdims=True)
+    side = sum_ref[:, width:].astype(f32)
+    lane = lax.broadcasted_iota(jnp.int32, side.shape, 1)
+    turned = jnp.transpose(jnp.where(lane == 2, gains, side))
+    sums_ref[...] = turned[2:3, :] / gain_ref[...]
+    layer = lax.broadcasted_iota(jnp.int32, prob_ref.shape, 0)
+    probs = prob_ref[...]
+    grads = jnp.where((layer >= 1) & (layer <= LAYER_AT), turned[0:1, :] + turned[1:2, :], 0.0)
+    bound_ref[...] = probs * (grads - jnp.sum(probs * grads, axis=0, keepdims=True))
 
 
 def gather_plane(v, ident):
@@ -788,11 +1135,7 @@
     fe = units // (groups * ranks)
     chan, unit = ce * groups, fe * groups
     splits = (0, unit // QUARTERS, unit)
-
-    def columns(w, size):
-        w = w.reshape(w.shape[0], groups, members, copies, size)
-        w = lax.dynamic_index_in_dim(w, x, axis=3, keepdims=False)
-        return jnp.moveaxis(w, 2, 0).reshape(members, w.shape[0], groups * size)
+    near = -(-2 * splits[1] // 128) * 128
 
     def half_rows(w):
         half = w.shape[0] // copies
@@ -839,18 +1182,12 @@
     seq_total = doc_ids.shape[0] // SEQ_LEN
     grad_z = cotangent.astype(f32) * (seq_total / (domain_count * per_token))[:, None]
 
-    ffn_own = jnp.concatenate(
-        [
-            columns(w, fe)[:, :, first:last]
-            for first, last in zip(splits[:-1], splits[1:])
-            for w in (ffn_gate, ffn_up)
-        ],
-        axis=2,
-    )
-    mix_w, out_ext, act_one, grad_m, ffn = spread(
+    mix_w, out_ext, act_one, grad_m, *ffn = spread(
         groups,
-        jnp.concatenate([columns(w_in, ce), columns(w_forget, ce), columns(w_gate_out, ce)], axis=2),
-        ffn_own,
+        splits,
+        near,
+        (w_in, w_forget, w_gate_out),
+        (ffn_gate, ffn_up),
         out_own,
         act_one_own,
         grad_z.astype(bf16),
@@ -858,23 +1195,38 @@
     )
     mix_w = mix_w.reshape(width, 3 * chan)
     down_w = gather_rows(half_rows(ffn_down))
-    ffn, down_w = lax.optimization_barrier((ffn.reshape(-1, 2 * unit), down_w))
-    ffn_all = gather_rows(ffn)
     act_one, grad_m = act_one.reshape(plane_rows, width), grad_m.reshape(plane_rows, width)
     out_ext = out_ext.reshape(chan, -1)
     out_w = out_ext[:, :width]
-    lower = jnp.sum(out_ext[:, width : width + 3].astype(f32), axis=1).reshape(1, chan)
-
-    proj, states, residual, state_scale, act_two = mixer(
+
+    (
+        proj,
+        states,
+        pre_grad,
+        grads_kept,
+        ffn_near,
+        residual,
+        hidden,
+        grads_rest,
+        act_two,
+        ffn_far,
+        state_scale,
+        lower,
+    ) = mixer(
+        groups,
         chan,
         act_one,
         mix_w,
         out_ext,
         keep,
-        lower,
         gain,
         tokens,
         ffn_gain.reshape(1, width),
+        grad_m,
+        down_w,
+        splits[1],
+        ffn[0].reshape(-1, near),
+        ffn[1].reshape(-1, 2 * unit - near),
         1,
     )
     act_two = act_two.reshape(plane_rows, width)
@@ -885,35 +1237,16 @@
     def scatter_rows(v):
         return lax.psum_scatter(v, "g", scatter_dimension=0, tiled=True)
 
-    backs = [dot_nt(grad_m, down_w[first:last]) for first, last in zip(splits[:-1], splits[1:])]
-    backs, ffn_all = lax.optimization_barrier((backs, ffn_all))
-    grads, pre_grads, hiddens, ffn_sums = [], [], [], []
-    for first, last in zip(splits[:-1], splits[1:]):
-        some = last - first
-        pre = dot(act_two, ffn_all[:, 2 * first : 2 * last])
-        gate_ffn, up_ffn = pre[:, :some], pre[:, some:]
-        sig = jax.nn.sigmoid(gate_ffn)
-        gate_silu = gate_ffn * sig
-        hidden = (gate_silu * up_ffn).astype(bf16)
-        back = backs[first > 0]
-        grad_gate = (back * up_ffn * (sig * (1.0 + gate_ffn * (1.0 - sig)))).astype(bf16)
-        grad_up = (back * gate_silu).astype(bf16)
-        pre_grads.append(jnp.concatenate([grad_gate, grad_up], axis=1))
-        hiddens.append(hidden)
-        grads.append(
-            jnp.concatenate(
-                [dot_tn(act_two, pre_grads[-1]).astype(bf16), dot_tn(grad_m, hidden).astype(bf16)], axis=1
-            )
-        )
-        if first == 0:
-            kept = grads[0].shape[1] // 128 * 128
-            ffn_sums.append(scatter_rows(grads[0][:, :kept]))
-            grads[0], act_two = lax.optimization_barrier((grads[0][:, kept:], act_two))
-    far_grads = jnp.concatenate(grads, axis=1)
-    pre_grads, hiddens, far_grads = lax.optimization_barrier((pre_grads, hiddens, far_grads))
-    ffn_sums.append(scatter_rows(far_grads))
-    down_part = dot(jnp.concatenate(hiddens, axis=1), down_w).astype(bf16)
-    back_part = dot_nt(jnp.concatenate(pre_grads, axis=1), ffn_all).astype(bf16)
+    ffn_sums = [scatter_rows(grads_kept)]
+    ffn_near, ffn_far = ffn_near.reshape(width, near), ffn_far.reshape(width, -1)
+    far_grads, pre_grad, hidden_far = feed(
+        groups, act_two, grad_m, ffn_near, ffn_far, down_w, pre_grad, grads_rest
+    )
+    ffn_sums.append(scatter_rows(far_grads.reshape(-1, 128)))
+    back_part = dot_nt(pre_grad[:, :near], ffn_near) + dot_nt(pre_grad[:, near:], ffn_far)
+    back_part = back_part.astype(bf16)
+    down_part = dot(hidden, down_w[: splits[1]]) + dot(hidden_far, down_w[splits[1] :])
+    down_part = down_part.astype(bf16)
 
     (back_term,) = scatter_plane([back_part], 3)
     scaled_two = back_term * ffn_gain
@@ -952,26 +1285,34 @@
         gain,
     )
     in_part = dot_nt(grad_proj, mix_w).astype(bf16)
-    mix_grads = dot_tn(act_one, grad_proj).astype(bf16).reshape(groups, -1, 3 * chan)
+    down_part, grad_proj = lax.optimization_barrier((down_part, grad_proj))
+    (down_term,) = scatter_plane([down_part], 5)
+    mix_grads = dot_tn(act_one, grad_proj).astype(bf16)
     top, rest = split_hi_lo(sums.reshape(chan, 1))
     out_grads = jnp.concatenate(
-        [dot_tn(mixed_out, grad_branch).astype(bf16), top, rest, jnp.zeros((chan, 3 * chan - 2), bf16)],
-        axis=1,
-    )
-    folds = out_grads.shape[1] // (3 * chan)
-    out_grads = out_grads[:, : folds * 3 * chan].reshape(groups, ce, folds, 3 * chan)
-    out_grads = jnp.moveaxis(out_grads, 2, 1).reshape(groups, folds * ce, 3 * chan)
-    late_grads = jnp.concatenate([mix_grads, out_grads], axis=1).reshape(-1, 3 * chan)
-    late_grads, ffn_sums, in_part, down_part = lax.optimization_barrier(
-        (late_grads, ffn_sums, in_part, down_part)
-    )
-    late_sum = scatter_rows(late_grads)
-    mix_sum = late_sum[: width // groups]
-    out_sum = jnp.moveaxis(late_sum[width // groups :].reshape(folds, ce, 3 * chan), 1, 0)
-    out_sum = out_sum.reshape(ce, -1).astype(f32)
-    summed_wout = out_sum[:, :width]
-    grad_lower = out_sum[:, width] + out_sum[:, width + 1]
-    grad_act, down_term = scatter_plane([in_part, down_part], 6)
+        [dot_tn(mixed_out, grad_branch).astype(bf16), top, rest, jnp.zeros((chan, 126), bf16)], axis=1
+    )
+    mix_grads, ffn_sums, in_part, out_grads, down_term = lax.optimization_barrier(
+        (mix_grads, ffn_sums, in_part, out_grads, down_term)
+    )
+    mix_sum = scatter_rows(mix_grads)
+    out_grads, mix_sum = lax.optimization_barrier((out_grads, mix_sum))
+    out_sum = scatter_rows(out_grads)
+    first_channel = (g * ranks + rank) * ce
+    summed_wout, summed_outg, grad_bounds = kernel_call(
+        close_kernel,
+        [
+            jax.ShapeDtypeStruct((ce, width), f32),
+            jax.ShapeDtypeStruct((1, ce), f32),
+            jax.ShapeDtypeStruct(bound_logits.shape, f32),
+        ],
+        out_sum,
+        half_rows(w_out),
+        lax.dynamic_slice_in_dim(out_gain, first_channel, ce, axis=0).reshape(1, ce),
+        layer_probs,
+    )
+    summed_outg = summed_outg.reshape(ce)
+    (grad_act,) = scatter_plane([in_part], 6)
     output_rows = (residual + down_term).astype(bf16)
 
     scaled_one = grad_act * norm_gain
@@ -979,13 +1320,36 @@
         scaled_one - normed_one * jnp.mean(scaled_one * normed_one, axis=-1, keepdims=True)
     )
 
+    first, lead, kept = splits[1], near - 2 * splits[1], grads_kept.shape[1]
+    some, far = unit - first, 2 * unit - near
+    segments = (
+        (0, 0, 0, 0, first),
+        (0, first, 1, 0, first),
+        (0, 2 * first, 2, 0, kept - 2 * first),
+        (1, 0, 0, first + lead, some - lead),
+        (1, some - lead, 1, first, some),
+        (1, far, 0, first, lead),
+        (1, far + lead, 2, first, some),
+        (1, far + lead + some, 2, kept - 2 * first, 3 * first - kept),
+    )
     summed_fgate, summed_fup, fdown = [
         v.astype(f32)
-        for v in collect([v.reshape(ranks, -1, v.shape[1]) for v in ffn_sums], splits, fe, 7)
+        for v in collect(
+            [ffn_sums[0], ffn_sums[1], ffn_sums[1]],
+            [(0, 8, ce), (0, 8, TILES * ce), (8 * TILES * ce, 4, ce)],
+            ce,
+            segments,
+            fe,
+            units,
+            7,
+        )
     ]
     summed_fdown = fdown.T
     summed_win, summed_wforget, summed_wgate = [
-        v.astype(f32) for v in collect([mix_sum.reshape(ranks, -1, 3 * chan)], (0, chan), ce, 8)
+        v.astype(f32)
+        for v in collect(
+            [mix_sum], [(0, 8, ce)], ce, [(0, n * chan, n, 0, chan) for n in range(3)], ce, width, 8
+        )
     ]
     first = (g * ranks + rank) * ce
 
@@ -996,12 +1360,7 @@
     summed_norm = own_gain(
         norm_gain, ((summed_win, w_in), (summed_wforget, w_forget), (summed_wgate, w_gate_out))
     )
-    summed_outg = own_gain(out_gain, ((summed_wout, w_out),))
     summed_ffng = own_gain(ffn_gain, ((summed_fgate, ffn_gate), (summed_fup, ffn_up)))
-    grad_probs = layer_pick * grad_lower[None, :]
-    grad_bounds = layer_probs * (
-        grad_probs - jnp.sum(layer_probs * grad_probs, axis=0, keepdims=True)
-    )
     return (
         output_rows,
         grad_tokens,

time: 536 us -> 503 us (0.938)
  Pallas kernels: 327 us -> 397 us
  matrix products: 67.1 us -> 36.7 us
  waiting for transfers between devices: 39.7 us -> 13.1 us
  local copies, waits for them, and re-layouts: 44.2 us -> 21 us
  other arithmetic: 37.1 us -> 19.2 us
    pallas_call x4 -> x5, Pallas kernels: 226 us -> 294 us  [the longest x1 121 us: spread(): pl.pallas_call(functools.partial(spread_kernel, groups, splits), out_shap...]
    all_gather x2 -> x1, waiting for transfers between devices: 25.7 us -> 0.02 us  [gather_rows(): return lax.all_gather(v, 'g', axis=0, tiled=True)]
    concatenate x6 -> x0, other arithmetic: 16.5 us -> none  [the longest x1 8.94 us: body(): far_grads = jnp.concatenate(grads, axis=1)]
    dot_general x6 -> x2, matrix products: 21.1 us -> 7.27 us  [dot_tn(): lax.dot_general(a, b, (((0,), (0,)), ((), ())), preferred_element_type=f32)]
    dot_general x3 -> x2, matrix products: 21.2 us -> 8.02 us  [dot(): return jnp.dot(a, b, preferred_element_type=f32)]
    unnamed x134 -> x85, local copies, waits for them, and re-layouts: 17.4 us -> 9.81 us
    reshape x4 -> x2, local copies, waits for them, and re-layouts: 6.47 us -> 1.01 us  [the longest x1 0.87 us: body(): lax.dynamic_slice_in_dim(out_gain, first_channel, ce, axis=0).reshape(1, ce)]
    dot_general x5 -> x4, matrix products: 24.8 us -> 21.4 us  [dot_nt(): lax.dot_general(a, b, (((1,), (1,)), ((), ())), preferred_element_type=f32)]
  transfers between devices with their start and end apart: 5 -> 5, of which waited for: 2 -> 3; matrix products, arithmetic and copies ran while one was open for 22% -> 13% of each run, Pallas kernels for 59% -> 59%
where the time goes in v5:
time: 503 us; the launch traced here: 502 us
  Pallas kernels  397 us (79%)
  matrix products  36.7 us (7%)
  local copies, waits for them, and re-layouts  21 us (4%)
  other arithmetic  19.2 us (4%)
  between operations  14.5 us (3%)
  waiting for transfers between devices  13.1 us (3%)
    pallas_call x1, Pallas kernels, spread(): pl.pallas_call(functools.partial(spread_kernel, groups, splits), out_shap...  121 us
    pallas_call x1, Pallas kernels, mixer(): pl.pallas_call(functools.partial(mixer_kernel, groups, chan), out_shape=m...  98.5 us
    pallas_call x3, Pallas kernels, scatter_plane(): pl.pallas_call(functools.partial(scatter_kernel, count), out_shape=[jax.S...  68.1 us
    pallas_call x2, Pallas kernels, collect(): pl.pallas_call(functools.partial(collect_kernel, streams, segments, size,...  43.4 us
    pallas_call x1, Pallas kernels, feed(): pl.pallas_call(functools.partial(feed_kernel, first), out_shape=outs, in_...  31.7 us
    pallas_call x1, Pallas kernels, gather_plane(): pl.pallas_call(gather_kernel, out_shape=jax.ShapeDtypeStruct((8,) + v.sha...  25.2 us
    dot_general x4, matrix products, dot_nt(): lax.dot_general(a, b, (((1,), (1,)), ((), ())), preferred_element_type=f32)  21.4 us
    reduce_scatter x4, waiting for transfers between devices, scatter_rows(): return lax.psum_scatter(v, 'g', scatter_dimension=0, tiled=True)  13 us
  transfers between devices with their start and end apart: 5, of which 3 were waited for; matrix products, arithmetic and copies ran while one was open for 13% of the time, Pallas kernels for 59%

profile of v5, /device:TPU:0, one launch (start us, length us, event | category | flops | bytes accessed | tf_op | source)
XLA Modules:
  0.0 502.3 jit_solution(12325182676006418172)
XLA Ops:
  20.4 120.7 %shard_map.255 = (bf16[4,4,128,768]{3,2,1,0:T(8,128)(2,1)}, bf16[4,64,2176]{2,1,0:T(8,128)(2,1)}, bf16[8,128,2048]{2,1,0:T(8,128)(2,1)}, bf16[8,128,2048]{2,1,0:...) custom-call(bf16[128,2048]{1,0:T(8,128)(2,1)} %refs_0_.1, bf16[128,2048]{1,0:T(8,128)(2,1)} %refs_1_.1, ...), custom_call_target="tpu_custom_call" | custom-call | tf_op jit(solution)/shard_map/pallas_call | solution.py:878
  141.2 98.5 %shard_map.256 = (f32[1024,768]{1,0:T(8,128)}, f32[1024,256]{1,0:T(8,128)}, bf16[1024,352]{1,0:T(8,128)(2,1)}, bf16[2048,512]{1,0:T(8,128)(2,1)}, bf16[4,512,384...) custom-call(bf16[1024,2048]{1,0:T(8,128)(2,1)} %bitcast.59, ...), custom_call_target="tpu_custom_call" | custom-call | tf_op jit(solution)/shard_map/pallas_call | solution.py:283
  240.0 31.7 %shard_map.257 = (bf16[4,6400,128]{2,1,0:T(8,128)(2,1)}, bf16[1024,1408]{1,0:T(8,128)(2,1)}, bf16[1024,528]{1,0:T(8,128)(2,1)}) custom-call(bf16[1024,2048]{1,0:T(8,128)(2,1)} %bitcast.63, bf16[1024,2048]{1,0:T(8,128)(2,1)} %bitcast.55, bf16[2048,384]{1,0:T(8,128)(2,1)} %bitcast.57, bf16[2048,1024]{1,0:T(8,128)(2,1)} %bitcast.61, ...), custom_call_target="tpu_custom_call" | custom-call | tf_op jit(solution)/shard_map/pallas_call | solution.py:449
  271.7 7.1 %fusion.9 = f32[1024,2048]{1,0:T(8,128)S(1)} fusion(bf16[2048,1024]{1,0:T(8,128)(2,1)} %bitcast.62, bf16[1024,1408]{1,0:T(8,128)(2,1)} %get-tuple-element.72), kind=kOutput, calls=%fused_computation.11 | convolution fusion | flops 4294967296 | bytes 14680064 | tf_op jit(solution)/shard_map/dot_general | solution.py:1100
  278.9 3.5 add_convert_fusion
  282.4 21.9 %shard_map.258 = f32[128,2048]{1,0:T(8,128)S(1)} custom-call(bf16[8,128,2048]{2,1,0:T(8,128)(2,1)S(1)} %bitcast.45), custom_call_target="tpu_custom_call" | custom-call | tf_op jit(solution)/shard_map/pallas_call | solution.py:1075
  307.8 25.2 %shard_map.259 = bf16[8,128,2176]{2,1,0:T(8,128)(2,1)S(1)} custom-call(bf16[128,2176]{1,0:T(8,128)(2,1)S(1)} %concatenate.17.own_ref), custom_call_target="tpu_custom_call" | custom-call | tf_op jit(solution)/shard_map/pallas_call | solution.py:1056
  333.0 2.1 copy-done.3
  335.7 3.7 fusion.2.do_ref
  339.4 9.0 %shard_map.260 = (bf16[1024,768]{1,0:T(8,128)(2,1)S(1)}, bf16[1024,256]{1,0:T(8,128)(2,1)S(1)}, f32[1,256]{1,0:T(1,128)S(1)}) custom-call(f32[1024,768]{1,0:T(8,128)} %get-tuple-element.70.proj_ref, f32[1024,256]{1,0:T(8,128)S(1)} %copy-done.8, f32[1024,256]{1,0:T(8,128)S(1)} %fusion.2.do_ref, f32[1024,2]{1,0:T(8,128)S(1)} %copy.69.info_ref, ...), custom_call_target="tpu_custom_call" | custom-call | tf_op jit(solution)/shard_map/pallas_call | solution.py:521
  350.0 5.5 %fusion.7 = f32[1024,2048]{1,0:T(8,128)S(1)} fusion(bf16[1024,528]{1,0:T(8,128)(2,1)} %get-tuple-element.69, bf16[704,2048]{1,0:T(8,128)(2,1)} %all-gather.2.cloned.1.call-done.down_hbm), kind=kOutput, calls=%fused_computation.9 | convolution fusion | flops 2214592512 | bytes 11862016 | tf_op jit(solution)/shard_map/dot_general | solution.py:1096
  355.6 2.5 add_convert_fusion.1
  358.1 23.4 %shard_map.261 = f32[128,2048]{1,0:T(8,128)S(1)} custom-call(bf16[8,128,2048]{2,1,0:T(8,128)(2,1)S(1)} %bitcast.46), custom_call_target="tpu_custom_call" | custom-call | tf_op jit(solution)/shard_map/pallas_call | solution.py:1075
  381.6 2.2 fusion.4
  383.8 3.3 concatenate.19
  387.1 7.1 %convolution_convert_fusion = bf16[1024,2048]{1,0:T(8,128)(2,1)} fusion(bf16[1024,768]{1,0:T(8,128)(2,1)S(1)} %copy-done.17, bf16[2048,768]{1,0:T(8,128)(2,1)} %bitcast.65), kind=kOutput, calls=%fused_computation.2 | convolution fusion | flops 3223322624 | bytes 8912896 | tf_op jit(solution)/shard_map/dot_general | solution.py:1100
  394.2 5.0 %convolution_convert_fusion.1 = bf16[2048,768]{1,0:T(8,128)(2,1)} fusion(bf16[1024,2048]{1,0:T(8,128)(2,1)S(1)} %bitcast.60, bf16[1024,768]{1,0:T(8,128)(2,1)S(1)} %copy-done.17), kind=kOutput, calls=%fused_computation.7 | convolution fusion | flops 3222798336 | bytes 8912896 | tf_op jit(solution)/shard_map/dot_general | solution.py:1104
  401.4 2.2 copy-done.5
  403.6 22.8 %shard_map.262 = f32[128,2048]{1,0:T(8,128)S(1)} custom-call(bf16[8,128,2048]{2,1,0:T(8,128)(2,1)S(1)} %bitcast.52), custom_call_target="tpu_custom_call" | custom-call | tf_op jit(solution)/shard_map/pallas_call | solution.py:1075
  427.5 30.4 %shard_map.265 = (bf16[64,5632]{1,0:T(8,128)(2,1)S(1)}, bf16[64,5632]{1,0:T(8,128)(2,1)S(1)}, bf16[64,5632]{1,0:T(8,128)(2,1)S(1)}) custom-call(bf16[512,512]{1,0:T(8,128)(2,1)S(1)} %copy-done.12, bf16[6400,128]{1,0:T(8,128)(2,1)S(1)} %copy-done.2, bf16[6400,128]{1,0:T(8,128)(2,1)S(1)} %copy-done.2), custom_call_target="tpu_custom_call" | custom-call | tf_op jit(solution)/shard_map/pallas_call | solution.py:1023
  458.2 2.1 multiply_reduce_fusion
  465.3 13.0 %shard_map.263 = (bf16[64,2048]{1,0:T(8,128)(2,1)S(1)}, bf16[64,2048]{1,0:T(8,128)(2,1)S(1)}, bf16[64,2048]{1,0:T(8,128)(2,1)S(1)}) custom-call(bf16[512,768]{1,0:T(8,128)(2,1)S(1)} %copy-done.9), custom_call_target="tpu_custom_call" | custom-call | tf_op jit(solution)/shard_map/pallas_call | solution.py:1023
  480.2 2.2 multiply_reduce_fusion.4
  483.1 10.9 %reduce-scatter.11.cloned.1.call-done.sum_ref = bf16[64,2176]{1,0:T(8,128)(2,1)} async-done(((bf16[256,2176]{1,0:T(8,128)(2,1)}), bf16[64,2176]{1,0:T(8,128)(2,1)}) %reduce-scatter.11.cloned.1.call-update) | async-done | bytes 278544 | tf_op jit(solution)/shard_map/reduce_scatter | solution.py:1238
  (158 shorter events, 31.8 us)
Async XLA Ops:
  7.2 10.1 %copy-start.34 = (bf16[128,2048]{1,0:T(8,128)(2,1)S(1)}, bf16[128,2048]{1,0:T(8,128)(2,1)}, u32[]{:S(2)}) copy-start(bf16[128,2048]{1,0:T(8,128)(2,1)} %param.24) | copy-start | bytes 1572868
  7.2 11.0 %copy-start.38 = (s32[4]{0:T(128)S(1)}, s32[4]{0:T(128)}, u32[]{:S(2)}) copy-start(s32[4]{0:T(128)} %param.20) | copy-start | bytes 52
  7.2 11.0 %copy-start.39 = (s32[128]{0:T(128)S(1)}, s32[128]{0:T(128)}, u32[]{:S(2)}) copy-start(s32[128]{0:T(128)} %param.18) | copy-start | bytes 1540
  7.2 11.1 %copy-start.20 = (bf16[128,2048]{1,0:T(8,128)(2,1)S(1)}, bf16[128,2048]{1,0:T(8,128)(2,1)}, u32[]{:S(2)}) copy-start(bf16[128,2048]{1,0:T(8,128)(2,1)} %token_hbm.1) | copy-start | bytes 1572868
  7.2 11.3 %copy-start.30 = (bf16[128,2048]{1,0:T(8,128)(2,1)S(1)}, bf16[128,2048]{1,0:T(8,128)(2,1)}, u32[]{:S(2)}) copy-start(bf16[128,2048]{1,0:T(8,128)(2,1)} %param.17) | copy-start | bytes 1572868
  7.3 133.9 %all-gather.2.cloned.1.call-start = ((), (), s32[]{:S(2)}) async-start(), calls=%async_computation.4 | async-start | bytes 3604480 | tf_op jit(solution)/shard_map/all_gather | solution.py:1145
  8.6 10.9 %copy-start.36 = (f32[2048]{0:T(1024)S(1)}, f32[2048]{0:T(1024)}, u32[]{:S(2)}) copy-start(f32[2048]{0:T(1024)} %param.28) | copy-start | bytes 24580
  9.5 389.7 %reduce-scatter.5.cloned.1.call-start = ((), (), s32[]{:S(2)}) async-start(), calls=%async_computation.5 | async-start | bytes 2621440 | tf_op jit(solution)/shard_map/reduce_scatter | solution.py:1238
  239.7 160.7 %reduce-scatter.7.cloned.1.call-start = ((), (), s32[]{:S(2)}) async-start(), calls=%async_computation.6 | async-start | bytes 8192000 | tf_op jit(solution)/shard_map/reduce_scatter | solution.py:1238
  271.7 191.8 %reduce-scatter.9.cloned.1.call-start = ((), (), s32[]{:S(2)}) async-start(), calls=%async_computation.7 | async-start | bytes 3932160 | tf_op jit(solution)/shard_map/reduce_scatter | solution.py:1238
  271.7 7.1 %copy-start.25 = (bf16[4,512,384]{2,1,0:T(8,128)(2,1)S(1)}, bf16[4,512,384]{2,1,0:T(8,128)(2,1)}, u32[]{:S(2)}) copy-start(bf16[4,512,384]{2,1,0:T(8,128)(2,1)} %get-tuple-element.65) | copy-start | bytes 4718596
  282.4 22.0 %copy-start.23 = (f32[128,2048]{1,0:T(8,128)S(1)}, f32[128,2048]{1,0:T(8,128)}, u32[]{:S(2)}) copy-start(f32[128,2048]{1,0:T(8,128)} %get-tuple-element.62) | copy-start | bytes 3145732
  282.4 22.1 %copy-start.35 = (f32[2048]{0:T(1024)S(1)}, f32[2048]{0:T(1024)}, u32[]{:S(2)}) copy-start(f32[2048]{0:T(1024)} %param.30) | copy-start | bytes 24580
  307.8 27.9 %copy-start.32 = (bf16[4,64,2176]{2,1,0:T(8,128)(2,1)S(1)}, bf16[4,64,2176]{2,1,0:T(8,128)(2,1)}, u32[]{:S(2)}) copy-start(bf16[4,64,2176]{2,1,0:T(8,128)(2,1)} %get-tuple-element.61) | copy-start | bytes 3342340
  355.5 26.0 %slice-start = ((s8[4456448]{0:T(1024)(128)(4,1)}), s8[4194304]{0:T(1024)(128)(4,1)S(1)}, s32[]{:S(2)}) async-start(s8[4456448]{0:T(1024)(128)(4,1)} %bitcast.49), calls=%async_computation.9 | async-start | bytes 8388608
  355.6 26.0 %slice-start.1 = ((s8[4456448]{0:T(1024)(128)(4,1)}), s8[262144]{0:T(1024)(128)(4,1)S(1)}, s32[]{:S(2)}) async-start(s8[4456448]{0:T(1024)(128)(4,1)} %bitcast.49), calls=%async_computation.10 | async-start | bytes 524288
  358.1 23.4 %copy-start.19 = (bf16[1024,256]{1,0:T(8,128)(2,1)S(1)}, bf16[1024,256]{1,0:T(8,128)(2,1)}, u32[]{:S(2)}) copy-start(bf16[1024,256]{1,0:T(8,128)(2,1)} %copy-done.18) | copy-start | bytes 1572868
  387.1 7.1 %copy-start.26 = (bf16[8,128,2048]{2,1,0:T(8,128)(2,1)S(1)}, bf16[8,128,2048]{2,1,0:T(8,128)(2,1)}, u32[]{:S(2)}) copy-start(bf16[8,128,2048]{2,1,0:T(8,128)(2,1)} %get-tuple-element.56) | copy-start | bytes 12582916
  400.5 25.9 %copy-start.2 = (bf16[6400,128]{1,0:T(8,128)(2,1)S(1)}, bf16[6400,128]{1,0:T(8,128)(2,1)}, u32[]{:S(2)}) copy-start(bf16[6400,128]{1,0:T(8,128)(2,1)} %reduce-scatter.7.cloned.1.call-done.refs_1_.refs_2_) | copy-start | bytes 4915204
  400.5 93.5 %reduce-scatter.11.cloned.1.call-start = ((), (), s32[]{:S(2)}) async-start(), calls=%async_computation.8 | async-start | bytes 1392640 | tf_op jit(solution)/shard_map/reduce_scatter | solution.py:1238
  427.5 30.4 %copy-start.22 = (bf16[128,2048]{1,0:T(8,128)(2,1)S(1)}, bf16[128,2048]{1,0:T(8,128)(2,1)}, u32[]{:S(2)}) copy-start(bf16[128,2048]{1,0:T(8,128)(2,1)} %token_hbm.1) | copy-start | bytes 1572868
  427.5 30.7 %copy-start.28 = (bf16[128,5632]{1,0:T(8,128)(2,1)S(1)}, bf16[128,5632]{1,0:T(8,128)(2,1)}, u32[]{:S(2)}) copy-start(bf16[128,5632]{1,0:T(8,128)(2,1)} %refs_3_.1) | copy-start | bytes 4325380
  427.5 30.7 %copy-start.29 = (bf16[128,5632]{1,0:T(8,128)(2,1)S(1)}, bf16[128,5632]{1,0:T(8,128)(2,1)}, u32[]{:S(2)}) copy-start(bf16[128,5632]{1,0:T(8,128)(2,1)} %refs_4_.1) | copy-start | bytes 4325380
  464.1 31.7 %copy-start.1 = (bf16[352,2048]{1,0:T(8,128)(2,1)S(1)}, bf16[352,2048]{1,0:T(8,128)(2,1)}, u32[]{:S(2)}) copy-start(bf16[352,2048]{1,0:T(8,128)(2,1)} %param.27) | copy-start | bytes 4325380
  (23 other events, 62.4 us)
Sparse Core Ops, SparseCore 0:
  10.2 80.7 all-gather.1
  239.8 43.7 reduce-scatter.4
  286.1 114.3 reduce-scatter.6
  402.7 60.7 reduce-scatter.8
  465.8 28.1 reduce-scatter.10

commit v6 on v5

--- a/solution.py
+++ b/solution.py
@@ -1194,7 +1194,8 @@
         0,
     )
     mix_w = mix_w.reshape(width, 3 * chan)
-    down_w = gather_rows(half_rows(ffn_down))
+    down_half = ffn_down.shape[0] // copies
+    down_w = gather_rows(jnp.where(x == 0, ffn_down[:down_half], ffn_down[down_half:]))
     act_one, grad_m = act_one.reshape(plane_rows, width), grad_m.reshape(plane_rows, width)
     out_ext = out_ext.reshape(chan, -1)
     out_w = out_ext[:, :width]

time: 503 us -> 503 us (level)
  transfers between devices with their start and end apart: 5 -> 5, of which waited for: 3 -> 3; matrix products, arithmetic and copies ran while one was open for 13% -> 12% of each run, Pallas kernels for 59% -> 60%
where the time goes in v6:
time: 503 us; the launch traced here: 502 us
  Pallas kernels  402 us (80%)
  matrix products  36.3 us (7%)
  other arithmetic  18.5 us (4%)
  local copies, waits for them, and re-layouts  17.1 us (3%)
  between operations  14.6 us (3%)
  waiting for transfers between devices  13.3 us (3%)
    pallas_call x1, Pallas kernels, spread(): pl.pallas_call(functools.partial(spread_kernel, groups, splits), out_shap...  125 us
    pallas_call x1, Pallas kernels, mixer(): pl.pallas_call(functools.partial(mixer_kernel, groups, chan), out_shape=m...  98.5 us
    pallas_call x3, Pallas kernels, scatter_plane(): pl.pallas_call(functools.partial(scatter_kernel, count), out_shape=[jax.S...  68.1 us
    pallas_call x2, Pallas kernels, collect(): pl.pallas_call(functools.partial(collect_kernel, streams, segments, size,...  43.4 us
    pallas_call x1, Pallas kernels, feed(): pl.pallas_call(functools.partial(feed_kernel, first), out_shape=outs, in_...  32.2 us
    pallas_call x1, Pallas kernels, gather_plane(): pl.pallas_call(gather_kernel, out_shape=jax.ShapeDtypeStruct((8,) + v.sha...  25.2 us
    dot_general x4, matrix products, dot_nt(): lax.dot_general(a, b, (((1,), (1,)), ((), ())), preferred_element_type=f32)  21.4 us
    reduce_scatter x4, waiting for transfers between devices, scatter_rows(): return lax.psum_scatter(v, 'g', scatter_dimension=0, tiled=True)  13.2 us
  transfers between devices with their start and end apart: 5, of which 3 were waited for; matrix products, arithmetic and copies ran while one was open for 12% of the time, Pallas kernels for 60%

profile of v6, /device:TPU:0, one launch (start us, length us, event | category | flops | bytes accessed | tf_op | source)
XLA Modules:
  0.0 502.3 jit_solution(13863424065726494089)
XLA Ops:
  7.3 2.4 slice_select_fusion
  16.5 124.7 %shard_map.255 = (bf16[4,4,128,768]{3,2,1,0:T(8,128)(2,1)}, bf16[4,64,2176]{2,1,0:T(8,128)(2,1)}, bf16[8,128,2048]{2,1,0:T(8,128)(2,1)}, bf16[8,128,2048]{2,1,0:...) custom-call(bf16[128,2048]{1,0:T(8,128)(2,1)} %refs_0_.1, bf16[128,2048]{1,0:T(8,128)(2,1)} %refs_1_.1, ...), custom_call_target="tpu_custom_call" | custom-call | tf_op jit(solution)/shard_map/pallas_call | solution.py:878
  141.2 98.5 %shard_map.256 = (f32[1024,768]{1,0:T(8,128)}, f32[1024,256]{1,0:T(8,128)}, bf16[1024,352]{1,0:T(8,128)(2,1)}, bf16[2048,512]{1,0:T(8,128)(2,1)}, bf16[4,512,384...) custom-call(bf16[1024,2048]{1,0:T(8,128)(2,1)} %bitcast.59, ...), custom_call_target="tpu_custom_call" | custom-call | tf_op jit(solution)/shard_map/pallas_call | solution.py:283
  239.9 32.2 %shard_map.257 = (bf16[4,6400,128]{2,1,0:T(8,128)(2,1)}, bf16[1024,1408]{1,0:T(8,128)(2,1)}, bf16[1024,528]{1,0:T(8,128)(2,1)}) custom-call(bf16[1024,2048]{1,0:T(8,128)(2,1)} %bitcast.63, bf16[1024,2048]{1,0:T(8,128)(2,1)} %bitcast.55, bf16[2048,384]{1,0:T(8,128)(2,1)} %bitcast.57, bf16[2048,1024]{1,0:T(8,128)(2,1)} %bitcast.61, ...), custom_call_target="tpu_custom_call" | custom-call | tf_op jit(solution)/shard_map/pallas_call | solution.py:449
  272.2 7.1 %fusion.9 = f32[1024,2048]{1,0:T(8,128)S(1)} fusion(bf16[2048,1024]{1,0:T(8,128)(2,1)} %bitcast.62, bf16[1024,1408]{1,0:T(8,128)(2,1)} %get-tuple-element.72), kind=kOutput, calls=%fused_computation.11 | convolution fusion | flops 4294967296 | bytes 14680064 | tf_op jit(solution)/shard_map/dot_general | solution.py:1100
  279.4 3.5 add_convert_fusion
  282.9 21.9 %shard_map.258 = f32[128,2048]{1,0:T(8,128)S(1)} custom-call(bf16[8,128,2048]{2,1,0:T(8,128)(2,1)S(1)} %bitcast.45), custom_call_target="tpu_custom_call" | custom-call | tf_op jit(solution)/shard_map/pallas_call | solution.py:1075
  308.1 25.2 %shard_map.259 = bf16[8,128,2176]{2,1,0:T(8,128)(2,1)S(1)} custom-call(bf16[128,2176]{1,0:T(8,128)(2,1)S(1)} %concatenate.17.own_ref), custom_call_target="tpu_custom_call" | custom-call | tf_op jit(solution)/shard_map/pallas_call | solution.py:1056
  333.3 2.1 copy-done.3
  336.0 3.6 fusion.2.do_ref
  339.7 9.1 %shard_map.260 = (bf16[1024,768]{1,0:T(8,128)(2,1)S(1)}, bf16[1024,256]{1,0:T(8,128)(2,1)S(1)}, f32[1,256]{1,0:T(1,128)S(1)}) custom-call(f32[1024,768]{1,0:T(8,128)} %get-tuple-element.70.proj_ref, f32[1024,256]{1,0:T(8,128)S(1)} %copy-done.6, f32[1024,256]{1,0:T(8,128)S(1)} %fusion.2.do_ref, f32[1024,2]{1,0:T(8,128)S(1)} %copy.69.info_ref, ...), custom_call_target="tpu_custom_call" | custom-call | tf_op jit(solution)/shard_map/pallas_call | solution.py:521
  351.3 5.1 %fusion.7 = f32[1024,2048]{1,0:T(8,128)S(1)} fusion(bf16[1024,528]{1,0:T(8,128)(2,1)S(1)} %copy-done.39, bf16[704,2048]{1,0:T(8,128)(2,1)} %all-gather.2.cloned.1.call-done.down_hbm), kind=kOutput, calls=%fused_computation.9 | convolution fusion | flops 2214592512 | bytes 11632640 | tf_op jit(solution)/shard_map/dot_general | solution.py:1096
  356.4 2.5 add_convert_fusion.1
  359.0 23.4 %shard_map.261 = f32[128,2048]{1,0:T(8,128)S(1)} custom-call(bf16[8,128,2048]{2,1,0:T(8,128)(2,1)S(1)} %bitcast.46), custom_call_target="tpu_custom_call" | custom-call | tf_op jit(solution)/shard_map/pallas_call | solution.py:1075
  382.4 2.2 fusion.4
  384.7 3.3 concatenate.19
  388.0 7.1 %convolution_convert_fusion = bf16[1024,2048]{1,0:T(8,128)(2,1)} fusion(bf16[1024,768]{1,0:T(8,128)(2,1)S(1)} %copy-done.15, bf16[2048,768]{1,0:T(8,128)(2,1)} %bitcast.65), kind=kOutput, calls=%fused_computation.2 | convolution fusion | flops 3223322624 | bytes 8912896 | tf_op jit(solution)/shard_map/dot_general | solution.py:1100
  395.1 5.0 %convolution_convert_fusion.1 = bf16[2048,768]{1,0:T(8,128)(2,1)} fusion(bf16[1024,2048]{1,0:T(8,128)(2,1)S(1)} %bitcast.60, bf16[1024,768]{1,0:T(8,128)(2,1)S(1)} %copy-done.15), kind=kOutput, calls=%fused_computation.7 | convolution fusion | flops 3222798336 | bytes 8912896 | tf_op jit(solution)/shard_map/dot_general | solution.py:1104
  401.4 2.2 copy-done.5
  403.6 22.8 %shard_map.262 = f32[128,2048]{1,0:T(8,128)S(1)} custom-call(bf16[8,128,2048]{2,1,0:T(8,128)(2,1)S(1)} %bitcast.52), custom_call_target="tpu_custom_call" | custom-call | tf_op jit(solution)/shard_map/pallas_call | solution.py:1075
  426.5 30.4 %shard_map.265 = (bf16[64,5632]{1,0:T(8,128)(2,1)S(1)}, bf16[64,5632]{1,0:T(8,128)(2,1)S(1)}, bf16[64,5632]{1,0:T(8,128)(2,1)S(1)}) custom-call(bf16[512,512]{1,0:T(8,128)(2,1)S(1)} %copy-done.10, bf16[6400,128]{1,0:T(8,128)(2,1)S(1)} %copy-done.2, bf16[6400,128]{1,0:T(8,128)(2,1)S(1)} %copy-done.2), custom_call_target="tpu_custom_call" | custom-call | tf_op jit(solution)/shard_map/pallas_call | solution.py:1023
  466.1 13.0 %shard_map.263 = (bf16[64,2048]{1,0:T(8,128)(2,1)S(1)}, bf16[64,2048]{1,0:T(8,128)(2,1)S(1)}, bf16[64,2048]{1,0:T(8,128)(2,1)S(1)}) custom-call(bf16[512,768]{1,0:T(8,128)(2,1)S(1)} %copy-done.7), custom_call_target="tpu_custom_call" | custom-call | tf_op jit(solution)/shard_map/pallas_call | solution.py:1023
  480.0 2.2 multiply_reduce_fusion.4
  482.9 11.1 %reduce-scatter.11.cloned.1.call-done.sum_ref = bf16[64,2176]{1,0:T(8,128)(2,1)} async-done(((bf16[256,2176]{1,0:T(8,128)(2,1)}), bf16[64,2176]{1,0:T(8,128)(2,1)}) %reduce-scatter.11.cloned.1.call-update) | async-done | bytes 278544 | tf_op jit(solution)/shard_map/reduce_scatter | solution.py:1239
  (162 shorter events, 26.9 us)
Async XLA Ops:
  7.3 7.2 %copy-start.28 = (bf16[128,2048]{1,0:T(8,128)(2,1)S(1)}, bf16[128,2048]{1,0:T(8,128)(2,1)}, u32[]{:S(2)}) copy-start(bf16[128,2048]{1,0:T(8,128)(2,1)} %param.17) | copy-start | bytes 1572868
  7.3 133.9 %all-gather.2.cloned.1.call-start = ((), (), s32[]{:S(2)}) async-start(), calls=%async_computation.4 | async-start | bytes 3604480 | tf_op jit(solution)/shard_map/all_gather | solution.py:1145
  7.3 8.1 %copy-start.34 = (f32[2048]{0:T(1024)S(1)}, f32[2048]{0:T(1024)}, u32[]{:S(2)}) copy-start(f32[2048]{0:T(1024)} %param.28) | copy-start | bytes 24580
  9.8 390.3 %reduce-scatter.5.cloned.1.call-start = ((), (), s32[]{:S(2)}) async-start(), calls=%async_computation.5 | async-start | bytes 2621440 | tf_op jit(solution)/shard_map/reduce_scatter | solution.py:1239
  239.7 160.7 %reduce-scatter.7.cloned.1.call-start = ((), (), s32[]{:S(2)}) async-start(), calls=%async_computation.6 | async-start | bytes 8192000 | tf_op jit(solution)/shard_map/reduce_scatter | solution.py:1239
  272.2 191.3 %reduce-scatter.9.cloned.1.call-start = ((), (), s32[]{:S(2)}) async-start(), calls=%async_computation.7 | async-start | bytes 3932160 | tf_op jit(solution)/shard_map/reduce_scatter | solution.py:1239
  272.2 7.1 %copy-start.23 = (bf16[4,512,384]{2,1,0:T(8,128)(2,1)S(1)}, bf16[4,512,384]{2,1,0:T(8,128)(2,1)}, u32[]{:S(2)}) copy-start(bf16[4,512,384]{2,1,0:T(8,128)(2,1)} %get-tuple-element.65) | copy-start | bytes 4718596
  282.9 21.9 %copy-start.21 = (f32[128,2048]{1,0:T(8,128)S(1)}, f32[128,2048]{1,0:T(8,128)}, u32[]{:S(2)}) copy-start(f32[128,2048]{1,0:T(8,128)} %get-tuple-element.62) | copy-start | bytes 3145732
  282.9 22.1 %copy-start.33 = (f32[2048]{0:T(1024)S(1)}, f32[2048]{0:T(1024)}, u32[]{:S(2)}) copy-start(f32[2048]{0:T(1024)} %param.30) | copy-start | bytes 24580
  308.1 27.9 %copy-start.30 = (bf16[4,64,2176]{2,1,0:T(8,128)(2,1)S(1)}, bf16[4,64,2176]{2,1,0:T(8,128)(2,1)}, u32[]{:S(2)}) copy-start(bf16[4,64,2176]{2,1,0:T(8,128)(2,1)} %get-tuple-element.61) | copy-start | bytes 3342340
  339.7 11.6 %copy-start.39 = (bf16[1024,528]{1,0:T(8,128)(2,1)S(1)}, bf16[1024,528]{1,0:T(8,128)(2,1)}, u32[]{:S(2)}) copy-start(bf16[1024,528]{1,0:T(8,128)(2,1)} %get-tuple-element.69) | copy-start | bytes 3244036
  356.4 26.0 %slice-start = ((s8[4456448]{0:T(1024)(128)(4,1)}), s8[4194304]{0:T(1024)(128)(4,1)S(1)}, s32[]{:S(2)}) async-start(s8[4456448]{0:T(1024)(128)(4,1)} %bitcast.49), calls=%async_computation.9 | async-start | bytes 8388608
  356.4 26.0 %slice-start.1 = ((s8[4456448]{0:T(1024)(128)(4,1)}), s8[262144]{0:T(1024)(128)(4,1)S(1)}, s32[]{:S(2)}) async-start(s8[4456448]{0:T(1024)(128)(4,1)} %bitcast.49), calls=%async_computation.10 | async-start | bytes 524288
  359.0 23.4 %copy-start.17 = (bf16[1024,256]{1,0:T(8,128)(2,1)S(1)}, bf16[1024,256]{1,0:T(8,128)(2,1)}, u32[]{:S(2)}) copy-start(bf16[1024,256]{1,0:T(8,128)(2,1)} %copy-done.16) | copy-start | bytes 1572868
  388.0 7.1 %copy-start.24 = (bf16[8,128,2048]{2,1,0:T(8,128)(2,1)S(1)}, bf16[8,128,2048]{2,1,0:T(8,128)(2,1)}, u32[]{:S(2)}) copy-start(bf16[8,128,2048]{2,1,0:T(8,128)(2,1)} %get-tuple-element.56) | copy-start | bytes 12582916
  400.4 26.0 %copy-start.10 = (bf16[512,512]{1,0:T(8,128)(2,1)S(1)}, bf16[512,512]{1,0:T(8,128)(2,1)}, u32[]{:S(2)}) copy-start(bf16[512,512]{1,0:T(8,128)(2,1)} %reduce-scatter.5.cloned.1.call-done.refs_0_) | copy-start | bytes 1572868
  400.5 26.0 %copy-start.2 = (bf16[6400,128]{1,0:T(8,128)(2,1)S(1)}, bf16[6400,128]{1,0:T(8,128)(2,1)}, u32[]{:S(2)}) copy-start(bf16[6400,128]{1,0:T(8,128)(2,1)} %reduce-scatter.7.cloned.1.call-done.refs_1_.refs_2_) | copy-start | bytes 4915204
  400.5 93.5 %reduce-scatter.11.cloned.1.call-start = ((), (), s32[]{:S(2)}) async-start(), calls=%async_computation.8 | async-start | bytes 1392640 | tf_op jit(solution)/shard_map/reduce_scatter | solution.py:1239
  426.4 30.5 %copy-start.20 = (bf16[128,2048]{1,0:T(8,128)(2,1)S(1)}, bf16[128,2048]{1,0:T(8,128)(2,1)}, u32[]{:S(2)}) copy-start(bf16[128,2048]{1,0:T(8,128)(2,1)} %token_hbm.1) | copy-start | bytes 1572868
  426.5 30.5 %copy-start.35 = (f32[2048]{0:T(1024)S(1)}, f32[2048]{0:T(1024)}, u32[]{:S(2)}) copy-start(f32[2048]{0:T(1024)} %param.28) | copy-start | bytes 24580
  426.5 30.8 %copy-start.26 = (bf16[128,5632]{1,0:T(8,128)(2,1)S(1)}, bf16[128,5632]{1,0:T(8,128)(2,1)}, u32[]{:S(2)}) copy-start(bf16[128,5632]{1,0:T(8,128)(2,1)} %refs_3_.1) | copy-start | bytes 4325380
  426.5 30.8 %copy-start.27 = (bf16[128,5632]{1,0:T(8,128)(2,1)S(1)}, bf16[128,5632]{1,0:T(8,128)(2,1)}, u32[]{:S(2)}) copy-start(bf16[128,5632]{1,0:T(8,128)(2,1)} %refs_4_.1) | copy-start | bytes 4325380
  461.6 17.4 %copy-start.29 = (bf16[128,2048]{1,0:T(8,128)(2,1)S(1)}, bf16[128,2048]{1,0:T(8,128)(2,1)}, u32[]{:S(2)}) copy-start(bf16[128,2048]{1,0:T(8,128)(2,1)} %refs_0_.1) | copy-start | bytes 1572868
  464.9 30.9 %copy-start.1 = (bf16[128,2048]{1,0:T(8,128)(2,1)S(1)}, bf16[128,2048]{1,0:T(8,128)(2,1)}, u32[]{:S(2)}) copy-start(bf16[128,2048]{1,0:T(8,128)(2,1)} %param.24) | copy-start | bytes 1572868
  (25 other events, 87.2 us)
Sparse Core Ops, SparseCore 0:
  10.2 84.4 all-gather.1
  239.8 43.7 reduce-scatter.4
  286.1 114.3 reduce-scatter.6
  402.7 60.7 reduce-scatter.8
  465.8 28.1 reduce-scatter.10
